TPU v7x, 32 devices: a whole 2x2x4 slice. The times are simulated.
32 devices in a mesh: cp: 16 (over z, x, core), sp: 2 (over y).
Axes of the slice: x: 2, y: 2, z: 4, core: 2. Of those that a mesh axis runs over, the one named last changes fastest.
Arguments:
- queries: bfloat16 [4096, 2048], P('cp', 'sp'), may hold values from -22 to 22
- keys: bfloat16 [4096, 128], P(('cp', 'sp')), may hold values from -5 to 5
- values: bfloat16 [4096, 128], P(('cp', 'sp')), may hold values from -6 to 6
- doc_ids: int32 [32], replicated, may hold values from 0 to 7, never falling along the last dimension, each value on 1 to 8 neighbouring positions
- span_order: int32 [16], replicated, may hold values from 0 to 15, each once
Outputs:
- attended: bfloat16 [4096, 2048], P('cp', 'sp')
Inputs may be any that keep to these rules, and one draw needn't show every extreme that they name: doc_ids never falls; each document covers 1 to 8 consecutive blocks, and one covers exactly 8. Index i of cp holds span span_order[i] of the sequence; each span once.
All inputs are finite; a program needn't handle non-finite values.
Results may differ from a plain program's by a relative error of at most 0.0036.
Values may be sent and summed in bfloat16 or wider, within the bound.
No kernel may reach another device: no remote copies, remote signals or barrier semaphores. Data moves between devices by JAX's collectives and lax.ppermute only.
A program may use at most 64 MiB of HBM per device.

v0:
```python
import math

import jax
import jax.numpy as jnp
from jax import lax
from jax.sharding import PartitionSpec as P

HD = 128
SPAN = 256
BLK = 128


NEGATIVE = -1e30


def true_position(row_ids, span_order):
    span_index = row_ids // SPAN
    lookup = jnp.arange(span_order.shape[0], dtype=jnp.int32)
    placed = jnp.sum(
        jnp.where(span_index[:, None] == lookup[None, :], span_order[None, :], 0), axis=1
    )
    return placed * SPAN + row_ids % SPAN


def doc_lookup(position, doc_ids):
    block_index = position // BLK
    lookup = jnp.arange(doc_ids.shape[0], dtype=jnp.int32)
    return jnp.sum(jnp.where(block_index[:, None] == lookup[None, :], doc_ids[None, :], 0), axis=1)


def make_folder(query_block, query_pos, query_doc, span_order, doc_ids):
    score_scale = 1.0 / math.sqrt(query_block.shape[2])

    def fold_piece(carried, piece, start):
        key_piece, value_piece = piece
        piece_rows = key_piece.shape[0]
        tile_rows = math.gcd(piece_rows, SPAN)
        tile_count = piece_rows // tile_rows
        key_tiles = key_piece.reshape(tile_count, tile_rows, key_piece.shape[1])
        value_tiles = value_piece.reshape(tile_count, tile_rows, value_piece.shape[1])

        def tile_step(state_now, tile_inputs):
            key_tile, value_tile, tile_index = tile_inputs
            row_ids = tile_index * tile_rows + jnp.arange(tile_rows, dtype=jnp.int32)
            key_pos = true_position(row_ids, span_order)
            key_doc = doc_lookup(key_pos, doc_ids)
            allowed = (key_pos[None, :] <= query_pos[:, None]) & (
                key_doc[None, :] == query_doc[:, None]
            )
            run_max, run_total, run_accum = state_now
            scores = (
                jnp.einsum("rhd,kd->hrk", query_block, key_tile, preferred_element_type=jnp.float32)
                * score_scale
            )
            masked = jnp.where(allowed[None], scores, NEGATIVE)
            new_max = jnp.maximum(run_max, jnp.max(masked, axis=2))
            rescale = jnp.exp(run_max - new_max)
            weights = jnp.where(allowed[None], jnp.exp(masked - new_max[:, :, None]), 0.0)
            new_total = run_total * rescale + jnp.sum(weights, axis=2)
            product = jnp.einsum(
                "hrk,kd->rhd",
                weights.astype(jnp.bfloat16),
                value_tile,
                preferred_element_type=jnp.float32,
            )
            new_accum = run_accum * jnp.transpose(rescale)[:, :, None] + product
            result = (new_max, new_total, new_accum)
            return (result, None)

        tile_ids = jnp.arange(tile_count, dtype=jnp.int32)
        carried, unused = lax.scan(tile_step, carried, (key_tiles, value_tiles, tile_ids))
        return carried

    return fold_piece


def shards(queries, keys, values, doc_ids, span_order):
    cp_index = lax.axis_index("cp")
    query_ids = cp_index * SPAN + jnp.arange(queries.shape[0], dtype=jnp.int32)
    query_count = queries.shape[0]
    head_count = queries.shape[1] // HD
    query_block = queries.reshape(query_count, head_count, HD)
    query_pos = true_position(query_ids, span_order)
    query_doc = doc_lookup(query_pos, doc_ids)
    folder = make_folder(query_block, query_pos, query_doc, span_order, doc_ids)
    initial = (
        jnp.full((head_count, query_count), NEGATIVE, jnp.float32),
        jnp.zeros((head_count, query_count), jnp.float32),
        jnp.zeros((query_count, head_count, HD), jnp.float32),
    )
    group_keys, group_values = (
        lax.all_gather(keys, "sp", axis=0, tiled=True),
        lax.all_gather(values, "sp", axis=0, tiled=True),
    )
    final = folder(
        initial,
        (
            lax.all_gather(group_keys, "cp", axis=0, tiled=True),
            lax.all_gather(group_values, "cp", axis=0, tiled=True),
        ),
        jnp.int32(0),
    )
    run_max, run_total, run_accum = final
    attended = (run_accum / jnp.transpose(run_total)[:, :, None]).astype(jnp.bfloat16)
    attended = attended.reshape(query_count, head_count * HD)
    return attended


def solution(mesh):
    in_specs = (P("cp", "sp"), P(("cp", "sp"), None), P(("cp", "sp"), None), P(), P())
    out_specs = P("cp", "sp")
    return jax.shard_map(shards, mesh=mesh, in_specs=in_specs, out_specs=out_specs, check_vma=False)
```

profile of v0, /device:TPU:0, one launch (start us, length us, event | category | flops | bytes accessed | tf_op | source)
XLA Modules:
  0.0 201.3 jit_solution(179635906846086908)
XLA Ops:
  6.5 7.3 %all_gather.12 = bf16[256,128]{1,0:T(8,128)(2,1)} all-gather(bf16[128,128]{1,0:T(8,128)(2,1)} %param.8), channel_id=1, replica_groups=mesh['cp'=16,'sp'=2] {'sp'}, dimensions={0}, use_global_device_ids=true | all-gather | bytes 98304 | tf_op jit(solution)/shard_map/all_gather | solution.py:92
  13.9 4.9 %all_gather.14 = bf16[256,128]{1,0:T(8,128)(2,1)} all-gather(bf16[128,128]{1,0:T(8,128)(2,1)} %param.9), channel_id=1, replica_groups=mesh['cp'=16,'sp'=2] {'sp'}, dimensions={0}, use_global_device_ids=true | all-gather | bytes 98304 | tf_op jit(solution)/shard_map/all_gather | solution.py:93
  18.9 1.2 copy.14
  20.7 31.8 %all-gather.3.cloned.1.call-done = bf16[4096,128]{1,0:T(8,128)(2,1)} async-done(((bf16[256,128]{1,0:T(8,128)(2,1)}), bf16[4096,128]{1,0:T(8,128)(2,1)}) %all-gather.3.cloned.1.call-update) | async-done | bytes 1048592 | tf_op jit(solution)/shard_map/all_gather | solution.py:98
  52.4 39.0 %all-gather.5.cloned.1.call-done = bf16[4096,128]{1,0:T(8,128)(2,1)} async-done(((bf16[256,128]{1,0:T(8,128)(2,1)}), bf16[4096,128]{1,0:T(8,128)(2,1)}) %all-gather.5.cloned.1.call-update) | async-done | bytes 1048592 | tf_op jit(solution)/shard_map/all_gather | solution.py:99
  91.5 100.6 %while.18 = (s32[]{:T(128)}, f32[8,256]{1,0:T(8,128)S(1)}, f32[8,256]{1,0:T(8,128)S(1)}, f32[256,8,128]{0,2,1:T(8,128)}, s32[16]{0:T(128)S(1)}, /*index=5*/s32[1...) while((s32[]{:T(128)}, f32[8,256]{1,0:T(8,128)S(1)}, ...), condition=%wide.region_7.8_spmd.clone, body=%wide.region_2.7_spmd.clone.sunk | while | flops 276294400 | bytes 9450873 | solution.py:71
  91.5 0.6 dynamic_slice.41
  92.9 1.3 fusion.40
  94.3 2.5 %fusion.44 = f32[256,8,128]{0,2,1:T(8,128)} fusion(f32[256,256,8]{1,0,2:T(8,128)S(1)} %get-tuple-element.377, f32[256,8,128]{0,2,1:T(8,128)} %get-tuple-element.397, f32[8,256]{1,0:T(8,128)S(1)} %get-tuple-element.410, pred[256,256]{0,1:T(8,128)(4,1)S(1)} %compare_and_fusion.2, f32[256,8]{0,1:T(8,128)S(1)} %get-tuple-element.378, pred[]{:T(512)S(6)} %compare.48, ...), kind=kOutput, calls=%fused_computation.6.clone.1 | convolution fusion | flops 137625600 | bytes 4342273 | tf_op jit(solution)/shard_map/while/body/eval_jaxpr/hrk,kd->rhd/dot_general | solution.py:60
  96.8 0.5 fusion.42
  97.4 0.6 dynamic_slice.41
  98.8 1.3 fusion.40
  100.2 2.9 %fusion.44 = f32[256,8,128]{0,2,1:T(8,128)} fusion(f32[256,256,8]{1,0,2:T(8,128)S(1)} %get-tuple-element.377, f32[256,8,128]{0,2,1:T(8,128)} %get-tuple-element.397, f32[8,256]{1,0:T(8,128)S(1)} %get-tuple-element.410, pred[256,256]{0,1:T(8,128)(4,1)S(1)} %compare_and_fusion.2, f32[256,8]{0,1:T(8,128)S(1)} %get-tuple-element.378, pred[]{:T(512)S(6)} %compare.48, ...), kind=kOutput, calls=%fused_computation.6.clone.1 | convolution fusion | flops 137625600 | bytes 4342273 | tf_op jit(solution)/shard_map/while/body/eval_jaxpr/hrk,kd->rhd/dot_general | solution.py:60
  103.1 0.5 fusion.42
  103.7 0.6 dynamic_slice.41
  105.1 1.3 fusion.40
  106.5 2.9 %fusion.44 = f32[256,8,128]{0,2,1:T(8,128)} fusion(f32[256,256,8]{1,0,2:T(8,128)S(1)} %get-tuple-element.377, f32[256,8,128]{0,2,1:T(8,128)} %get-tuple-element.397, f32[8,256]{1,0:T(8,128)S(1)} %get-tuple-element.410, pred[256,256]{0,1:T(8,128)(4,1)S(1)} %compare_and_fusion.2, f32[256,8]{0,1:T(8,128)S(1)} %get-tuple-element.378, pred[]{:T(512)S(6)} %compare.48, ...), kind=kOutput, calls=%fused_computation.6.clone.1 | convolution fusion | flops 137625600 | bytes 4342273 | tf_op jit(solution)/shard_map/while/body/eval_jaxpr/hrk,kd->rhd/dot_general | solution.py:60
  109.4 0.5 fusion.42
  110.0 0.6 dynamic_slice.41
  111.5 1.3 fusion.40
  112.8 2.9 %fusion.44 = f32[256,8,128]{0,2,1:T(8,128)} fusion(f32[256,256,8]{1,0,2:T(8,128)S(1)} %get-tuple-element.377, f32[256,8,128]{0,2,1:T(8,128)} %get-tuple-element.397, f32[8,256]{1,0:T(8,128)S(1)} %get-tuple-element.410, pred[256,256]{0,1:T(8,128)(4,1)S(1)} %compare_and_fusion.2, f32[256,8]{0,1:T(8,128)S(1)} %get-tuple-element.378, pred[]{:T(512)S(6)} %compare.48, ...), kind=kOutput, calls=%fused_computation.6.clone.1 | convolution fusion | flops 137625600 | bytes 4342273 | tf_op jit(solution)/shard_map/while/body/eval_jaxpr/hrk,kd->rhd/dot_general | solution.py:60
  115.8 0.5 fusion.42
  116.3 0.6 dynamic_slice.41
  117.8 1.3 fusion.40
  119.1 2.9 %fusion.44 = f32[256,8,128]{0,2,1:T(8,128)} fusion(f32[256,256,8]{1,0,2:T(8,128)S(1)} %get-tuple-element.377, f32[256,8,128]{0,2,1:T(8,128)} %get-tuple-element.397, f32[8,256]{1,0:T(8,128)S(1)} %get-tuple-element.410, pred[256,256]{0,1:T(8,128)(4,1)S(1)} %compare_and_fusion.2, f32[256,8]{0,1:T(8,128)S(1)} %get-tuple-element.378, pred[]{:T(512)S(6)} %compare.48, ...), kind=kOutput, calls=%fused_computation.6.clone.1 | convolution fusion | flops 137625600 | bytes 4342273 | tf_op jit(solution)/shard_map/while/body/eval_jaxpr/hrk,kd->rhd/dot_general | solution.py:60
  122.1 0.5 fusion.42
  122.6 0.6 dynamic_slice.41
  124.1 1.3 fusion.40
  125.4 2.9 %fusion.44 = f32[256,8,128]{0,2,1:T(8,128)} fusion(f32[256,256,8]{1,0,2:T(8,128)S(1)} %get-tuple-element.377, f32[256,8,128]{0,2,1:T(8,128)} %get-tuple-element.397, f32[8,256]{1,0:T(8,128)S(1)} %get-tuple-element.410, pred[256,256]{0,1:T(8,128)(4,1)S(1)} %compare_and_fusion.2, f32[256,8]{0,1:T(8,128)S(1)} %get-tuple-element.378, pred[]{:T(512)S(6)} %compare.48, ...), kind=kOutput, calls=%fused_computation.6.clone.1 | convolution fusion | flops 137625600 | bytes 4342273 | tf_op jit(solution)/shard_map/while/body/eval_jaxpr/hrk,kd->rhd/dot_general | solution.py:60
  128.4 0.5 fusion.42
  128.9 0.6 dynamic_slice.41
  130.4 1.3 fusion.40
  131.8 2.9 %fusion.44 = f32[256,8,128]{0,2,1:T(8,128)} fusion(f32[256,256,8]{1,0,2:T(8,128)S(1)} %get-tuple-element.377, f32[256,8,128]{0,2,1:T(8,128)} %get-tuple-element.397, f32[8,256]{1,0:T(8,128)S(1)} %get-tuple-element.410, pred[256,256]{0,1:T(8,128)(4,1)S(1)} %compare_and_fusion.2, f32[256,8]{0,1:T(8,128)S(1)} %get-tuple-element.378, pred[]{:T(512)S(6)} %compare.48, ...), kind=kOutput, calls=%fused_computation.6.clone.1 | convolution fusion | flops 137625600 | bytes 4342273 | tf_op jit(solution)/shard_map/while/body/eval_jaxpr/hrk,kd->rhd/dot_general | solution.py:60
  134.7 0.5 fusion.42
  135.3 0.6 dynamic_slice.41
  136.7 1.3 fusion.40
  138.1 2.9 %fusion.44 = f32[256,8,128]{0,2,1:T(8,128)} fusion(f32[256,256,8]{1,0,2:T(8,128)S(1)} %get-tuple-element.377, f32[256,8,128]{0,2,1:T(8,128)} %get-tuple-element.397, f32[8,256]{1,0:T(8,128)S(1)} %get-tuple-element.410, pred[256,256]{0,1:T(8,128)(4,1)S(1)} %compare_and_fusion.2, f32[256,8]{0,1:T(8,128)S(1)} %get-tuple-element.378, pred[]{:T(512)S(6)} %compare.48, ...), kind=kOutput, calls=%fused_computation.6.clone.1 | convolution fusion | flops 137625600 | bytes 4342273 | tf_op jit(solution)/shard_map/while/body/eval_jaxpr/hrk,kd->rhd/dot_general | solution.py:60
  141.0 0.5 fusion.42
  141.6 0.6 dynamic_slice.41
  143.0 1.3 fusion.40
  144.4 2.9 %fusion.44 = f32[256,8,128]{0,2,1:T(8,128)} fusion(f32[256,256,8]{1,0,2:T(8,128)S(1)} %get-tuple-element.377, f32[256,8,128]{0,2,1:T(8,128)} %get-tuple-element.397, f32[8,256]{1,0:T(8,128)S(1)} %get-tuple-element.410, pred[256,256]{0,1:T(8,128)(4,1)S(1)} %compare_and_fusion.2, f32[256,8]{0,1:T(8,128)S(1)} %get-tuple-element.378, pred[]{:T(512)S(6)} %compare.48, ...), kind=kOutput, calls=%fused_computation.6.clone.1 | convolution fusion | flops 137625600 | bytes 4342273 | tf_op jit(solution)/shard_map/while/body/eval_jaxpr/hrk,kd->rhd/dot_general | solution.py:60
  147.9 0.6 dynamic_slice.41
  149.4 1.3 fusion.40
  150.7 2.9 %fusion.44 = f32[256,8,128]{0,2,1:T(8,128)} fusion(f32[256,256,8]{1,0,2:T(8,128)S(1)} %get-tuple-element.377, f32[256,8,128]{0,2,1:T(8,128)} %get-tuple-element.397, f32[8,256]{1,0:T(8,128)S(1)} %get-tuple-element.410, pred[256,256]{0,1:T(8,128)(4,1)S(1)} %compare_and_fusion.2, f32[256,8]{0,1:T(8,128)S(1)} %get-tuple-element.378, pred[]{:T(512)S(6)} %compare.48, ...), kind=kOutput, calls=%fused_computation.6.clone.1 | convolution fusion | flops 137625600 | bytes 4342273 | tf_op jit(solution)/shard_map/while/body/eval_jaxpr/hrk,kd->rhd/dot_general | solution.py:60
  154.2 0.6 dynamic_slice.41
  155.7 1.3 fusion.40
  157.0 2.9 %fusion.44 = f32[256,8,128]{0,2,1:T(8,128)} fusion(f32[256,256,8]{1,0,2:T(8,128)S(1)} %get-tuple-element.377, f32[256,8,128]{0,2,1:T(8,128)} %get-tuple-element.397, f32[8,256]{1,0:T(8,128)S(1)} %get-tuple-element.410, pred[256,256]{0,1:T(8,128)(4,1)S(1)} %compare_and_fusion.2, f32[256,8]{0,1:T(8,128)S(1)} %get-tuple-element.378, pred[]{:T(512)S(6)} %compare.48, ...), kind=kOutput, calls=%fused_computation.6.clone.1 | convolution fusion | flops 137625600 | bytes 4342273 | tf_op jit(solution)/shard_map/while/body/eval_jaxpr/hrk,kd->rhd/dot_general | solution.py:60
  160.5 0.6 dynamic_slice.41
  162.0 1.3 fusion.40
  163.3 2.9 %fusion.44 = f32[256,8,128]{0,2,1:T(8,128)} fusion(f32[256,256,8]{1,0,2:T(8,128)S(1)} %get-tuple-element.377, f32[256,8,128]{0,2,1:T(8,128)} %get-tuple-element.397, f32[8,256]{1,0:T(8,128)S(1)} %get-tuple-element.410, pred[256,256]{0,1:T(8,128)(4,1)S(1)} %compare_and_fusion.2, f32[256,8]{0,1:T(8,128)S(1)} %get-tuple-element.378, pred[]{:T(512)S(6)} %compare.48, ...), kind=kOutput, calls=%fused_computation.6.clone.1 | convolution fusion | flops 137625600 | bytes 4342273 | tf_op jit(solution)/shard_map/while/body/eval_jaxpr/hrk,kd->rhd/dot_general | solution.py:60
  166.8 0.6 dynamic_slice.41
  168.3 1.3 fusion.40
  169.7 2.9 %fusion.44 = f32[256,8,128]{0,2,1:T(8,128)} fusion(f32[256,256,8]{1,0,2:T(8,128)S(1)} %get-tuple-element.377, f32[256,8,128]{0,2,1:T(8,128)} %get-tuple-element.397, f32[8,256]{1,0:T(8,128)S(1)} %get-tuple-element.410, pred[256,256]{0,1:T(8,128)(4,1)S(1)} %compare_and_fusion.2, f32[256,8]{0,1:T(8,128)S(1)} %get-tuple-element.378, pred[]{:T(512)S(6)} %compare.48, ...), kind=kOutput, calls=%fused_computation.6.clone.1 | convolution fusion | flops 137625600 | bytes 4342273 | tf_op jit(solution)/shard_map/while/body/eval_jaxpr/hrk,kd->rhd/dot_general | solution.py:60
  173.2 0.6 dynamic_slice.41
  174.6 1.3 fusion.40
  176.0 2.9 %fusion.44 = f32[256,8,128]{0,2,1:T(8,128)} fusion(f32[256,256,8]{1,0,2:T(8,128)S(1)} %get-tuple-element.377, f32[256,8,128]{0,2,1:T(8,128)} %get-tuple-element.397, f32[8,256]{1,0:T(8,128)S(1)} %get-tuple-element.410, pred[256,256]{0,1:T(8,128)(4,1)S(1)} %compare_and_fusion.2, f32[256,8]{0,1:T(8,128)S(1)} %get-tuple-element.378, pred[]{:T(512)S(6)} %compare.48, ...), kind=kOutput, calls=%fused_computation.6.clone.1 | convolution fusion | flops 137625600 | bytes 4342273 | tf_op jit(solution)/shard_map/while/body/eval_jaxpr/hrk,kd->rhd/dot_general | solution.py:60
  179.5 0.6 dynamic_slice.41
  180.9 1.3 fusion.40
  182.3 2.9 %fusion.44 = f32[256,8,128]{0,2,1:T(8,128)} fusion(f32[256,256,8]{1,0,2:T(8,128)S(1)} %get-tuple-element.377, f32[256,8,128]{0,2,1:T(8,128)} %get-tuple-element.397, f32[8,256]{1,0:T(8,128)S(1)} %get-tuple-element.410, pred[256,256]{0,1:T(8,128)(4,1)S(1)} %compare_and_fusion.2, f32[256,8]{0,1:T(8,128)S(1)} %get-tuple-element.378, pred[]{:T(512)S(6)} %compare.48, ...), kind=kOutput, calls=%fused_computation.6.clone.1 | convolution fusion | flops 137625600 | bytes 4342273 | tf_op jit(solution)/shard_map/while/body/eval_jaxpr/hrk,kd->rhd/dot_general | solution.py:60
  185.8 0.6 dynamic_slice.41
  187.3 1.3 fusion.40
  188.6 2.9 %fusion.44 = f32[256,8,128]{0,2,1:T(8,128)} fusion(f32[256,256,8]{1,0,2:T(8,128)S(1)} %get-tuple-element.377, f32[256,8,128]{0,2,1:T(8,128)} %get-tuple-element.397, f32[8,256]{1,0:T(8,128)S(1)} %get-tuple-element.410, pred[256,256]{0,1:T(8,128)(4,1)S(1)} %compare_and_fusion.2, f32[256,8]{0,1:T(8,128)S(1)} %get-tuple-element.378, pred[]{:T(512)S(6)} %compare.48, ...), kind=kOutput, calls=%fused_computation.6.clone.1 | convolution fusion | flops 137625600 | bytes 4342273 | tf_op jit(solution)/shard_map/while/body/eval_jaxpr/hrk,kd->rhd/dot_general | solution.py:60
  192.1 1.3 divide_convert_fusion
  193.4 1.0 copy.19
  (153 shorter events, 10.7 us)
Async XLA Ops:
  6.5 13.9 %copy-start = (s32[16]{0:T(128)S(1)}, s32[16]{0:T(128)}, u32[]{:S(2)}) copy-start(s32[16]{0:T(128)} %param.11) | copy-start | bytes 196
  6.5 14.0 %copy-start.1 = (s32[32]{0:T(128)S(1)}, s32[32]{0:T(128)}, u32[]{:S(2)}) copy-start(s32[32]{0:T(128)} %param.10) | copy-start | bytes 388
  6.5 45.9 %all-gather.3.cloned.1.call-start = ((), (), s32[]{:S(2)}) async-start(), calls=%async_computation | async-start | bytes 1114112 | tf_op jit(solution)/shard_map/all_gather | solution.py:98
  13.9 77.6 %all-gather.5.cloned.1.call-start = ((), (), s32[]{:S(2)}) async-start(), calls=%async_computation.1 | async-start | bytes 1114112 | tf_op jit(solution)/shard_map/all_gather | solution.py:99
Sparse Core Ops, SparseCore 0:
  14.0 38.3 all-gather.2
  54.6 36.8 all-gather.4
where the time goes:
time: 203 us; the launch traced here: 201 us
  waiting for transfers between devices  70.8 us (35%)
  matrix products  67.7 us (33%)
  other arithmetic  15.7 us (8%)
  between operations  13.5 us (7%)
  blocking collectives  12.2 us (6%)
  local copies, waits for them, and re-layouts  11.4 us (6%)
  loops' own time  9.85 us (5%)
    dot_general x16, matrix products, tile_step(): jnp.einsum('hrk,kd->rhd', weights.astype(jnp.bfloat16), value_tile, prefe...  46.6 us
    all_gather x1, waiting for transfers between devices, shards(): lax.all_gather(group_values, 'cp', axis=0, tiled=True)  39 us
    all_gather x1, waiting for transfers between devices, shards(): lax.all_gather(group_keys, 'cp', axis=0, tiled=True)  31.8 us
    dot_general x16, matrix products, tile_step(): jnp.einsum('rhd,kd->hrk', query_block, key_tile, preferred_element_type=j...  21.1 us
    another operation x1, loops' own time, fold_piece(): lax.scan(tile_step, carried, (key_tiles, value_tiles, tile_ids))  9.85 us
    dynamic_slice x16, local copies, waits for them, and re-layouts, fold_piece(): lax.scan(tile_step, carried, (key_tiles, value_tiles, tile_ids))  8.85 us
    reduce_sum x16, other arithmetic, tile_step(): new_total = run_total * rescale + jnp.sum(weights, axis=2)  8.21 us
    all_gather x1, blocking collectives, shards(): lax.all_gather(keys, 'sp', axis=0, tiled=True)  7.3 us
  transfers between devices with their start and end apart: 2, of which 2 were waited for; matrix products, arithmetic and copies ran while one was open for 1% of the time, Pallas kernels for 0%

commit v1 on v0

v1 whole, which is shorter than its diff:
```python
import functools
import math

import jax
import jax.numpy as jnp
from jax import lax
from jax.experimental import pallas as pl
from jax.experimental.pallas import tpu as pltpu
from jax.sharding import PartitionSpec as P

HD = 128
SPAN = 256
BLK = 128
NEGATIVE = -1e30
SCALE2 = math.log2(math.e) / math.sqrt(HD)


def flip(array, axis, size, mask):
    return lax.ppermute(array, axis, [(i, i ^ mask) for i in range(size)])


def select_kernel(reach, order_ref, cp_ref, *refs):
    sources, out_ref = refs[:-1], refs[-1]
    cp = cp_ref[0]
    own_span = order_ref[cp]
    count = order_ref.shape[0]
    for back in range(1, reach + 1):
        span = jnp.maximum(own_span - back, 0)
        holder = jnp.int32(0)
        for index in range(count):
            holder = jnp.where(order_ref[index] == span, jnp.int32(index), holder)
        apart = holder ^ cp
        slot = apart >> 2
        for low, source in enumerate(sources):

            @pl.when((apart & 3) == low)
            def _():
                out_ref[back - 1] = source[slot]


def attend_half(half, span, doc_ref, q_ref, own_ref, prev_ref, buf, scores, max_ref, acc_ref, fresh):
    reach = prev_ref.shape[0]
    heads = q_ref.shape[1] // HD
    pairs = scores.shape[0]
    buf[0:BLK, 0 : 2 * HD] = own_ref[...]
    for back in range(reach):
        buf[(back + 1) * BLK : (back + 2) * BLK, 0 : 2 * HD] = prev_ref[back]
    rows = lax.broadcasted_iota(jnp.int32, (BLK, 2 * BLK), 0)
    cols = lax.broadcasted_iota(jnp.int32, (BLK, 2 * BLK), 1)
    for a in range(2):
        doc = doc_ref[2 * span + a]
        first = jnp.where(half <= a, 0, 1)
        count = jnp.int32(0)
        for back in range(reach + 1):
            block = 2 * (span - back) + half
            same = doc_ref[jnp.maximum(block, 0)] == doc
            inside = (block >= 0) & (back >= first)
            count = count + jnp.where(same & inside, 1, 0)
        diagonal = half == a

        if fresh:
            max_ref[a] = jnp.full(max_ref.shape[1:], NEGATIVE, jnp.float32)
            acc_ref[a] = jnp.zeros(acc_ref.shape[1:], jnp.float32)

        @pl.when(count > 0)
        def _():
            old_max = max_ref[a]

            def score_step(pair, unused):
                start = pl.multiple_of((first + 2 * pair) * BLK, BLK)
                key_pair = buf[pl.ds(start, 2 * BLK), 0:HD]
                limit = jnp.where(diagonal & (pair == 0), 0, 2 * BLK)
                open_low = (cols < BLK) & (cols <= rows + limit)
                open_high = (cols >= BLK) & (cols < (count - 2 * pair) * BLK)
                bias = jnp.where(open_low | open_high, 0.0, NEGATIVE)
                for h in range(heads):
                    block = lax.dot_general(
                        q_ref[a * BLK : (a + 1) * BLK, h * HD : (h + 1) * HD],
                        key_pair,
                        (((1,), (1,)), ((), ())),
                        preferred_element_type=jnp.float32,
                    )
                    block = block + bias
                    scores[pair, h] = block
                    best = jnp.maximum(block[:, :BLK], block[:, BLK:])
                    max_ref[a, h] = jnp.maximum(max_ref[a, h], best)
                return unused

            steps = (count + 1) // 2
            lax.fori_loop(0, steps, score_step, 0)
            for h in range(heads):
                top = jnp.max(max_ref[a, h], axis=1, keepdims=True)
                top = jnp.broadcast_to(top, (BLK, HD))
                max_ref[a, h] = top
                if not fresh:
                    keep = jnp.exp2((old_max[h] - top) * SCALE2)
                    acc_ref[a, h, :, 0:HD] = acc_ref[a, h, :, 0:HD] * keep
                    acc_ref[a, h, :, HD:] = acc_ref[a, h, :, HD:] * keep

            def value_step(pair, unused):
                start = pl.multiple_of((first + 2 * pair) * BLK, BLK)
                value_pair = buf[pl.ds(start, 2 * BLK), HD : 3 * HD]
                for h in range(heads):
                    top = max_ref[a, h]
                    low = jnp.exp2((scores[pair, h, :, :BLK] - top) * SCALE2)
                    high = jnp.exp2((scores[pair, h, :, BLK:] - top) * SCALE2)
                    weights = jnp.concatenate([low, high], axis=1).astype(jnp.bfloat16)
                    acc_ref[a, h] += jnp.dot(weights, value_pair, preferred_element_type=jnp.float32)
                return unused

            lax.fori_loop(0, steps, value_step, 0)


def attend_kernel(
    doc_ref, order_ref, place_ref, q_ref, own_ref, prev_ref, other_own_ref, other_prev_ref, out_ref,
    buf, scores, max_ref, acc_ref,
):
    span = order_ref[place_ref[0]]
    half = place_ref[1]
    heads = q_ref.shape[1] // HD
    buf[:, 2 * HD :] = jnp.ones((buf.shape[0], HD), buf.dtype)
    attend_half(half, span, doc_ref, q_ref, own_ref, prev_ref, buf, scores, max_ref, acc_ref, True)
    attend_half(1 - half, span, doc_ref, q_ref, other_own_ref, other_prev_ref, buf, scores, max_ref, acc_ref, False)
    for a in range(2):
        for h in range(heads):
            result = acc_ref[a, h, :, 0:HD] / acc_ref[a, h, :, HD:]
            out_ref[a * BLK : (a + 1) * BLK, h * HD : (h + 1) * HD] = result.astype(out_ref.dtype)


VMEM = pl.BlockSpec(memory_space=pltpu.VMEM)
SMEM = pl.BlockSpec(memory_space=pltpu.SMEM)


def select(order, place, sources, reach):
    return pl.pallas_call(
        functools.partial(select_kernel, reach),
        out_shape=jax.ShapeDtypeStruct((reach,) + sources[0].shape[1:], sources[0].dtype),
        in_specs=[SMEM, SMEM] + [VMEM] * len(sources),
        out_specs=VMEM,
        name="select",
    )(order, place, *sources)


def attend(docs, order, place, queries, own, prev, other_own, other_prev):
    reach = prev.shape[0]
    heads = queries.shape[1] // HD
    pairs = (reach + 1) // 2
    slots = 2 * pairs + 1
    return pl.pallas_call(
        attend_kernel,
        out_shape=jax.ShapeDtypeStruct(queries.shape, queries.dtype),
        in_specs=[SMEM] * 3 + [VMEM] * 5,
        out_specs=VMEM,
        scratch_shapes=[
            pltpu.VMEM((slots * BLK, 3 * HD), jnp.bfloat16),
            pltpu.VMEM((pairs, heads, BLK, 2 * BLK), jnp.float32),
            pltpu.VMEM((2, heads, BLK, HD), jnp.float32),
            pltpu.VMEM((2, heads, BLK, 2 * HD), jnp.float32),
        ],
        compiler_params=pltpu.CompilerParams(vmem_limit_bytes=32 * 1024 * 1024),
        name="attend",
    )(docs, order, place, queries, own, prev, other_own, other_prev)


def shards(cp_size, sp_size, queries, keys, values, doc_ids, span_order):
    longest = doc_ids.shape[0] // 4
    reach = longest // 2
    cp_index = lax.axis_index("cp").astype(jnp.int32)
    own = jnp.concatenate([keys, values], axis=1)
    if cp_size == 16 and sp_size == 2:
        place = jnp.stack([cp_index, lax.axis_index("sp").astype(jnp.int32)])
        near = [flip(own, "cp", cp_size, 4 * j) for j in (3, 2, 1)][::-1]
        line = jnp.stack([own] + near)
        side = flip(line, "cp", cp_size, 2)
        other_own = flip(own, "sp", sp_size, 1)
        core_line = flip(line, "cp", cp_size, 1)
        core_side = flip(side, "cp", cp_size, 1)
        prev = select(span_order, place, [line, core_line, side, core_side], reach)
        other_prev = flip(prev, "sp", sp_size, 1)
    else:
        place = jnp.stack([cp_index, jnp.int32(0)])
        pair = lax.all_gather(own, ("cp", "sp"), axis=0, tiled=True).reshape(cp_size, 2, BLK, 2 * HD)
        holder = jnp.argsort(span_order)
        back = jnp.maximum(span_order[cp_index] - jnp.arange(reach + 1, dtype=jnp.int32), 0)
        chosen = pair[holder[back]]
        own, other_own = chosen[0, 0], chosen[0, 1]
        prev, other_prev = chosen[1:, 0], chosen[1:, 1]
    return attend(doc_ids, span_order, place, queries, own, prev, other_own, other_prev)


def solution(mesh):
    in_specs = (P("cp", "sp"), P(("cp", "sp"), None), P(("cp", "sp"), None), P(), P())
    out_specs = P("cp", "sp")
    body = functools.partial(shards, mesh.shape["cp"], mesh.shape["sp"])
    return jax.shard_map(body, mesh=mesh, in_specs=in_specs, out_specs=out_specs, check_vma=False)
```

time: 203 us -> 41.9 us (0.21)
  matrix products: 67.7 us -> 0 us
  waiting for transfers between devices: 70.8 us -> 20 us
  other arithmetic: 15.7 us -> 0.71 us
  between operations: 13.5 us -> 0.09 us
  blocking collectives: 12.2 us -> 0 us
  loops' own time: 9.85 us -> 0 us
  starting transfers between devices: 0.04 us -> 9.27 us
  Pallas kernels: 0 us -> 9.14 us
  local copies, waits for them, and re-layouts: 11.4 us -> 2.47 us
    all_gather x2 -> x0, waiting for transfers between devices: 70.8 us -> none  [the longest x1 39 us: shards(): lax.all_gather(group_values, 'cp', axis=0, tiled=True)]
    dot_general x32 -> x0, matrix products: 67.7 us -> none  [the longest x16 46.6 us: tile_step(): jnp.einsum('hrk,kd->rhd', weights.astype(jnp.bfloat16), value_tile, prefe...]
    ppermute x0 -> x8, waiting for transfers between devices: none -> 20 us  [flip(): return lax.ppermute(array, axis, [(i, i ^ mask) for i in range(size)])]
    all_gather x2 -> x0, blocking collectives: 12.2 us -> none  [the longest x1 7.3 us: shards(): lax.all_gather(keys, 'sp', axis=0, tiled=True)]
    reduce_sum x50 -> x0, other arithmetic: 11.3 us -> none  [the longest x16 8.21 us: tile_step(): new_total = run_total * rescale + jnp.sum(weights, axis=2)]
    another operation x1 -> x0, loops' own time: 9.85 us -> none  [fold_piece(): lax.scan(tile_step, carried, (key_tiles, value_tiles, tile_ids))]
    ppermute x0 -> x8, starting transfers between devices: none -> 9.27 us  [flip(): return lax.ppermute(array, axis, [(i, i ^ mask) for i in range(size)])]
    pallas_call x0 -> x2, Pallas kernels: none -> 9.14 us  [the longest x1 7.1 us: attend(): pl.pallas_call(attend_kernel, out_shape=jax.ShapeDtypeStruct(queries.shap...]
  transfers between devices with their start and end apart: 2 -> 8, of which waited for: 2 -> 5; matrix products, arithmetic and copies ran while one was open for 1% -> 2% of each run, Pallas kernels for 0% -> 0%
where the time goes in v1:
time: 41.9 us; the launch traced here: 41.7 us
  waiting for transfers between devices  20 us (48%)
  starting transfers between devices  9.27 us (22%)
  Pallas kernels  9.14 us (22%)
  local copies, waits for them, and re-layouts  2.47 us (6%)
  other arithmetic  0.71 us (2%)
    ppermute x8, waiting for transfers between devices, flip(): return lax.ppermute(array, axis, [(i, i ^ mask) for i in range(size)])  20 us
    ppermute x8, starting transfers between devices, flip(): return lax.ppermute(array, axis, [(i, i ^ mask) for i in range(size)])  9.27 us
    pallas_call x1, Pallas kernels, attend(): pl.pallas_call(attend_kernel, out_shape=jax.ShapeDtypeStruct(queries.shap...  7.1 us
    unnamed x21, local copies, waits for them, and re-layouts  2.46 us
    pallas_call x1, Pallas kernels, select(): pl.pallas_call(functools.partial(select_kernel, reach), out_shape=jax.Sha...  2.04 us
  transfers between devices with their start and end apart: 8, of which 5 were waited for; matrix products, arithmetic and copies ran while one was open for 2% of the time, Pallas kernels for 0%

profile of v1, /device:TPU:0, one launch (start us, length us, event | category | flops | bytes accessed | tf_op | source)
XLA Modules:
  0.0 41.7 jit_solution(17958326282355748214)
XLA Ops:
  0.0 0.0 copy-start.9
  0.0 0.8 %constant_dynamic-update-slice_fusion.1 = bf16[128,256]{1,0:T(8,128)(2,1)S(1)} fusion(bf16[128,128]{1,0:T(8,128)(2,1)} %param.6), kind=kLoop, calls=%fused_computation.2 | loop fusion | bytes 65536
  0.8 0.0 copy-done.9
  0.8 3.1 %collective-permute-start = (bf16[128,256]{1,0:T(8,128)(2,1)S(1)}, bf16[128,256]{1,0:T(8,128)(2,1)S(1)}, u32[]{:S(2)}, u32[]{:S(2)}) collective-permute-start(bf16[128,256]{1,0:T(8,128)(2,1)S(1)} %constant_dynamic-update-slice_fusion.own_ref), channel_id=1, source_target_pairs={{0,8},{2,10},{4,12},{6,14},{8,0},{10,2},{12,4},{14,6},{16,24},{18,... | collective-permute-start | bytes 196616 | tf_op jit(solution)/shard_map/ppermute | solution.py:19
  3.9 2.6 %collective-permute-start.1 = (bf16[128,256]{1,0:T(8,128)(2,1)S(1)}, bf16[128,256]{1,0:T(8,128)(2,1)S(1)}, u32[]{:S(2)}, u32[]{:S(2)}) collective-permute-start(bf16[128,256]{1,0:T(8,128)(2,1)S(1)} %constant_dynamic-update-slice_fusion.own_ref), channel_id=1, source_target_pairs={{0,16},{2,18},{4,20},{6,22},{8,24},{10,26},{12,28},{14,30},{16,0},... | collective-permute-start | bytes 196616 | tf_op jit(solution)/shard_map/ppermute | solution.py:19
  6.5 0.0 collective-permute-start.2
  6.5 0.0 collective-permute-done
  6.5 4.7 %collective-permute-done.1 = bf16[128,256]{1,0:T(8,128)(2,1)S(1)} collective-permute-done((bf16[128,256]{1,0:T(8,128)(2,1)S(1)}, bf16[128,256]{1,0:T(8,128)(2,1)S(1)}, u32[]{:S(2)}, u32[]{:S(2)}) %collective-permute-start.1) | collective-permute-done | bytes 65568 | tf_op jit(solution)/shard_map/ppermute | solution.py:19
  11.1 1.4 %collective-permute-done.2 = bf16[128,256]{1,0:T(8,128)(2,1)S(1)} collective-permute-done((bf16[128,256]{1,0:T(8,128)(2,1)S(1)}, bf16[128,256]{1,0:T(8,128)(2,1)S(1)}, u32[]{:S(2)}, u32[]{:S(2)}) %collective-permute-start.2) | collective-permute-done | bytes 65568 | tf_op jit(solution)/shard_map/ppermute | solution.py:19
  12.6 0.0 copy-start.5
  12.6 1.6 %collective-permute-start.4 = (bf16[4,128,256]{2,1,0:T(8,128)(2,1)S(1)}, bf16[4,128,256]{2,1,0:T(8,128)(2,1)S(1)}, u32[]{:S(2)}, u32[]{:S(2)}) collective-permute-start(bf16[4,128,256]{2,1,0:T(8,128)(2,1)S(1)} %pad_maximum_fusion.refs_0_), channel_id=1, source_target_pairs={{0,4},{2,6},{4,0},{6,2},{8,12},{10,14},{12,8},{14,10},{16,20},{18,... | collective-permute-start | bytes 786440 | tf_op jit(solution)/shard_map/ppermute | solution.py:19
  14.2 0.0 collective-permute-start.3
  14.2 4.9 %collective-permute-done.4.refs_2_ = bf16[4,128,256]{2,1,0:T(8,128)(2,1)S(1)} collective-permute-done((bf16[4,128,256]{2,1,0:T(8,128)(2,1)S(1)}, bf16[4,128,256]{2,1,0:T(8,128)(2,1)S(1)}, u32[]{:S(2)}, u32[]{:S(2)}) %collective-permute-start.4) | collective-permute-done | bytes 262176 | tf_op jit(solution)/shard_map/ppermute | solution.py:19
  19.1 0.0 copy-start.6
  19.1 0.0 collective-permute-start.5
  19.1 0.7 %pad_add_fusion.cp_ref.place_ref = s32[2]{0:T(128)} fusion(s32[1]{0:T(128)} %bitcast.1, s32[1]{0:T(128)} %bitcast), kind=kLoop, calls=%fused_computation.3 | loop fusion | flops 2 | bytes 16 | tf_op jit(solution)/shard_map/stack | solution.py:171
  19.8 0.0 copy-start.1
  19.8 0.0 copy-start.2
  19.8 0.0 copy-start.3
  19.8 0.0 copy-start.4
  19.8 0.0 collective-permute-done.3.refs_1_
  19.8 0.0 copy-start.7
  19.8 0.8 %collective-permute-done.5.refs_3_ = bf16[4,128,256]{2,1,0:T(8,128)(2,1)S(1)} collective-permute-done((bf16[4,128,256]{2,1,0:T(8,128)(2,1)S(1)}, bf16[4,128,256]{2,1,0:T(8,128)(2,1)S(1)}, u32[]{:S(2)}, u32[]{:S(2)}) %collective-permute-start.5) | collective-permute-done | bytes 262176 | tf_op jit(solution)/shard_map/ppermute | solution.py:19
  20.6 0.0 copy-done.5
  20.6 0.0 copy-done.6
  20.6 0.0 copy-done.7
  20.6 0.0 copy-start.8
  20.7 0.7 %copy-done.8 = bf16[4,128,256]{2,1,0:T(8,128)(2,1)} copy-done((bf16[4,128,256]{2,1,0:T(8,128)(2,1)}, bf16[4,128,256]{2,1,0:T(8,128)(2,1)S(1)}, u32[]{:S(2)}) %copy-start.8) | copy-done | bytes 262168
  21.4 2.0 %select.1.prev_ref = bf16[4,128,256]{2,1,0:T(8,128)(2,1)} custom-call(s32[16]{0:T(128)} %order_ref.3, s32[2]{0:T(128)} %pad_add_fusion.cp_ref.place_ref, bf16[4,128,256]{2,1,0:T(8,128)(2,1)} %copy-done.5, bf16[4,128,256]{2,1,0:T(8,128)(2,1)} %copy-done.7, bf16[4,128,256]{2,1,0:T(8,128)(2,1)} %copy-done.6, bf16[4,128,256]{2,1,0:T(8,128)(2,1)} %copy-done.8), custom_call_target="tpu_custom_call" | custom-call | tf_op jit(solution)/shard_map/select/pallas_call | solution.py:135
  23.4 1.5 %collective-permute-start.7 = (bf16[4,128,256]{2,1,0:T(8,128)(2,1)}, bf16[4,128,256]{2,1,0:T(8,128)(2,1)S(1)}, u32[]{:S(2)}, u32[]{:S(2)}) collective-permute-start(bf16[4,128,256]{2,1,0:T(8,128)(2,1)} %select.1.prev_ref), channel_id=1, source_target_pairs={{0,1},{1,0},{2,3},{3,2},{4,5},{5,4},{6,7},{7,6},{8,9},{9,8},{10,11... | collective-permute-start | bytes 786440 | tf_op jit(solution)/shard_map/ppermute | solution.py:19
  24.9 0.5 %collective-permute-start.6 = (bf16[128,256]{1,0:T(8,128)(2,1)S(1)}, bf16[128,256]{1,0:T(8,128)(2,1)S(1)}, u32[]{:S(2)}, u32[]{:S(2)}) collective-permute-start(bf16[128,256]{1,0:T(8,128)(2,1)S(1)} %constant_dynamic-update-slice_fusion.own_ref), channel_id=1, source_target_pairs={{0,1},{1,0},{2,3},{3,2},{4,5},{5,4},{6,7},{7,6},{8,9},{9,8},{10,11... | collective-permute-start | bytes 196616 | tf_op jit(solution)/shard_map/ppermute | solution.py:19
  25.4 8.1 %collective-permute-done.6.other_own_ref = bf16[128,256]{1,0:T(8,128)(2,1)S(1)} collective-permute-done((bf16[128,256]{1,0:T(8,128)(2,1)S(1)}, bf16[128,256]{1,0:T(8,128)(2,1)S(1)}, u32[]{:S(2)}, u32[]{:S(2)}) %collective-permute-start.6) | collective-permute-done | bytes 65568 | tf_op jit(solution)/shard_map/ppermute | solution.py:19
  33.6 0.0 collective-permute-done.7.other_prev_ref
  33.6 0.0 copy-done.1
  33.6 0.0 copy-done.2
  33.6 0.0 copy-done.3
  33.6 0.0 copy-done.4
  33.6 0.0 copy-start
  33.6 0.9 %copy-done = bf16[4,128,256]{2,1,0:T(8,128)(2,1)S(1)} copy-done((bf16[4,128,256]{2,1,0:T(8,128)(2,1)S(1)}, bf16[4,128,256]{2,1,0:T(8,128)(2,1)}, u32[]{:S(2)}) %copy-start) | copy-done | bytes 262168
  34.6 7.1 %attend.1 = bf16[256,1024]{1,0:T(8,128)(2,1)} custom-call(s32[32]{0:T(128)S(1)} %copy-done.4, s32[16]{0:T(128)S(1)} %copy-done.2, s32[2]{0:T(128)S(1)} %copy-done.3, bf16[256,1024]{1,0:T(8,128)(2,1)S(1)} %copy-done.1, bf16[128,256]{1,0:T(8,128)(2,1)S(1)} %constant_dynamic-update-slice_fusion.own_ref, bf16[4,128,256]{2,1,0:T(8,128)(2,1)S(1)} %copy-done, ...), custom_call_target="tpu_custom_call" | custom-call | tf_op jit(solution)/shard_map/attend/pallas_call | solution.py:149
  (2 shorter events, 0.0 us)
Async XLA Ops:
  0.0 0.8 %copy-start.9 = (bf16[128,128]{1,0:T(8,128)(2,1)S(1)}, bf16[128,128]{1,0:T(8,128)(2,1)}, u32[]{:S(2)}) copy-start(bf16[128,128]{1,0:T(8,128)(2,1)} %param.7) | copy-start | bytes 98308
  0.8 5.7 %collective-permute-start = (bf16[128,256]{1,0:T(8,128)(2,1)S(1)}, bf16[128,256]{1,0:T(8,128)(2,1)S(1)}, u32[]{:S(2)}, u32[]{:S(2)}) collective-permute-start(bf16[128,256]{1,0:T(8,128)(2,1)S(1)} %constant_dynamic-update-slice_fusion.own_ref), channel_id=1, source_target_pairs={{0,8},{2,10},{4,12},{6,14},{8,0},{10,2},{12,4},{14,6},{16,24},{18,... | collective-permute-start | bytes 196616 | tf_op jit(solution)/shard_map/ppermute | solution.py:19
  3.9 7.3 %collective-permute-start.1 = (bf16[128,256]{1,0:T(8,128)(2,1)S(1)}, bf16[128,256]{1,0:T(8,128)(2,1)S(1)}, u32[]{:S(2)}, u32[]{:S(2)}) collective-permute-start(bf16[128,256]{1,0:T(8,128)(2,1)S(1)} %constant_dynamic-update-slice_fusion.own_ref), channel_id=1, source_target_pairs={{0,16},{2,18},{4,20},{6,22},{8,24},{10,26},{12,28},{14,30},{16,0},... | collective-permute-start | bytes 196616 | tf_op jit(solution)/shard_map/ppermute | solution.py:19
  6.5 6.1 %collective-permute-start.2 = (bf16[128,256]{1,0:T(8,128)(2,1)S(1)}, bf16[128,256]{1,0:T(8,128)(2,1)S(1)}, u32[]{:S(2)}, u32[]{:S(2)}) collective-permute-start(bf16[128,256]{1,0:T(8,128)(2,1)S(1)} %constant_dynamic-update-slice_fusion.own_ref), channel_id=1, source_target_pairs={{0,24},{2,26},{4,28},{6,30},{8,16},{10,18},{12,20},{14,22},{16,8},... | collective-permute-start | bytes 196616 | tf_op jit(solution)/shard_map/ppermute | solution.py:19
  12.6 8.0 %copy-start.5 = (bf16[4,128,256]{2,1,0:T(8,128)(2,1)}, bf16[4,128,256]{2,1,0:T(8,128)(2,1)S(1)}, u32[]{:S(2)}) copy-start(bf16[4,128,256]{2,1,0:T(8,128)(2,1)S(1)} %pad_maximum_fusion.refs_0_) | copy-start | bytes 786436
  12.6 6.5 %collective-permute-start.4 = (bf16[4,128,256]{2,1,0:T(8,128)(2,1)S(1)}, bf16[4,128,256]{2,1,0:T(8,128)(2,1)S(1)}, u32[]{:S(2)}, u32[]{:S(2)}) collective-permute-start(bf16[4,128,256]{2,1,0:T(8,128)(2,1)S(1)} %pad_maximum_fusion.refs_0_), channel_id=1, source_target_pairs={{0,4},{2,6},{4,0},{6,2},{8,12},{10,14},{12,8},{14,10},{16,20},{18,... | collective-permute-start | bytes 786440 | tf_op jit(solution)/shard_map/ppermute | solution.py:19
  14.2 5.6 %collective-permute-start.3 = (bf16[4,128,256]{2,1,0:T(8,128)(2,1)S(1)}, bf16[4,128,256]{2,1,0:T(8,128)(2,1)S(1)}, u32[]{:S(2)}, u32[]{:S(2)}) collective-permute-start(bf16[4,128,256]{2,1,0:T(8,128)(2,1)S(1)} %pad_maximum_fusion.refs_0_), channel_id=1, source_target_pairs={{0,2},{2,0},{4,6},{6,4},{8,10},{10,8},{12,14},{14,12},{16,18},{18,... | collective-permute-start | bytes 786440 | tf_op jit(solution)/shard_map/ppermute | solution.py:19
  19.1 1.5 %copy-start.6 = (bf16[4,128,256]{2,1,0:T(8,128)(2,1)}, bf16[4,128,256]{2,1,0:T(8,128)(2,1)S(1)}, u32[]{:S(2)}) copy-start(bf16[4,128,256]{2,1,0:T(8,128)(2,1)S(1)} %collective-permute-done.4.refs_2_) | copy-start | bytes 786436
  19.1 1.5 %collective-permute-start.5 = (bf16[4,128,256]{2,1,0:T(8,128)(2,1)S(1)}, bf16[4,128,256]{2,1,0:T(8,128)(2,1)S(1)}, u32[]{:S(2)}, u32[]{:S(2)}) collective-permute-start(bf16[4,128,256]{2,1,0:T(8,128)(2,1)S(1)} %collective-permute-done.4.refs_2_), channel_id=1, source_target_pairs={{0,2},{2,0},{4,6},{6,4},{8,10},{10,8},{12,14},{14,12},{16,18},{18,... | collective-permute-start | bytes 786440 | tf_op jit(solution)/shard_map/ppermute | solution.py:19
  19.8 13.8 %copy-start.1 = (bf16[256,1024]{1,0:T(8,128)(2,1)S(1)}, bf16[256,1024]{1,0:T(8,128)(2,1)}, u32[]{:S(2)}) copy-start(bf16[256,1024]{1,0:T(8,128)(2,1)} %q_ref.1) | copy-start | bytes 1572868
  19.8 13.8 %copy-start.2 = (s32[16]{0:T(128)S(1)}, s32[16]{0:T(128)}, u32[]{:S(2)}) copy-start(s32[16]{0:T(128)} %order_ref.3) | copy-start | bytes 196
  19.8 13.8 %copy-start.3 = (s32[2]{0:T(128)S(1)}, s32[2]{0:T(128)}, u32[]{:S(2)}) copy-start(s32[2]{0:T(128)} %pad_add_fusion.cp_ref.place_ref) | copy-start | bytes 28
  19.8 13.8 %copy-start.4 = (s32[32]{0:T(128)S(1)}, s32[32]{0:T(128)}, u32[]{:S(2)}) copy-start(s32[32]{0:T(128)} %doc_ref.1) | copy-start | bytes 388
  19.8 0.8 %copy-start.7 = (bf16[4,128,256]{2,1,0:T(8,128)(2,1)}, bf16[4,128,256]{2,1,0:T(8,128)(2,1)S(1)}, u32[]{:S(2)}) copy-start(bf16[4,128,256]{2,1,0:T(8,128)(2,1)S(1)} %collective-permute-done.3.refs_1_) | copy-start | bytes 786436
  20.6 0.7 %copy-start.8 = (bf16[4,128,256]{2,1,0:T(8,128)(2,1)}, bf16[4,128,256]{2,1,0:T(8,128)(2,1)S(1)}, u32[]{:S(2)}) copy-start(bf16[4,128,256]{2,1,0:T(8,128)(2,1)S(1)} %collective-permute-done.5.refs_3_) | copy-start | bytes 786436
  23.4 10.2 %collective-permute-start.7 = (bf16[4,128,256]{2,1,0:T(8,128)(2,1)}, bf16[4,128,256]{2,1,0:T(8,128)(2,1)S(1)}, u32[]{:S(2)}, u32[]{:S(2)}) collective-permute-start(bf16[4,128,256]{2,1,0:T(8,128)(2,1)} %select.1.prev_ref), channel_id=1, source_target_pairs={{0,1},{1,0},{2,3},{3,2},{4,5},{5,4},{6,7},{7,6},{8,9},{9,8},{10,11... | collective-permute-start | bytes 786440 | tf_op jit(solution)/shard_map/ppermute | solution.py:19
  24.9 8.6 %collective-permute-start.6 = (bf16[128,256]{1,0:T(8,128)(2,1)S(1)}, bf16[128,256]{1,0:T(8,128)(2,1)S(1)}, u32[]{:S(2)}, u32[]{:S(2)}) collective-permute-start(bf16[128,256]{1,0:T(8,128)(2,1)S(1)} %constant_dynamic-update-slice_fusion.own_ref), channel_id=1, source_target_pairs={{0,1},{1,0},{2,3},{3,2},{4,5},{5,4},{6,7},{7,6},{8,9},{9,8},{10,11... | collective-permute-start | bytes 196616 | tf_op jit(solution)/shard_map/ppermute | solution.py:19
  33.6 1.0 %copy-start = (bf16[4,128,256]{2,1,0:T(8,128)(2,1)S(1)}, bf16[4,128,256]{2,1,0:T(8,128)(2,1)}, u32[]{:S(2)}) copy-start(bf16[4,128,256]{2,1,0:T(8,128)(2,1)} %select.1.prev_ref) | copy-start | bytes 786436

commit v2 on v1

--- a/solution.py
+++ b/solution.py
@@ -38,13 +38,13 @@
                 out_ref[back - 1] = source[slot]
 
 
-def attend_half(half, span, doc_ref, q_ref, own_ref, prev_ref, buf, scores, max_ref, acc_ref, fresh):
+def fold_half(half, span, doc_ref, q_ref, own_ref, prev_ref, start_max, buf, scores, max_ref, acc_ref):
     reach = prev_ref.shape[0]
     heads = q_ref.shape[1] // HD
-    pairs = scores.shape[0]
     buf[0:BLK, 0 : 2 * HD] = own_ref[...]
     for back in range(reach):
         buf[(back + 1) * BLK : (back + 2) * BLK, 0 : 2 * HD] = prev_ref[back]
+    buf[:, 2 * HD :] = jnp.ones((buf.shape[0], HD), buf.dtype)
     rows = lax.broadcasted_iota(jnp.int32, (BLK, 2 * BLK), 0)
     cols = lax.broadcasted_iota(jnp.int32, (BLK, 2 * BLK), 1)
     for a in range(2):
@@ -57,15 +57,15 @@
             inside = (block >= 0) & (back >= first)
             count = count + jnp.where(same & inside, 1, 0)
         diagonal = half == a
-
-        if fresh:
+        steps = (count + 1) // 2
+        if start_max is None:
             max_ref[a] = jnp.full(max_ref.shape[1:], NEGATIVE, jnp.float32)
-            acc_ref[a] = jnp.zeros(acc_ref.shape[1:], jnp.float32)
+        else:
+            max_ref[a] = start_max[a]
+        acc_ref[a] = jnp.zeros(acc_ref.shape[1:], jnp.float32)
 
         @pl.when(count > 0)
         def _():
-            old_max = max_ref[a]
-
             def score_step(pair, unused):
                 start = pl.multiple_of((first + 2 * pair) * BLK, BLK)
                 key_pair = buf[pl.ds(start, 2 * BLK), 0:HD]
@@ -86,16 +86,10 @@
                     max_ref[a, h] = jnp.maximum(max_ref[a, h], best)
                 return unused
 
-            steps = (count + 1) // 2
             lax.fori_loop(0, steps, score_step, 0)
             for h in range(heads):
                 top = jnp.max(max_ref[a, h], axis=1, keepdims=True)
-                top = jnp.broadcast_to(top, (BLK, HD))
-                max_ref[a, h] = top
-                if not fresh:
-                    keep = jnp.exp2((old_max[h] - top) * SCALE2)
-                    acc_ref[a, h, :, 0:HD] = acc_ref[a, h, :, 0:HD] * keep
-                    acc_ref[a, h, :, HD:] = acc_ref[a, h, :, HD:] * keep
+                max_ref[a, h] = jnp.broadcast_to(top, (BLK, HD))
 
             def value_step(pair, unused):
                 start = pl.multiple_of((first + 2 * pair) * BLK, BLK)
@@ -111,19 +105,21 @@
             lax.fori_loop(0, steps, value_step, 0)
 
 
-def attend_kernel(
-    doc_ref, order_ref, place_ref, q_ref, own_ref, prev_ref, other_own_ref, other_prev_ref, out_ref,
-    buf, scores, max_ref, acc_ref,
+def first_kernel(doc_ref, order_ref, place_ref, q_ref, own_ref, prev_ref, max_ref, acc_ref, buf, scores):
+    span, half = order_ref[place_ref[0]], place_ref[1]
+    fold_half(half, span, doc_ref, q_ref, own_ref, prev_ref, None, buf, scores, max_ref, acc_ref)
+
+
+def second_kernel(
+    doc_ref, order_ref, place_ref, q_ref, own_ref, prev_ref, old_max, old_acc, out_ref, buf, scores, max_ref, acc_ref
 ):
-    span = order_ref[place_ref[0]]
-    half = place_ref[1]
-    heads = q_ref.shape[1] // HD
-    buf[:, 2 * HD :] = jnp.ones((buf.shape[0], HD), buf.dtype)
-    attend_half(half, span, doc_ref, q_ref, own_ref, prev_ref, buf, scores, max_ref, acc_ref, True)
-    attend_half(1 - half, span, doc_ref, q_ref, other_own_ref, other_prev_ref, buf, scores, max_ref, acc_ref, False)
+    span, half = order_ref[place_ref[0]], 1 - place_ref[1]
+    fold_half(half, span, doc_ref, q_ref, own_ref, prev_ref, old_max, buf, scores, max_ref, acc_ref)
     for a in range(2):
-        for h in range(heads):
-            result = acc_ref[a, h, :, 0:HD] / acc_ref[a, h, :, HD:]
+        for h in range(q_ref.shape[1] // HD):
+            keep = jnp.exp2((old_max[a, h] - max_ref[a, h]) * SCALE2)
+            total = old_acc[a, h, :, HD:] * keep + acc_ref[a, h, :, HD:]
+            result = (old_acc[a, h, :, 0:HD] * keep + acc_ref[a, h, :, 0:HD]) / total
             out_ref[a * BLK : (a + 1) * BLK, h * HD : (h + 1) * HD] = result.astype(out_ref.dtype)
 
 
@@ -137,29 +133,43 @@
         out_shape=jax.ShapeDtypeStruct((reach,) + sources[0].shape[1:], sources[0].dtype),
         in_specs=[SMEM, SMEM] + [VMEM] * len(sources),
         out_specs=VMEM,
+        compiler_params=pltpu.CompilerParams(vmem_limit_bytes=4 * 1024 * 1024),
         name="select",
     )(order, place, *sources)
 
 
-def attend(docs, order, place, queries, own, prev, other_own, other_prev):
+def attend(docs, order, place, queries, own, prev, state=None):
     reach = prev.shape[0]
     heads = queries.shape[1] // HD
     pairs = (reach + 1) // 2
-    slots = 2 * pairs + 1
+    max_shape, acc_shape = (2, heads, BLK, HD), (2, heads, BLK, 2 * HD)
+    scratch = [
+        pltpu.VMEM(((2 * pairs + 1) * BLK, 3 * HD), jnp.bfloat16),
+        pltpu.VMEM((pairs, heads, BLK, 2 * BLK), jnp.float32),
+    ]
+    shared = dict(
+        compiler_params=pltpu.CompilerParams(vmem_limit_bytes=12 * 1024 * 1024),
+        cost_estimate=pl.CostEstimate(flops=1 << 30, bytes_accessed=1 << 22, transcendentals=1 << 20),
+    )
+    if state is None:
+        return pl.pallas_call(
+            first_kernel,
+            out_shape=[jax.ShapeDtypeStruct(max_shape, jnp.float32), jax.ShapeDtypeStruct(acc_shape, jnp.float32)],
+            in_specs=[SMEM] * 3 + [VMEM] * 3,
+            out_specs=[VMEM, VMEM],
+            scratch_shapes=scratch,
+            name="attend_first",
+            **shared,
+        )(docs, order, place, queries, own, prev)
     return pl.pallas_call(
-        attend_kernel,
+        second_kernel,
         out_shape=jax.ShapeDtypeStruct(queries.shape, queries.dtype),
         in_specs=[SMEM] * 3 + [VMEM] * 5,
         out_specs=VMEM,
-        scratch_shapes=[
-            pltpu.VMEM((slots * BLK, 3 * HD), jnp.bfloat16),
-            pltpu.VMEM((pairs, heads, BLK, 2 * BLK), jnp.float32),
-            pltpu.VMEM((2, heads, BLK, HD), jnp.float32),
-            pltpu.VMEM((2, heads, BLK, 2 * HD), jnp.float32),
-        ],
-        compiler_params=pltpu.CompilerParams(vmem_limit_bytes=32 * 1024 * 1024),
-        name="attend",
-    )(docs, order, place, queries, own, prev, other_own, other_prev)
+        scratch_shapes=scratch + [pltpu.VMEM(max_shape, jnp.float32), pltpu.VMEM(acc_shape, jnp.float32)],
+        name="attend_second",
+        **shared,
+    )(docs, order, place, queries, own, prev, *state)
 
 
 def shards(cp_size, sp_size, queries, keys, values, doc_ids, span_order):
@@ -174,6 +184,7 @@
         side = flip(line, "cp", cp_size, 2)
         other_own = flip(own, "sp", sp_size, 1)
         core_line = flip(line, "cp", cp_size, 1)
+        side, other_own = lax.optimization_barrier((side, other_own))
         core_side = flip(side, "cp", cp_size, 1)
         prev = select(span_order, place, [line, core_line, side, core_side], reach)
         other_prev = flip(prev, "sp", sp_size, 1)
@@ -185,7 +196,8 @@
         chosen = pair[holder[back]]
         own, other_own = chosen[0, 0], chosen[0, 1]
         prev, other_prev = chosen[1:, 0], chosen[1:, 1]
-    return attend(doc_ids, span_order, place, queries, own, prev, other_own, other_prev)
+    state = attend(doc_ids, span_order, place, queries, own, prev)
+    return attend(doc_ids, span_order, place, queries, other_own, other_prev, state)
 
 
 def solution(mesh):

time: 41.9 us -> 35.9 us (0.86)
  waiting for transfers between devices: 20 us -> 13.1 us
  local copies, waits for them, and re-layouts: 2.47 us -> 4.54 us
  Pallas kernels: 9.14 us -> 7.59 us
  starting transfers between devices: 9.27 us -> 10.6 us
  other arithmetic: 0.71 us -> 0.11 us
    ppermute x8, waiting for transfers between devices: 20 us -> 13.1 us  [flip(): return lax.ppermute(array, axis, [(i, i ^ mask) for i in range(size)])]
    pallas_call x1, Pallas kernels: 2.04 us -> 0.7 us  [select(): pl.pallas_call(functools.partial(select_kernel, reach), out_shape=jax.Sha...]
    ppermute x8, starting transfers between devices: 9.27 us -> 10.6 us  [flip(): return lax.ppermute(array, axis, [(i, i ^ mask) for i in range(size)])]
    unnamed x21 -> x9, local copies, waits for them, and re-layouts: 2.46 us -> 3.77 us
    concatenate x1, local copies, waits for them, and re-layouts: 0.01 us -> 0.77 us  [shards(): own = jnp.concatenate([keys, values], axis=1)]
    another operation x1, other arithmetic: 0.68 us -> 0.07 us  [shards(): place = jnp.stack([cp_index, lax.axis_index('sp').astype(jnp.int32)])]
    pallas_call x1 -> x2, Pallas kernels: 7.1 us -> 6.89 us  [the longest x1 4.39 us: attend(): pl.pallas_call(second_kernel, out_shape=jax.ShapeDtypeStruct(queries.shap...]
  transfers between devices with their start and end apart: 8 -> 8, of which waited for: 5 -> 6; matrix products, arithmetic and copies ran while one was open for 2% -> 0% of each run, Pallas kernels for 0% -> 7%
where the time goes in v2:
time: 35.9 us
  waiting for transfers between devices  13.1 us (36%)
  starting transfers between devices  10.6 us (30%)
  Pallas kernels  7.59 us (21%)
  local copies, waits for them, and re-layouts  4.54 us (13%)
    ppermute x8, waiting for transfers between devices, flip(): return lax.ppermute(array, axis, [(i, i ^ mask) for i in range(size)])  13.1 us
    ppermute x8, starting transfers between devices, flip(): return lax.ppermute(array, axis, [(i, i ^ mask) for i in range(size)])  10.6 us
    pallas_call x1, Pallas kernels, attend(): pl.pallas_call(second_kernel, out_shape=jax.ShapeDtypeStruct(queries.shap...  4.39 us
    unnamed x9, local copies, waits for them, and re-layouts  3.77 us
    pallas_call x1, Pallas kernels, attend(): pl.pallas_call(first_kernel, out_shape=[jax.ShapeDtypeStruct(max_shape, j...  2.5 us
    concatenate x1, local copies, waits for them, and re-layouts, shards(): own = jnp.concatenate([keys, values], axis=1)  0.77 us
  transfers between devices with their start and end apart: 8, of which 6 were waited for; matrix products, arithmetic and copies ran while one was open for 0% of the time, Pallas kernels for 7%

profile of v2, /device:TPU:0, one launch (start us, length us, event | category | flops | bytes accessed | tf_op | source)
XLA Modules:
  0.0 35.9 jit_solution(13920191157757739060)
XLA Ops:
  0.0 0.8 %constant_dynamic-update-slice_fusion.1 = bf16[128,256]{1,0:T(8,128)(2,1)S(1)} fusion(bf16[128,128]{1,0:T(8,128)(2,1)} %param.6), kind=kLoop, calls=%fused_computation.2 | loop fusion | bytes 65536
  0.8 0.8 %constant_dynamic-update-slice_fusion.own_ref = bf16[128,256]{1,0:T(8,128)(2,1)S(1)} fusion(bf16[128,256]{1,0:T(8,128)(2,1)S(1)} %constant_dynamic-update-slice_fusion.1, bf16[128,128]{1,0:T(8,128)(2,1)} %param.7), kind=kLoop, calls=%fused_computation.1 | loop fusion | bytes 65536 | tf_op jit(solution)/shard_map/concatenate | solution.py:179
  1.5 5.1 %collective-permute-start.2 = (bf16[128,256]{1,0:T(8,128)(2,1)S(1)}, bf16[128,256]{1,0:T(8,128)(2,1)S(1)}, u32[]{:S(2)}, u32[]{:S(2)}) collective-permute-start(bf16[128,256]{1,0:T(8,128)(2,1)S(1)} %constant_dynamic-update-slice_fusion.own_ref), channel_id=1, source_target_pairs={{0,24},{2,26},{4,28},{6,30},{8,16},{10,18},{12,20},{14,22},{16,8},... | collective-permute-start | bytes 196616 | tf_op jit(solution)/shard_map/ppermute | solution.py:19
  6.6 0.0 collective-permute-start.1
  6.6 0.6 %collective-permute-start = (bf16[128,256]{1,0:T(8,128)(2,1)S(1)}, bf16[128,256]{1,0:T(8,128)(2,1)S(1)}, u32[]{:S(2)}, u32[]{:S(2)}) collective-permute-start(bf16[128,256]{1,0:T(8,128)(2,1)S(1)} %constant_dynamic-update-slice_fusion.own_ref), channel_id=1, source_target_pairs={{0,8},{2,10},{4,12},{6,14},{8,0},{10,2},{12,4},{14,6},{16,24},{18,... | collective-permute-start | bytes 196616 | tf_op jit(solution)/shard_map/ppermute | solution.py:19
  7.3 1.9 %collective-permute-done.2 = bf16[128,256]{1,0:T(8,128)(2,1)S(1)} collective-permute-done((bf16[128,256]{1,0:T(8,128)(2,1)S(1)}, bf16[128,256]{1,0:T(8,128)(2,1)S(1)}, u32[]{:S(2)}, u32[]{:S(2)}) %collective-permute-start.2) | collective-permute-done | bytes 65568 | tf_op jit(solution)/shard_map/ppermute | solution.py:19
  9.2 3.0 %collective-permute-done.1 = bf16[128,256]{1,0:T(8,128)(2,1)S(1)} collective-permute-done((bf16[128,256]{1,0:T(8,128)(2,1)S(1)}, bf16[128,256]{1,0:T(8,128)(2,1)S(1)}, u32[]{:S(2)}, u32[]{:S(2)}) %collective-permute-start.1) | collective-permute-done | bytes 65568 | tf_op jit(solution)/shard_map/ppermute | solution.py:19
  12.2 0.0 collective-permute-done
  12.3 1.6 %collective-permute-start.3 = (bf16[4,128,256]{2,1,0:T(8,128)(2,1)S(1)}, bf16[4,128,256]{2,1,0:T(8,128)(2,1)S(1)}, u32[]{:S(2)}, u32[]{:S(2)}) collective-permute-start(bf16[4,128,256]{2,1,0:T(8,128)(2,1)S(1)} %pad_maximum_fusion.refs_0_), channel_id=1, source_target_pairs={{0,4},{2,6},{4,0},{6,2},{8,12},{10,14},{12,8},{14,10},{16,20},{18,... | collective-permute-start | bytes 786440 | tf_op jit(solution)/shard_map/ppermute | solution.py:19
  13.8 1.5 %collective-permute-start.4 = (bf16[128,256]{1,0:T(8,128)(2,1)S(1)}, bf16[128,256]{1,0:T(8,128)(2,1)S(1)}, u32[]{:S(2)}, u32[]{:S(2)}) collective-permute-start(bf16[128,256]{1,0:T(8,128)(2,1)S(1)} %constant_dynamic-update-slice_fusion.own_ref), channel_id=1, source_target_pairs={{0,1},{1,0},{2,3},{3,2},{4,5},{5,4},{6,7},{7,6},{8,9},{9,8},{10,11... | collective-permute-start | bytes 196616 | tf_op jit(solution)/shard_map/ppermute | solution.py:19
  15.4 0.0 collective-permute-start.5
  15.4 2.7 %collective-permute-done.4.own_ref = bf16[128,256]{1,0:T(8,128)(2,1)S(1)} collective-permute-done((bf16[128,256]{1,0:T(8,128)(2,1)S(1)}, bf16[128,256]{1,0:T(8,128)(2,1)S(1)}, u32[]{:S(2)}, u32[]{:S(2)}) %collective-permute-start.4) | collective-permute-done | bytes 65568 | tf_op jit(solution)/shard_map/ppermute | solution.py:19
  18.1 2.1 %collective-permute-done.3.refs_2_ = bf16[4,128,256]{2,1,0:T(8,128)(2,1)S(1)} collective-permute-done((bf16[4,128,256]{2,1,0:T(8,128)(2,1)S(1)}, bf16[4,128,256]{2,1,0:T(8,128)(2,1)S(1)}, u32[]{:S(2)}, u32[]{:S(2)}) %collective-permute-start.3) | collective-permute-done | bytes 262176 | tf_op jit(solution)/shard_map/ppermute | solution.py:19
  20.2 0.0 collective-permute-start.6
  20.2 0.1 pad_add_fusion.cp_ref.place_ref
  20.3 0.0 collective-permute-done.5.refs_1_
  20.3 1.5 %collective-permute-done.6.refs_3_ = bf16[4,128,256]{2,1,0:T(8,128)(2,1)S(1)} collective-permute-done((bf16[4,128,256]{2,1,0:T(8,128)(2,1)S(1)}, bf16[4,128,256]{2,1,0:T(8,128)(2,1)S(1)}, u32[]{:S(2)}, u32[]{:S(2)}) %collective-permute-start.6) | collective-permute-done | bytes 262176 | tf_op jit(solution)/shard_map/ppermute | solution.py:19
  21.8 0.0 copy-start.1
  21.8 0.7 %copy-done.1 = s32[16]{0:T(128)S(1)} copy-done((s32[16]{0:T(128)S(1)}, s32[16]{0:T(128)}, u32[]{:S(2)}) %copy-start.1) | copy-done | bytes 88
  22.4 0.7 %select.1.prev_ref = bf16[4,128,256]{2,1,0:T(8,128)(2,1)S(1)} custom-call(s32[16]{0:T(128)S(1)} %copy-done.1, s32[2]{0:T(128)S(1)} %pad_add_fusion.cp_ref.place_ref, bf16[4,128,256]{2,1,0:T(8,128)(2,1)S(1)} %pad_maximum_fusion.refs_0_, bf16[4,128,256]{2,1,0:T(8,128)(2,1)S(1)} %collective-permute-done.5.refs_1_, ...), custom_call_target="tpu_custom_call" | custom-call | tf_op jit(solution)/shard_map/select/pallas_call | solution.py:131
  23.1 1.8 %collective-permute-start.7 = (bf16[4,128,256]{2,1,0:T(8,128)(2,1)S(1)}, bf16[4,128,256]{2,1,0:T(8,128)(2,1)S(1)}, u32[]{:S(2)}, u32[]{:S(2)}) collective-permute-start(bf16[4,128,256]{2,1,0:T(8,128)(2,1)S(1)} %select.1.prev_ref), channel_id=1, source_target_pairs={{0,1},{1,0},{2,3},{3,2},{4,5},{5,4},{6,7},{7,6},{8,9},{9,8},{10,11... | collective-permute-start | bytes 786440 | tf_op jit(solution)/shard_map/ppermute | solution.py:19
  24.9 0.0 copy-start
  24.9 1.0 %copy-done = bf16[256,1024]{1,0:T(8,128)(2,1)S(1)} copy-done((bf16[256,1024]{1,0:T(8,128)(2,1)S(1)}, bf16[256,1024]{1,0:T(8,128)(2,1)}, u32[]{:S(2)}) %copy-start) | copy-done | bytes 524312
  25.9 0.0 copy-start.2
  25.9 0.7 %copy-done.2 = s32[16]{0:T(128)S(1)} copy-done((s32[16]{0:T(128)S(1)}, s32[16]{0:T(128)}, u32[]{:S(2)}) %copy-start.2) | copy-done | bytes 88
  26.6 0.0 copy-start.3
  26.6 0.7 %copy-done.3 = s32[32]{0:T(128)S(1)} copy-done((s32[32]{0:T(128)S(1)}, s32[32]{0:T(128)}, u32[]{:S(2)}) %copy-start.3) | copy-done | bytes 152
  27.2 2.5 %attend_first.1 = (f32[2,8,128,128]{3,2,1,0:T(8,128)S(1)}, f32[2,8,128,256]{3,2,1,0:T(8,128)S(1)}) custom-call(s32[32]{0:T(128)S(1)} %copy-done.3, s32[16]{0:T(128)S(1)} %copy-done.2, s32[2]{0:T(128)S(1)} %pad_add_fusion.cp_ref.place_ref, bf16[256,1024]{1,0:T(8,128)(2,1)S(1)} %copy-done, bf16[128,256]{1,0:T(8,128)(2,1)S(1)} %constant_dynamic-update-slice_fusion.own_ref, ...), custom_call_target="tpu_custom_call" | custom-call | flops 1073741824 | bytes 4194304 | tf_op jit(solution)/shard_map/attend_first/pallas_call | solution.py:155
  29.8 1.8 %collective-permute-done.7.prev_ref = bf16[4,128,256]{2,1,0:T(8,128)(2,1)S(1)} collective-permute-done((bf16[4,128,256]{2,1,0:T(8,128)(2,1)S(1)}, bf16[4,128,256]{2,1,0:T(8,128)(2,1)S(1)}, u32[]{:S(2)}, u32[]{:S(2)}) %collective-permute-start.7) | collective-permute-done | bytes 262176 | tf_op jit(solution)/shard_map/ppermute | solution.py:19
  31.5 4.4 %attend_second.1 = bf16[256,1024]{1,0:T(8,128)(2,1)} custom-call(s32[32]{0:T(128)S(1)} %copy-done.3, s32[16]{0:T(128)S(1)} %copy-done.2, s32[2]{0:T(128)S(1)} %pad_add_fusion.cp_ref.place_ref, bf16[256,1024]{1,0:T(8,128)(2,1)S(1)} %copy-done, bf16[128,256]{1,0:T(8,128)(2,1)S(1)} %collective-permute-done.4.own_ref, ...), custom_call_target="tpu_custom_call" | custom-call | flops 1073741824 | bytes 4194304 | tf_op jit(solution)/shard_map/attend_second/pallas_call | solution.py:164
  (1 shorter events, 0.0 us)
Async XLA Ops:
  1.5 7.7 %collective-permute-start.2 = (bf16[128,256]{1,0:T(8,128)(2,1)S(1)}, bf16[128,256]{1,0:T(8,128)(2,1)S(1)}, u32[]{:S(2)}, u32[]{:S(2)}) collective-permute-start(bf16[128,256]{1,0:T(8,128)(2,1)S(1)} %constant_dynamic-update-slice_fusion.own_ref), channel_id=1, source_target_pairs={{0,24},{2,26},{4,28},{6,30},{8,16},{10,18},{12,20},{14,22},{16,8},... | collective-permute-start | bytes 196616 | tf_op jit(solution)/shard_map/ppermute | solution.py:19
  6.6 5.6 %collective-permute-start.1 = (bf16[128,256]{1,0:T(8,128)(2,1)S(1)}, bf16[128,256]{1,0:T(8,128)(2,1)S(1)}, u32[]{:S(2)}, u32[]{:S(2)}) collective-permute-start(bf16[128,256]{1,0:T(8,128)(2,1)S(1)} %constant_dynamic-update-slice_fusion.own_ref), channel_id=1, source_target_pairs={{0,16},{2,18},{4,20},{6,22},{8,24},{10,26},{12,28},{14,30},{16,0},... | collective-permute-start | bytes 196616 | tf_op jit(solution)/shard_map/ppermute | solution.py:19
  6.6 5.6 %collective-permute-start = (bf16[128,256]{1,0:T(8,128)(2,1)S(1)}, bf16[128,256]{1,0:T(8,128)(2,1)S(1)}, u32[]{:S(2)}, u32[]{:S(2)}) collective-permute-start(bf16[128,256]{1,0:T(8,128)(2,1)S(1)} %constant_dynamic-update-slice_fusion.own_ref), channel_id=1, source_target_pairs={{0,8},{2,10},{4,12},{6,14},{8,0},{10,2},{12,4},{14,6},{16,24},{18,... | collective-permute-start | bytes 196616 | tf_op jit(solution)/shard_map/ppermute | solution.py:19
  12.3 7.9 %collective-permute-start.3 = (bf16[4,128,256]{2,1,0:T(8,128)(2,1)S(1)}, bf16[4,128,256]{2,1,0:T(8,128)(2,1)S(1)}, u32[]{:S(2)}, u32[]{:S(2)}) collective-permute-start(bf16[4,128,256]{2,1,0:T(8,128)(2,1)S(1)} %pad_maximum_fusion.refs_0_), channel_id=1, source_target_pairs={{0,4},{2,6},{4,0},{6,2},{8,12},{10,14},{12,8},{14,10},{16,20},{18,... | collective-permute-start | bytes 786440 | tf_op jit(solution)/shard_map/ppermute | solution.py:19
  13.8 4.3 %collective-permute-start.4 = (bf16[128,256]{1,0:T(8,128)(2,1)S(1)}, bf16[128,256]{1,0:T(8,128)(2,1)S(1)}, u32[]{:S(2)}, u32[]{:S(2)}) collective-permute-start(bf16[128,256]{1,0:T(8,128)(2,1)S(1)} %constant_dynamic-update-slice_fusion.own_ref), channel_id=1, source_target_pairs={{0,1},{1,0},{2,3},{3,2},{4,5},{5,4},{6,7},{7,6},{8,9},{9,8},{10,11... | collective-permute-start | bytes 196616 | tf_op jit(solution)/shard_map/ppermute | solution.py:19
  15.4 4.9 %collective-permute-start.5 = (bf16[4,128,256]{2,1,0:T(8,128)(2,1)S(1)}, bf16[4,128,256]{2,1,0:T(8,128)(2,1)S(1)}, u32[]{:S(2)}, u32[]{:S(2)}) collective-permute-start(bf16[4,128,256]{2,1,0:T(8,128)(2,1)S(1)} %pad_maximum_fusion.refs_0_), channel_id=1, source_target_pairs={{0,2},{2,0},{4,6},{6,4},{8,10},{10,8},{12,14},{14,12},{16,18},{18,... | collective-permute-start | bytes 786440 | tf_op jit(solution)/shard_map/ppermute | solution.py:19
  20.2 1.5 %collective-permute-start.6 = (bf16[4,128,256]{2,1,0:T(8,128)(2,1)S(1)}, bf16[4,128,256]{2,1,0:T(8,128)(2,1)S(1)}, u32[]{:S(2)}, u32[]{:S(2)}) collective-permute-start(bf16[4,128,256]{2,1,0:T(8,128)(2,1)S(1)} %collective-permute-done.3.refs_2_), channel_id=1, source_target_pairs={{0,2},{2,0},{4,6},{6,4},{8,10},{10,8},{12,14},{14,12},{16,18},{18,... | collective-permute-start | bytes 786440 | tf_op jit(solution)/shard_map/ppermute | solution.py:19
  21.8 0.7 %copy-start.1 = (s32[16]{0:T(128)S(1)}, s32[16]{0:T(128)}, u32[]{:S(2)}) copy-start(s32[16]{0:T(128)} %order_ref.5) | copy-start | bytes 196
  23.1 8.4 %collective-permute-start.7 = (bf16[4,128,256]{2,1,0:T(8,128)(2,1)S(1)}, bf16[4,128,256]{2,1,0:T(8,128)(2,1)S(1)}, u32[]{:S(2)}, u32[]{:S(2)}) collective-permute-start(bf16[4,128,256]{2,1,0:T(8,128)(2,1)S(1)} %select.1.prev_ref), channel_id=1, source_target_pairs={{0,1},{1,0},{2,3},{3,2},{4,5},{5,4},{6,7},{7,6},{8,9},{9,8},{10,11... | collective-permute-start | bytes 786440 | tf_op jit(solution)/shard_map/ppermute | solution.py:19
  24.9 1.0 %copy-start = (bf16[256,1024]{1,0:T(8,128)(2,1)S(1)}, bf16[256,1024]{1,0:T(8,128)(2,1)}, u32[]{:S(2)}) copy-start(bf16[256,1024]{1,0:T(8,128)(2,1)} %q_ref.3) | copy-start | bytes 1572868
  25.9 0.7 %copy-start.2 = (s32[16]{0:T(128)S(1)}, s32[16]{0:T(128)}, u32[]{:S(2)}) copy-start(s32[16]{0:T(128)} %order_ref.5) | copy-start | bytes 196
  26.6 0.7 %copy-start.3 = (s32[32]{0:T(128)S(1)}, s32[32]{0:T(128)}, u32[]{:S(2)}) copy-start(s32[32]{0:T(128)} %doc_ref.3) | copy-start | bytes 388

commit v3 on v0

v3 whole, which is shorter than its diff:
```python
import functools
import math

import jax
import jax.numpy as jnp
from jax import lax
from jax.experimental import pallas as pl
from jax.experimental.pallas import tpu as pltpu
from jax.sharding import PartitionSpec as P

HD = 128
SPAN = 256
BLK = 128
NEGATIVE = -1e30
HEAD = 2
SCALE2 = math.log2(math.e) / math.sqrt(HD)


def flip(array, axis, size, mask):
    return lax.ppermute(array, axis, [(i, i ^ mask) for i in range(size)])


def select_kernel(places, meta_ref, *refs):
    sources, out_ref = refs[:-1], refs[-1]
    cp = meta_ref[0]
    own_span = meta_ref[HEAD + cp]
    for back in range(1, out_ref.shape[0] // BLK + 1):
        span = jnp.maximum(own_span - back, 0)
        holder = jnp.int32(0)
        for index in range(len(places)):
            holder = jnp.where(meta_ref[HEAD + index] == span, jnp.int32(index), holder)
        apart = holder ^ cp
        for distance, (source, slot) in enumerate(places):

            @pl.when(apart == distance)
            def _():
                out_ref[(back - 1) * BLK : back * BLK, :] = sources[source][slot]


def layout(meta_ref, cp_size):
    span = meta_ref[HEAD + meta_ref[0]]
    doc_at = HEAD + cp_size
    return span, doc_at, meta_ref[doc_at + 2 * span] == meta_ref[doc_at + 2 * span + 1]


def earlier_count(meta_ref, span, doc_at, half, reach):
    doc = meta_ref[doc_at + 2 * span]
    count = jnp.int32(0)
    for back in range(1, reach + 1):
        block = 2 * (span - back) + half
        held = (block >= 0) & (meta_ref[doc_at + jnp.maximum(block, 0)] == doc)
        count = count + jnp.where(held, 1, 0)
    return count


def score(q_ref, a, h, keys):
    return lax.dot_general(
        q_ref[a * BLK : (a + 1) * BLK, h * HD : (h + 1) * HD],
        keys,
        (((1,), (1,)), ((), ())),
        preferred_element_type=jnp.float32,
    )


def weigh(scores, top):
    parts = [jnp.exp2((scores[:, c : c + BLK] - top) * SCALE2) for c in range(0, scores.shape[1], BLK)]
    return jnp.concatenate(parts, axis=1).astype(jnp.bfloat16)


def with_ones(values):
    return jnp.concatenate([values, jnp.ones_like(values)], axis=1)


def fold(a, count, q_ref, buf, scores, max_ref, acc_ref, own):
    heads = q_ref.shape[1] // HD
    pairs = count // 2
    odd = count % 2 == 1

    def keep(pair, h, block):
        best = block[:, :BLK]
        if block.shape[1] > BLK:
            best = jnp.maximum(best, block[:, BLK:])
        scores[pair, h, :, : block.shape[1]] = block
        max_ref[a, h] = jnp.maximum(max_ref[a, h], best)

    def score_step(pair, unused):
        keys = buf[pl.ds(pl.multiple_of(pair * 2 * BLK, BLK), 2 * BLK), 0:HD]
        for h in range(heads):
            keep(pair, h, score(q_ref, a, h, keys))
        return unused

    if own is not None:
        own_rows, own_bias = own
        width = own_bias.shape[1]
        last = scores.shape[0] - 1
        for h in range(heads):
            block = score(q_ref, a, h, own_rows[:, 0:HD]) + own_bias
            scores[last, h, :, :width] = block
            max_ref[a, h] = jnp.maximum(block[:, :BLK], block[:, width - BLK :])
    lax.fori_loop(0, pairs, score_step, 0)

    @pl.when(odd)
    def _():
        keys = buf[pl.ds(pl.multiple_of(pairs * 2 * BLK, BLK), BLK), 0:HD]
        for h in range(heads):
            keep(pairs, h, score(q_ref, a, h, keys))

    for h in range(heads):
        top = jnp.max(max_ref[a, h], axis=1, keepdims=True)
        max_ref[a, h] = jnp.broadcast_to(top, (BLK, HD))

    def value_step(pair, unused):
        values = with_ones(buf[pl.ds(pl.multiple_of(pair * 2 * BLK, BLK), 2 * BLK), HD:])
        for h in range(heads):
            weights = weigh(scores[pair, h], max_ref[a, h])
            acc_ref[a, h] += jnp.dot(weights, values, preferred_element_type=jnp.float32)
        return unused

    if own is not None:
        values = with_ones(own_rows[:, HD:])
        for h in range(heads):
            weights = weigh(scores[last, h, :, :width], max_ref[a, h])
            acc_ref[a, h] = jnp.dot(weights, values, preferred_element_type=jnp.float32)
    lax.fori_loop(0, pairs, value_step, 0)

    @pl.when(odd)
    def _():
        values = with_ones(buf[pl.ds(pl.multiple_of(pairs * 2 * BLK, BLK), BLK), HD:])
        for h in range(heads):
            weights = weigh(scores[pairs, h, :, :BLK], max_ref[a, h])
            acc_ref[a, h] += jnp.dot(weights, values, preferred_element_type=jnp.float32)


def first_kernel(cp_size, meta_ref, q_ref, own_ref, other_ref, prev_ref, max_ref, acc_ref, scores):
    half = meta_ref[1]
    span, doc_at, same = layout(meta_ref, cp_size)
    count = earlier_count(meta_ref, span, doc_at, half, prev_ref.shape[0] // BLK)
    swap = half == 1
    mine, other = own_ref[...], other_ref[...]
    low, high = jnp.where(swap, other, mine), jnp.where(swap, mine, other)
    rows = lax.broadcasted_iota(jnp.int32, (BLK, BLK), 0)
    cols = lax.broadcasted_iota(jnp.int32, (BLK, BLK), 1)
    causal = jnp.where(cols <= rows, 0.0, NEGATIVE)
    before = jnp.where(same, jnp.zeros_like(causal), NEGATIVE)
    fold(0, count, q_ref, prev_ref, scores, max_ref, acc_ref, (low, causal))
    both = jnp.concatenate([low, high], axis=0), jnp.concatenate([before, causal], axis=1)
    fold(1, jnp.where(same, count, 0), q_ref, prev_ref, scores, max_ref, acc_ref, both)


def second_kernel(cp_size, meta_ref, q_ref, prev_ref, old_max, old_acc, out_ref, scores, max_ref, acc_ref):
    half = 1 - meta_ref[1]
    span, doc_at, same = layout(meta_ref, cp_size)
    count = earlier_count(meta_ref, span, doc_at, half, prev_ref.shape[0] // BLK)
    for a in range(2):
        used = count if a == 0 else jnp.where(same, count, 0)
        rows = slice(a * BLK, (a + 1) * BLK)

        @pl.when(used == 0)
        def _():
            for h in range(q_ref.shape[1] // HD):
                result = old_acc[a, h, :, 0:HD] / old_acc[a, h, :, HD:]
                out_ref[rows, h * HD : (h + 1) * HD] = result.astype(out_ref.dtype)

        @pl.when(used > 0)
        def _():
            max_ref[a] = old_max[a]
            acc_ref[a] = jnp.zeros(acc_ref.shape[1:], jnp.float32)
            fold(a, used, q_ref, prev_ref, scores, max_ref, acc_ref, None)
            for h in range(q_ref.shape[1] // HD):
                fade = jnp.exp2((old_max[a, h] - max_ref[a, h]) * SCALE2)
                total = old_acc[a, h, :, HD:] * fade + acc_ref[a, h, :, HD:]
                result = (old_acc[a, h, :, 0:HD] * fade + acc_ref[a, h, :, 0:HD]) / total
                out_ref[rows, h * HD : (h + 1) * HD] = result.astype(out_ref.dtype)


VMEM = pl.BlockSpec(memory_space=pltpu.VMEM)
SMEM = pl.BlockSpec(memory_space=pltpu.SMEM)
SHARED = dict(
    compiler_params=pltpu.CompilerParams(vmem_limit_bytes=16 * 1024 * 1024),
    cost_estimate=pl.CostEstimate(flops=1 << 30, bytes_accessed=1 << 22, transcendentals=1 << 20),
)


def select(meta, sources, places, reach):
    return pl.pallas_call(
        functools.partial(select_kernel, places),
        out_shape=jax.ShapeDtypeStruct((reach * BLK, 2 * HD), jnp.bfloat16),
        in_specs=[SMEM] + [VMEM] * len(sources),
        out_specs=VMEM,
        compiler_params=pltpu.CompilerParams(vmem_limit_bytes=4 * 1024 * 1024),
        name="select",
    )(meta, *sources)


def attend_first(cp_size, meta, queries, own, other, prev):
    heads = queries.shape[1] // HD
    pairs = prev.shape[0] // (2 * BLK)
    max_shape, acc_shape = (2, heads, BLK, HD), (2, heads, BLK, 2 * HD)
    return pl.pallas_call(
        functools.partial(first_kernel, cp_size),
        out_shape=[jax.ShapeDtypeStruct(max_shape, jnp.float32), jax.ShapeDtypeStruct(acc_shape, jnp.float32)],
        in_specs=[SMEM] + [VMEM] * 4,
        out_specs=[VMEM, VMEM],
        scratch_shapes=[pltpu.VMEM((pairs + 1, heads, BLK, 2 * BLK), jnp.float32)],
        name="attend_first",
        **SHARED,
    )(meta, queries, own, other, prev)


def attend_second(cp_size, meta, queries, prev, state):
    heads = queries.shape[1] // HD
    pairs = prev.shape[0] // (2 * BLK)
    return pl.pallas_call(
        functools.partial(second_kernel, cp_size),
        out_shape=jax.ShapeDtypeStruct(queries.shape, queries.dtype),
        in_specs=[SMEM] + [VMEM] * 4,
        out_specs=VMEM,
        scratch_shapes=[pltpu.VMEM((pairs, heads, BLK, 2 * BLK), jnp.float32)]
        + [pltpu.VMEM(part.shape, jnp.float32) for part in state],
        name="attend_second",
        **SHARED,
    )(meta, queries, prev, *state)


def shards(cp_size, sp_size, queries, keys, values, doc_ids, span_order):
    reach = doc_ids.shape[0] // 8
    staged = cp_size == 16 and sp_size == 2
    cp_index = lax.axis_index("cp").astype(jnp.int32)
    half = lax.axis_index("sp").astype(jnp.int32) if staged else jnp.int32(0)
    meta = jnp.concatenate([jnp.stack([cp_index, half]), span_order, doc_ids])
    own = lax.pad(keys, jnp.bfloat16(0), ((0, 0, 0), (0, HD, 0)))
    own = own + lax.pad(values, jnp.bfloat16(0), ((0, 0, 0), (HD, 0, 0)))
    if staged:
        by_x = lambda array: flip(array, "cp", cp_size, 2)
        by_y = lambda array: flip(array, "sp", sp_size, 1)
        by_core = lambda array: flip(array, "cp", cp_size, 1)
        far = {j: flip(own, "cp", cp_size, 4 * j) for j in (3, 2, 1)}
        far[0] = own
        other = by_y(own)
        sources, places = [], {}
        for group in ((3, 0), (1, 2)):
            line = jnp.stack([far[j] for j in group])
            side, meta, other = lax.optimization_barrier((by_x(line), meta, other))
            for flips, array in ((0, line), (2, side), (1, by_core(line)), (3, by_core(side))):
                for slot, j in enumerate(group):
                    places[4 * j ^ flips] = (len(sources), slot)
                sources.append(array)
        prev = select(meta, sources, [places[distance] for distance in range(cp_size)], reach)
        other_prev = by_y(prev)
    else:
        pair = lax.all_gather(own, ("cp", "sp"), axis=0, tiled=True).reshape(cp_size, 2, BLK, 2 * HD)
        holder = jnp.argsort(span_order)
        back = jnp.maximum(span_order[cp_index] - jnp.arange(reach + 1, dtype=jnp.int32), 0)
        chosen = pair[holder[back]]
        own, other = chosen[0, 0], chosen[0, 1]
        prev, other_prev = (chosen[1:, k].reshape(reach * BLK, 2 * HD) for k in (0, 1))
    state = attend_first(cp_size, meta, queries, own, other, prev)
    return attend_second(cp_size, meta, queries, other_prev, state)


def solution(mesh):
    in_specs = (P("cp", "sp"), P(("cp", "sp"), None), P(("cp", "sp"), None), P(), P())
    out_specs = P("cp", "sp")
    body = functools.partial(shards, mesh.shape["cp"], mesh.shape["sp"])
    return jax.shard_map(body, mesh=mesh, in_specs=in_specs, out_specs=out_specs, check_vma=False)
```

time: 203 us -> 32.5 us (0.16)
  matrix products: 67.7 us -> 0 us
  waiting for transfers between devices: 70.8 us -> 8.39 us
  other arithmetic: 15.7 us -> 1.56 us
  between operations: 13.5 us -> 0.05 us
  starting transfers between devices: 0.04 us -> 13.3 us
  blocking collectives: 12.2 us -> 0 us
  local copies, waits for them, and re-layouts: 11.4 us -> 1.04 us
  loops' own time: 9.85 us -> 0 us
  Pallas kernels: 0 us -> 7.7 us
    all_gather x2 -> x0, waiting for transfers between devices: 70.8 us -> none  [the longest x1 39 us: shards(): lax.all_gather(group_values, 'cp', axis=0, tiled=True)]
    dot_general x32 -> x0, matrix products: 67.7 us -> none  [the longest x16 46.6 us: tile_step(): jnp.einsum('hrk,kd->rhd', weights.astype(jnp.bfloat16), value_tile, prefe...]
    ppermute x0 -> x11, starting transfers between devices: none -> 13.3 us  [flip(): return lax.ppermute(array, axis, [(i, i ^ mask) for i in range(size)])]
    all_gather x2 -> x0, blocking collectives: 12.2 us -> none  [the longest x1 7.3 us: shards(): lax.all_gather(keys, 'sp', axis=0, tiled=True)]
    reduce_sum x50 -> x0, other arithmetic: 11.3 us -> none  [the longest x16 8.21 us: tile_step(): new_total = run_total * rescale + jnp.sum(weights, axis=2)]
    another operation x1 -> x0, loops' own time: 9.85 us -> none  [fold_piece(): lax.scan(tile_step, carried, (key_tiles, value_tiles, tile_ids))]
    dynamic_slice x16 -> x0, local copies, waits for them, and re-layouts: 8.85 us -> none  [fold_piece(): lax.scan(tile_step, carried, (key_tiles, value_tiles, tile_ids))]
    ppermute x0 -> x11, waiting for transfers between devices: none -> 8.39 us  [flip(): return lax.ppermute(array, axis, [(i, i ^ mask) for i in range(size)])]
  transfers between devices with their start and end apart: 2 -> 11, of which waited for: 2 -> 6; matrix products, arithmetic and copies ran while one was open for 1% -> 2% of each run, Pallas kernels for 0% -> 10%
where the time goes in v3:
time: 32.5 us; the launch traced here: 32.1 us
  starting transfers between devices  13.3 us (41%)
  waiting for transfers between devices  8.39 us (26%)
  Pallas kernels  7.7 us (24%)
  other arithmetic  1.56 us (5%)
  local copies, waits for them, and re-layouts  1.04 us (3%)
    ppermute x11, starting transfers between devices, flip(): return lax.ppermute(array, axis, [(i, i ^ mask) for i in range(size)])  13.3 us
    ppermute x11, waiting for transfers between devices, flip(): return lax.ppermute(array, axis, [(i, i ^ mask) for i in range(size)])  8.39 us
    pallas_call x1, Pallas kernels, attend_second(): pl.pallas_call(functools.partial(second_kernel, cp_size), out_shape=jax.S...  3.67 us
    pallas_call x1, Pallas kernels, attend_first(): pl.pallas_call(functools.partial(first_kernel, cp_size), out_shape=[jax.S...  3.12 us
    unnamed x2, local copies, waits for them, and re-layouts  1.04 us
    pallas_call x1, Pallas kernels, select(): pl.pallas_call(functools.partial(select_kernel, places), out_shape=jax.Sh...  0.91 us
    another operation x3, other arithmetic, shards(): line = jnp.stack([far[j] for j in group])  0.81 us
    concatenate x1, other arithmetic, shards(): meta = jnp.concatenate([jnp.stack([cp_index, half]), span_order, doc_ids])  0.75 us
  transfers between devices with their start and end apart: 11, of which 6 were waited for; matrix products, arithmetic and copies ran while one was open for 2% of the time, Pallas kernels for 10%

profile of v3, /device:TPU:0, one launch (start us, length us, event | category | flops | bytes accessed | tf_op | source)
XLA Modules:
  0.0 32.1 jit_solution(6559582179945863570)
XLA Ops:
  0.0 0.8 %fusion = (bf16[1,128,256]{2,1,0:T(8,128)(2,1)S(1)}, bf16[128,256]{1,0:T(8,128)(2,1)S(1)}) fusion(bf16[128,128]{1,0:T(8,128)(2,1)} %param.7, bf16[128,128]{1,0:T(8,128)(2,1)} %param.6), kind=kLoop, calls=%fused_computation.4 | loop fusion | flops 131072 | bytes 196608 | tf_op jit(solution)/shard_map/stack | solution.py:242
  0.8 5.1 %collective-permute-start.3 = (bf16[128,256]{1,0:T(8,128)(2,1)S(1)}, bf16[128,256]{1,0:T(8,128)(2,1)S(1)}, u32[]{:S(2)}, u32[]{:S(2)}) collective-permute-start(bf16[128,256]{1,0:T(8,128)(2,1)S(1)} %get-tuple-element.22.own_ref), channel_id=1, source_target_pairs={{0,24},{2,26},{4,28},{6,30},{8,16},{10,18},{12,20},{14,22},{16,8},... | collective-permute-start | bytes 196616 | tf_op jit(solution)/shard_map/ppermute | solution.py:20
  5.9 0.0 collective-permute-start.1
  5.9 0.6 %collective-permute-start = (bf16[128,256]{1,0:T(8,128)(2,1)S(1)}, bf16[128,256]{1,0:T(8,128)(2,1)S(1)}, u32[]{:S(2)}, u32[]{:S(2)}) collective-permute-start(bf16[128,256]{1,0:T(8,128)(2,1)S(1)} %get-tuple-element.22.own_ref), channel_id=1, source_target_pairs={{0,8},{2,10},{4,12},{6,14},{8,0},{10,2},{12,4},{14,6},{16,24},{18,... | collective-permute-start | bytes 196616 | tf_op jit(solution)/shard_map/ppermute | solution.py:20
  6.5 1.9 %collective-permute-done.3 = bf16[128,256]{1,0:T(8,128)(2,1)S(1)} collective-permute-done((bf16[128,256]{1,0:T(8,128)(2,1)S(1)}, bf16[128,256]{1,0:T(8,128)(2,1)S(1)}, u32[]{:S(2)}, u32[]{:S(2)}) %collective-permute-start.3) | collective-permute-done | bytes 65568 | tf_op jit(solution)/shard_map/ppermute | solution.py:20
  8.5 1.9 %collective-permute-start.4 = (bf16[2,128,256]{2,1,0:T(8,128)(2,1)S(1)}, bf16[2,128,256]{2,1,0:T(8,128)(2,1)S(1)}, u32[]{:S(2)}, u32[]{:S(2)}) collective-permute-start(bf16[2,128,256]{2,1,0:T(8,128)(2,1)S(1)} %pad_maximum_fusion.1.refs_0_), channel_id=1, source_target_pairs={{0,4},{2,6},{4,0},{6,2},{8,12},{10,14},{12,8},{14,10},{16,20},{18,... | collective-permute-start | bytes 393224 | tf_op jit(solution)/shard_map/ppermute | solution.py:20
  10.4 1.1 %collective-permute-done.1 = bf16[128,256]{1,0:T(8,128)(2,1)S(1)} collective-permute-done((bf16[128,256]{1,0:T(8,128)(2,1)S(1)}, bf16[128,256]{1,0:T(8,128)(2,1)S(1)}, u32[]{:S(2)}, u32[]{:S(2)}) %collective-permute-start.1) | collective-permute-done | bytes 65568 | tf_op jit(solution)/shard_map/ppermute | solution.py:20
  11.5 0.0 collective-permute-done
  11.5 1.6 %collective-permute-start.2 = (bf16[2,128,256]{2,1,0:T(8,128)(2,1)S(1)}, bf16[2,128,256]{2,1,0:T(8,128)(2,1)S(1)}, u32[]{:S(2)}, u32[]{:S(2)}) collective-permute-start(bf16[2,128,256]{2,1,0:T(8,128)(2,1)S(1)} %pad_maximum_fusion.refs_4_), channel_id=1, source_target_pairs={{0,4},{2,6},{4,0},{6,2},{8,12},{10,14},{12,8},{14,10},{16,20},{18,... | collective-permute-start | bytes 393224 | tf_op jit(solution)/shard_map/ppermute | solution.py:20
  13.1 1.5 %collective-permute-start.5 = (bf16[128,256]{1,0:T(8,128)(2,1)S(1)}, bf16[128,256]{1,0:T(8,128)(2,1)S(1)}, u32[]{:S(2)}, u32[]{:S(2)}) collective-permute-start(bf16[128,256]{1,0:T(8,128)(2,1)S(1)} %get-tuple-element.22.own_ref), channel_id=1, source_target_pairs={{0,1},{1,0},{2,3},{3,2},{4,5},{5,4},{6,7},{7,6},{8,9},{9,8},{10,11... | collective-permute-start | bytes 196616 | tf_op jit(solution)/shard_map/ppermute | solution.py:20
  14.6 0.7 %pad_add_fusion.1.meta_ref = s32[50]{0:T(128)S(1)} fusion(s32[32]{0:T(128)} %param.8, s32[16]{0:T(128)} %param.9, s32[1]{0:T(128)} %bitcast.5, s32[1]{0:T(128)} %bitcast.4), kind=kLoop, calls=%fused_computation.3 | loop fusion | flops 150 | bytes 400 | tf_op jit(solution)/shard_map/concatenate | solution.py:230
  15.4 0.0 collective-permute-start.8
  15.4 0.5 %collective-permute-start.6 = (bf16[2,128,256]{2,1,0:T(8,128)(2,1)S(1)}, bf16[2,128,256]{2,1,0:T(8,128)(2,1)S(1)}, u32[]{:S(2)}, u32[]{:S(2)}) collective-permute-start(bf16[2,128,256]{2,1,0:T(8,128)(2,1)S(1)} %pad_maximum_fusion.1.refs_0_), channel_id=1, source_target_pairs={{0,2},{2,0},{4,6},{6,4},{8,10},{10,8},{12,14},{14,12},{16,18},{18,... | collective-permute-start | bytes 393224 | tf_op jit(solution)/shard_map/ppermute | solution.py:20
  15.9 1.5 %collective-permute-done.5.other_ref = bf16[128,256]{1,0:T(8,128)(2,1)S(1)} collective-permute-done((bf16[128,256]{1,0:T(8,128)(2,1)S(1)}, bf16[128,256]{1,0:T(8,128)(2,1)S(1)}, u32[]{:S(2)}, u32[]{:S(2)}) %collective-permute-start.5) | collective-permute-done | bytes 65568 | tf_op jit(solution)/shard_map/ppermute | solution.py:20
  17.4 0.0 collective-permute-done.4.refs_1_
  17.4 0.0 collective-permute-done.2.refs_5_
  17.4 0.0 collective-permute-start.9
  17.4 0.5 %collective-permute-start.7 = (bf16[2,128,256]{2,1,0:T(8,128)(2,1)S(1)}, bf16[2,128,256]{2,1,0:T(8,128)(2,1)S(1)}, u32[]{:S(2)}, u32[]{:S(2)}) collective-permute-start(bf16[2,128,256]{2,1,0:T(8,128)(2,1)S(1)} %collective-permute-done.4.refs_1_), channel_id=1, source_target_pairs={{0,2},{2,0},{4,6},{6,4},{8,10},{10,8},{12,14},{14,12},{16,18},{18,... | collective-permute-start | bytes 393224 | tf_op jit(solution)/shard_map/ppermute | solution.py:20
  17.9 0.0 collective-permute-done.8.refs_6_
  17.9 0.0 collective-permute-done.6.refs_2_
  17.9 0.8 %collective-permute-done.9.refs_7_ = bf16[2,128,256]{2,1,0:T(8,128)(2,1)S(1)} collective-permute-done((bf16[2,128,256]{2,1,0:T(8,128)(2,1)S(1)}, bf16[2,128,256]{2,1,0:T(8,128)(2,1)S(1)}, u32[]{:S(2)}, u32[]{:S(2)}) %collective-permute-start.9) | collective-permute-done | bytes 131104 | tf_op jit(solution)/shard_map/ppermute | solution.py:20
  18.7 0.2 collective-permute-done.7.refs_3_
  18.9 0.9 %select.3.prev_ref = bf16[512,256]{1,0:T(8,128)(2,1)S(1)} custom-call(s32[50]{0:T(128)S(1)} %pad_add_fusion.1.meta_ref, bf16[2,128,256]{2,1,0:T(8,128)(2,1)S(1)} %pad_maximum_fusion.1.refs_0_, bf16[2,128,256]{2,1,0:T(8,128)(2,1)S(1)} %collective-permute-done.4.refs_1_, bf16[2,128,256]{2,1,0:T(8,128)(2,1)S(1)} %collective-permute-done.6.refs_2_, ...), custom_call_target="tpu_custom_call" | custom-call | tf_op jit(solution)/shard_map/select/pallas_call | solution.py:185
  19.8 1.6 %collective-permute-start.10 = (bf16[512,256]{1,0:T(8,128)(2,1)S(1)}, bf16[512,256]{1,0:T(8,128)(2,1)S(1)}, u32[]{:S(2)}, u32[]{:S(2)}) collective-permute-start(bf16[512,256]{1,0:T(8,128)(2,1)S(1)} %select.3.prev_ref), channel_id=1, source_target_pairs={{0,1},{1,0},{2,3},{3,2},{4,5},{5,4},{6,7},{7,6},{8,9},{9,8},{10,11... | collective-permute-start | bytes 786440 | tf_op jit(solution)/shard_map/ppermute | solution.py:20
  21.4 0.0 copy-start
  21.4 1.0 %copy-done = bf16[256,1024]{1,0:T(8,128)(2,1)S(1)} copy-done((bf16[256,1024]{1,0:T(8,128)(2,1)S(1)}, bf16[256,1024]{1,0:T(8,128)(2,1)}, u32[]{:S(2)}) %copy-start) | copy-done | bytes 524312
  22.4 3.1 %attend_first.1 = (f32[2,8,128,128]{3,2,1,0:T(8,128)S(1)}, f32[2,8,128,256]{3,2,1,0:T(8,128)S(1)}) custom-call(s32[50]{0:T(128)S(1)} %pad_add_fusion.1.meta_ref, bf16[256,1024]{1,0:T(8,128)(2,1)S(1)} %copy-done, bf16[128,256]{1,0:T(8,128)(2,1)S(1)} %get-tuple-element.22.own_ref, bf16[128,256]{1,0:T(8,128)(2,1)S(1)} %collective-permute-done.5.other_ref, ...), custom_call_target="tpu_custom_call" | custom-call | flops 1073741824 | bytes 4194304 | tf_op jit(solution)/shard_map/attend_first/pallas_call | solution.py:199
  25.6 2.8 %collective-permute-done.10.prev_ref = bf16[512,256]{1,0:T(8,128)(2,1)S(1)} collective-permute-done((bf16[512,256]{1,0:T(8,128)(2,1)S(1)}, bf16[512,256]{1,0:T(8,128)(2,1)S(1)}, u32[]{:S(2)}, u32[]{:S(2)}) %collective-permute-start.10) | collective-permute-done | bytes 262176 | tf_op jit(solution)/shard_map/ppermute | solution.py:20
  28.4 3.7 %attend_second.1 = bf16[256,1024]{1,0:T(8,128)(2,1)} custom-call(s32[50]{0:T(128)S(1)} %pad_add_fusion.1.meta_ref, bf16[256,1024]{1,0:T(8,128)(2,1)S(1)} %copy-done, bf16[512,256]{1,0:T(8,128)(2,1)S(1)} %collective-permute-done.10.prev_ref, f32[2,8,128,128]{3,2,1,0:T(8,128)S(1)} %get-tuple-element.19.old_max, f32[2,8,128,256]{3,2,1,0:T(8,128)S(1)} %get-tuple-element.20.old_acc), custom_call_target="tpu_custom_call" | custom-call | flops 1073741824 | bytes 4194304 | tf_op jit(solution)/shard_map/attend_second/pallas_call | solution.py:213
  (2 shorter events, 0.0 us)
Async XLA Ops:
  0.8 7.7 %collective-permute-start.3 = (bf16[128,256]{1,0:T(8,128)(2,1)S(1)}, bf16[128,256]{1,0:T(8,128)(2,1)S(1)}, u32[]{:S(2)}, u32[]{:S(2)}) collective-permute-start(bf16[128,256]{1,0:T(8,128)(2,1)S(1)} %get-tuple-element.22.own_ref), channel_id=1, source_target_pairs={{0,24},{2,26},{4,28},{6,30},{8,16},{10,18},{12,20},{14,22},{16,8},... | collective-permute-start | bytes 196616 | tf_op jit(solution)/shard_map/ppermute | solution.py:20
  5.9 5.6 %collective-permute-start.1 = (bf16[128,256]{1,0:T(8,128)(2,1)S(1)}, bf16[128,256]{1,0:T(8,128)(2,1)S(1)}, u32[]{:S(2)}, u32[]{:S(2)}) collective-permute-start(bf16[128,256]{1,0:T(8,128)(2,1)S(1)} %get-tuple-element.22.own_ref), channel_id=1, source_target_pairs={{0,16},{2,18},{4,20},{6,22},{8,24},{10,26},{12,28},{14,30},{16,0},... | collective-permute-start | bytes 196616 | tf_op jit(solution)/shard_map/ppermute | solution.py:20
  5.9 5.6 %collective-permute-start = (bf16[128,256]{1,0:T(8,128)(2,1)S(1)}, bf16[128,256]{1,0:T(8,128)(2,1)S(1)}, u32[]{:S(2)}, u32[]{:S(2)}) collective-permute-start(bf16[128,256]{1,0:T(8,128)(2,1)S(1)} %get-tuple-element.22.own_ref), channel_id=1, source_target_pairs={{0,8},{2,10},{4,12},{6,14},{8,0},{10,2},{12,4},{14,6},{16,24},{18,... | collective-permute-start | bytes 196616 | tf_op jit(solution)/shard_map/ppermute | solution.py:20
  8.5 8.9 %collective-permute-start.4 = (bf16[2,128,256]{2,1,0:T(8,128)(2,1)S(1)}, bf16[2,128,256]{2,1,0:T(8,128)(2,1)S(1)}, u32[]{:S(2)}, u32[]{:S(2)}) collective-permute-start(bf16[2,128,256]{2,1,0:T(8,128)(2,1)S(1)} %pad_maximum_fusion.1.refs_0_), channel_id=1, source_target_pairs={{0,4},{2,6},{4,0},{6,2},{8,12},{10,14},{12,8},{14,10},{16,20},{18,... | collective-permute-start | bytes 393224 | tf_op jit(solution)/shard_map/ppermute | solution.py:20
  11.5 5.8 %collective-permute-start.2 = (bf16[2,128,256]{2,1,0:T(8,128)(2,1)S(1)}, bf16[2,128,256]{2,1,0:T(8,128)(2,1)S(1)}, u32[]{:S(2)}, u32[]{:S(2)}) collective-permute-start(bf16[2,128,256]{2,1,0:T(8,128)(2,1)S(1)} %pad_maximum_fusion.refs_4_), channel_id=1, source_target_pairs={{0,4},{2,6},{4,0},{6,2},{8,12},{10,14},{12,8},{14,10},{16,20},{18,... | collective-permute-start | bytes 393224 | tf_op jit(solution)/shard_map/ppermute | solution.py:20
  13.1 4.3 %collective-permute-start.5 = (bf16[128,256]{1,0:T(8,128)(2,1)S(1)}, bf16[128,256]{1,0:T(8,128)(2,1)S(1)}, u32[]{:S(2)}, u32[]{:S(2)}) collective-permute-start(bf16[128,256]{1,0:T(8,128)(2,1)S(1)} %get-tuple-element.22.own_ref), channel_id=1, source_target_pairs={{0,1},{1,0},{2,3},{3,2},{4,5},{5,4},{6,7},{7,6},{8,9},{9,8},{10,11... | collective-permute-start | bytes 196616 | tf_op jit(solution)/shard_map/ppermute | solution.py:20
  15.4 2.5 %collective-permute-start.8 = (bf16[2,128,256]{2,1,0:T(8,128)(2,1)S(1)}, bf16[2,128,256]{2,1,0:T(8,128)(2,1)S(1)}, u32[]{:S(2)}, u32[]{:S(2)}) collective-permute-start(bf16[2,128,256]{2,1,0:T(8,128)(2,1)S(1)} %pad_maximum_fusion.refs_4_), channel_id=1, source_target_pairs={{0,2},{2,0},{4,6},{6,4},{8,10},{10,8},{12,14},{14,12},{16,18},{18,... | collective-permute-start | bytes 393224 | tf_op jit(solution)/shard_map/ppermute | solution.py:20
  15.4 2.5 %collective-permute-start.6 = (bf16[2,128,256]{2,1,0:T(8,128)(2,1)S(1)}, bf16[2,128,256]{2,1,0:T(8,128)(2,1)S(1)}, u32[]{:S(2)}, u32[]{:S(2)}) collective-permute-start(bf16[2,128,256]{2,1,0:T(8,128)(2,1)S(1)} %pad_maximum_fusion.1.refs_0_), channel_id=1, source_target_pairs={{0,2},{2,0},{4,6},{6,4},{8,10},{10,8},{12,14},{14,12},{16,18},{18,... | collective-permute-start | bytes 393224 | tf_op jit(solution)/shard_map/ppermute | solution.py:20
  17.4 1.4 %collective-permute-start.9 = (bf16[2,128,256]{2,1,0:T(8,128)(2,1)S(1)}, bf16[2,128,256]{2,1,0:T(8,128)(2,1)S(1)}, u32[]{:S(2)}, u32[]{:S(2)}) collective-permute-start(bf16[2,128,256]{2,1,0:T(8,128)(2,1)S(1)} %collective-permute-done.2.refs_5_), channel_id=1, source_target_pairs={{0,2},{2,0},{4,6},{6,4},{8,10},{10,8},{12,14},{14,12},{16,18},{18,... | collective-permute-start | bytes 393224 | tf_op jit(solution)/shard_map/ppermute | solution.py:20
  17.4 1.5 %collective-permute-start.7 = (bf16[2,128,256]{2,1,0:T(8,128)(2,1)S(1)}, bf16[2,128,256]{2,1,0:T(8,128)(2,1)S(1)}, u32[]{:S(2)}, u32[]{:S(2)}) collective-permute-start(bf16[2,128,256]{2,1,0:T(8,128)(2,1)S(1)} %collective-permute-done.4.refs_1_), channel_id=1, source_target_pairs={{0,2},{2,0},{4,6},{6,4},{8,10},{10,8},{12,14},{14,12},{16,18},{18,... | collective-permute-start | bytes 393224 | tf_op jit(solution)/shard_map/ppermute | solution.py:20
  19.8 8.6 %collective-permute-start.10 = (bf16[512,256]{1,0:T(8,128)(2,1)S(1)}, bf16[512,256]{1,0:T(8,128)(2,1)S(1)}, u32[]{:S(2)}, u32[]{:S(2)}) collective-permute-start(bf16[512,256]{1,0:T(8,128)(2,1)S(1)} %select.3.prev_ref), channel_id=1, source_target_pairs={{0,1},{1,0},{2,3},{3,2},{4,5},{5,4},{6,7},{7,6},{8,9},{9,8},{10,11... | collective-permute-start | bytes 786440 | tf_op jit(solution)/shard_map/ppermute | solution.py:20
  21.4 1.0 %copy-start = (bf16[256,1024]{1,0:T(8,128)(2,1)S(1)}, bf16[256,1024]{1,0:T(8,128)(2,1)}, u32[]{:S(2)}) copy-start(bf16[256,1024]{1,0:T(8,128)(2,1)} %q_ref.3) | copy-start | bytes 1572868

commit v4 on v0

v4 whole, which is shorter than its diff:
```python
import functools
import math

import jax
import jax.numpy as jnp
from jax import lax
from jax.experimental import pallas as pl
from jax.experimental.pallas import tpu as pltpu
from jax.sharding import PartitionSpec as P

HD = 128
SPAN = 256
BLK = 128
NEGATIVE = -1e30
HEAD = 2
SCALE2 = math.log2(math.e) / math.sqrt(HD)
LINES = ((3, 0), (1, 2))


def flip(array, axis, size, mask):
    return lax.ppermute(array, axis, [(i, i ^ mask) for i in range(size)])


def locate(apart):
    line = apart >> 2
    group = (line ^ (line >> 1)) & 1
    return group * 4 + (apart & 1) * 2 + ((apart >> 1) & 1), 1 - (line & 1)


def select_kernel(cp_size, meta_ref, *refs):
    sources, (keys_ref, values_ref) = refs[:-2], refs[-2:]
    cp = meta_ref[0]
    own_span = meta_ref[HEAD + cp]
    for back in range(1, keys_ref.shape[0] // BLK + 1):
        span = jnp.maximum(own_span - back, 0)
        holder = jnp.int32(0)
        for index in range(cp_size):
            holder = jnp.where(meta_ref[HEAD + index] == span, jnp.int32(index), holder)
        source, slot = locate(holder ^ cp)
        for index, ref in enumerate(sources):

            @pl.when(source == index)
            def _():
                rows = slice((back - 1) * BLK, back * BLK)
                keys_ref[rows, :] = ref[slot, :, 0:HD]
                values_ref[rows, :] = ref[slot, :, HD:]


def extent(meta_ref, cp_size, half, reach):
    span = meta_ref[HEAD + meta_ref[0]]
    doc_at = HEAD + cp_size
    doc = meta_ref[doc_at + 2 * span]
    count = jnp.int32(0)
    for back in range(1, reach + 1):
        block = 2 * (span - back) + half
        held = (block >= 0) & (meta_ref[doc_at + jnp.maximum(block, 0)] == doc)
        count = count + jnp.where(held, 1, 0)
    return count, doc == meta_ref[doc_at + 2 * span + 1]


def stack_kernel(q_ref, out_ref, sems):
    heads = out_ref.shape[1] // BLK
    copies = [
        pltpu.make_async_copy(
            q_ref.at[pl.ds(a * BLK, BLK), pl.ds(h * HD, HD)], out_ref.at[a, pl.ds(h * BLK, BLK), :], sems.at[a, h]
        )
        for a in range(2)
        for h in range(heads)
    ]
    for copy in copies:
        copy.start()
    for copy in copies:
        copy.wait()


def score(queries, keys):
    return lax.dot_general(queries, keys, (((1,), (1,)), ((), ())), preferred_element_type=jnp.float32)


def row_top(blocks):
    best = blocks[0]
    for block in blocks[1:]:
        best = jnp.maximum(best, block)
    return jnp.max(best, axis=1, keepdims=True)


def row_sum(blocks):
    added = blocks[0]
    for block in blocks[1:]:
        added = added + block
    return jnp.sum(added, axis=1, keepdims=True)


def split(scores):
    return [scores[:, c : c + BLK] for c in range(0, scores.shape[1], BLK)]


def with_ones(values):
    return jnp.concatenate([values, jnp.ones_like(values)], axis=1)


def cases(count, most, body):
    for n in range(most + 1):
        pl.when(count == n)(functools.partial(body, n))


def first_kernel(cp_size, chunk, meta_ref, q_ref, own_ref, other_ref, keys_ref, values_ref, max_ref, acc_ref):
    half = meta_ref[1]
    reach = keys_ref.shape[0] // BLK
    count, same = extent(meta_ref, cp_size, half, reach)
    swap = half == 1
    mine, other = own_ref[...], other_ref[...]
    low, high = jnp.where(swap, other, mine), jnp.where(swap, mine, other)
    rows = lax.broadcasted_iota(jnp.int32, (BLK, BLK), 0)
    cols = lax.broadcasted_iota(jnp.int32, (BLK, BLK), 1)
    causal = jnp.where(cols <= rows, 0.0, NEGATIVE)
    causal = jnp.concatenate([causal] * chunk, axis=0)

    def attend(a, own, n):
        own_values = with_ones(own[:, HD:])
        for group in range(q_ref.shape[1] // (BLK * chunk)):
            at = slice(group * chunk * BLK, (group + 1) * chunk * BLK)
            queries = q_ref[a, at]
            blocks = split(score(queries, own[:, 0:HD]))
            blocks[-1] = blocks[-1] + causal
            if n:
                blocks = blocks + split(score(queries, keys_ref[0 : n * BLK, :]))
            top = row_top(blocks)
            weights = [jnp.exp2((block - top) * SCALE2).astype(jnp.bfloat16) for block in blocks]
            mid = own.shape[0] // BLK
            total = jnp.dot(
                jnp.concatenate(weights[:mid], axis=1), own_values, preferred_element_type=jnp.float32
            )
            if n:
                total = total + jnp.dot(
                    jnp.concatenate(weights[mid:], axis=1),
                    with_ones(values_ref[0 : n * BLK, :]),
                    preferred_element_type=jnp.float32,
                )
            max_ref[a, at] = jnp.broadcast_to(top, (chunk * BLK, HD))
            acc_ref[a, at] = total

    cases(count, reach, functools.partial(attend, 0, low))

    @pl.when(same)
    def _():
        cases(count, reach, functools.partial(attend, 1, jnp.concatenate([low, high], axis=0)))

    @pl.when(jnp.logical_not(same))
    def _():
        attend(1, high, 0)


def weigh_kernel(cp_size, chunk, meta_ref, q_ref, keys_ref, max_ref, acc_ref, weights_ref, rest_ref):
    reach = keys_ref.shape[0] // BLK
    count, same = extent(meta_ref, cp_size, 1 - meta_ref[1], reach)

    def weigh(a, n):
        for group in range(q_ref.shape[1] // (BLK * chunk)):
            at = slice(group * chunk * BLK, (group + 1) * chunk * BLK)
            old, total = acc_ref[a, at, 0:HD], acc_ref[a, at, HD:]
            if n:
                blocks = split(score(q_ref[a, at], keys_ref[0 : n * BLK, :]))
                old_top = max_ref[a, at]
                top = jnp.maximum(row_top(blocks), old_top)
                fade = jnp.exp2((old_top - top) * SCALE2)
                blocks = [jnp.exp2((block - top) * SCALE2) for block in blocks]
                share = 1.0 / (total * fade + row_sum(blocks))
                for index, block in enumerate(blocks):
                    weights_ref[a, at, index * BLK : (index + 1) * BLK] = (block * share).astype(jnp.bfloat16)
                rest_ref[a, at] = old * (fade * share)
            else:
                rest_ref[a, at] = old / total
            empty = reach - n
            if empty:
                weights_ref[a, at, n * BLK :] = jnp.zeros((chunk * BLK, empty * BLK), jnp.bfloat16)

    for a in range(2):
        cases(count if a == 0 else jnp.where(same, count, 0), reach, functools.partial(weigh, a))


def finish_kernel(chunk, weights_ref, rest_ref, values_ref, out_ref, done, sems):
    groups = rest_ref.shape[1] // (BLK * chunk)
    copies = []
    for a in range(2):
        for group in range(groups):
            at = slice(group * chunk * BLK, (group + 1) * chunk * BLK)
            result = rest_ref[a, at] + jnp.dot(
                weights_ref[a, at], values_ref[...], preferred_element_type=jnp.float32
            )
            result = result.astype(done.dtype)
            for h in range(chunk):
                done[a, group, :, h * HD : (h + 1) * HD] = result[h * BLK : (h + 1) * BLK]
            place = out_ref.at[pl.ds(a * BLK, BLK), pl.ds(group * chunk * HD, chunk * HD)]
            copies.append(pltpu.make_async_copy(done.at[a, group], place, sems.at[a, group]))
            copies[-1].start()
    for copy in copies:
        copy.wait()


VMEM = pl.BlockSpec(memory_space=pltpu.VMEM)
SMEM = pl.BlockSpec(memory_space=pltpu.SMEM)
ANY = pl.BlockSpec(memory_space=pl.ANY)


def local_call(kernel, name, outs, in_specs, grant, flops, **extra):
    return pl.pallas_call(
        kernel,
        out_shape=outs,
        in_specs=in_specs,
        compiler_params=pltpu.CompilerParams(vmem_limit_bytes=grant * 1024 * 1024),
        cost_estimate=pl.CostEstimate(flops=flops, bytes_accessed=1 << 20, transcendentals=0),
        name=name,
        **{"out_specs": [VMEM] * len(outs), **extra},
    )


def stack_queries(queries):
    heads = queries.shape[1] // HD
    outs = [jax.ShapeDtypeStruct((2, heads * BLK, HD), queries.dtype)]
    scratch = [pltpu.SemaphoreType.DMA((2, heads))]
    return local_call(stack_kernel, "stack_queries", outs, [ANY], 4, 1 << 20, scratch_shapes=scratch)(queries)[0]


def attend(cp_size, meta, queries, own, other, keys, values, other_keys, other_values):
    reach, rows = keys.shape[0] // BLK, queries.shape[1]
    chunk = min(rows // BLK, 4)
    groups = rows // (BLK * chunk)
    state = lambda width, dtype=jnp.float32: jax.ShapeDtypeStruct((2, rows, width), dtype)
    kernel = functools.partial(first_kernel, cp_size, chunk)
    outs, ins = [state(HD), state(2 * HD)], [SMEM] + [VMEM] * 5
    top, acc = local_call(kernel, "attend_first", outs, ins, 12, 1 << 31)(meta, queries, own, other, keys, values)
    kernel = functools.partial(weigh_kernel, cp_size, chunk)
    outs, ins = [state(reach * BLK, jnp.bfloat16), state(HD)], [SMEM] + [VMEM] * 4
    weights, rest = local_call(kernel, "attend_weigh", outs, ins, 12, 1 << 30)(meta, queries, other_keys, top, acc)
    outs = [jax.ShapeDtypeStruct((2 * BLK, rows // BLK * HD), queries.dtype)]
    scratch = [
        pltpu.VMEM((2, groups, BLK, chunk * HD), queries.dtype),
        pltpu.SemaphoreType.DMA((2, groups)),
    ]
    kernel = functools.partial(finish_kernel, chunk)
    finish = local_call(
        kernel, "attend_finish", outs, [VMEM] * 3, 8, 1 << 29, out_specs=[ANY], scratch_shapes=scratch
    )
    return finish(weights, rest, other_values)[0]


def shards(cp_size, sp_size, queries, keys, values, doc_ids, span_order):
    reach = doc_ids.shape[0] // 8
    staged = cp_size == 16 and sp_size == 2
    cp_index = lax.axis_index("cp").astype(jnp.int32)
    half = lax.axis_index("sp").astype(jnp.int32) if staged else jnp.int32(0)
    meta = jnp.concatenate([jnp.stack([cp_index, half]), span_order, doc_ids])
    own = lax.pad(keys, jnp.bfloat16(0), ((0, 0, 0), (0, HD, 0)))
    own = own + lax.pad(values, jnp.bfloat16(0), ((0, 0, 0), (HD, 0, 0)))
    queries = stack_queries(queries)
    if staged:
        by_x = lambda array: flip(array, "cp", cp_size, 2)
        by_y = lambda array: flip(array, "sp", sp_size, 1)
        by_core = lambda array: flip(array, "cp", cp_size, 1)
        far = {j: flip(own, "cp", cp_size, 4 * j) for j in (3, 2, 1)}
        far[0] = own
        other = by_y(own)
        sources = []
        for group in LINES:
            line = jnp.stack([far[j] for j in group])
            side, meta, other, queries = lax.optimization_barrier((by_x(line), meta, other, queries))
            sources += [line, side, by_core(line), by_core(side)]
        part = jax.ShapeDtypeStruct((reach * BLK, HD), jnp.bfloat16)
        picked = local_call(
            functools.partial(select_kernel, cp_size), "select", [part] * 2, [SMEM] + [VMEM] * len(sources), 4, 1 << 20
        )(meta, *sources)
        others = [by_y(array) for array in picked]
    else:
        pair = lax.all_gather(own, ("cp", "sp"), axis=0, tiled=True).reshape(cp_size, 2, BLK, 2, HD)
        holder = jnp.argsort(span_order)
        back = jnp.maximum(span_order[cp_index] - jnp.arange(reach + 1, dtype=jnp.int32), 0)
        chosen = pair[holder[back]]
        own, other = (chosen[0, k].reshape(BLK, 2 * HD) for k in (0, 1))
        picked, others = ([chosen[1:, k, :, part].reshape(reach * BLK, HD) for part in (0, 1)] for k in (0, 1))
    return attend(cp_size, meta, queries, own, other, *picked, *others)


def solution(mesh):
    in_specs = (P("cp", "sp"), P(("cp", "sp"), None), P(("cp", "sp"), None), P(), P())
    out_specs = P("cp", "sp")
    body = functools.partial(shards, mesh.shape["cp"], mesh.shape["sp"])
    return jax.shard_map(body, mesh=mesh, in_specs=in_specs, out_specs=out_specs, check_vma=False)
```

time: 203 us -> 30.1 us (0.15)
  matrix products: 67.7 us -> 0 us
  waiting for transfers between devices: 70.8 us -> 7.13 us
  other arithmetic: 15.7 us -> 1.57 us
  starting transfers between devices: 0.04 us -> 13.9 us
  between operations: 13.5 us -> 0.22 us
  blocking collectives: 12.2 us -> 0 us
  local copies, waits for them, and re-layouts: 11.4 us -> 1.04 us
  loops' own time: 9.85 us -> 0 us
  Pallas kernels: 0 us -> 6.1 us
    all_gather x2 -> x0, waiting for transfers between devices: 70.8 us -> none  [the longest x1 39 us: shards(): lax.all_gather(group_values, 'cp', axis=0, tiled=True)]
    dot_general x32 -> x0, matrix products: 67.7 us -> none  [the longest x16 46.6 us: tile_step(): jnp.einsum('hrk,kd->rhd', weights.astype(jnp.bfloat16), value_tile, prefe...]
    ppermute x0 -> x12, starting transfers between devices: none -> 13.9 us  [flip(): return lax.ppermute(array, axis, [(i, i ^ mask) for i in range(size)])]
    all_gather x2 -> x0, blocking collectives: 12.2 us -> none  [the longest x1 7.3 us: shards(): lax.all_gather(keys, 'sp', axis=0, tiled=True)]
    reduce_sum x50 -> x0, other arithmetic: 11.3 us -> none  [the longest x16 8.21 us: tile_step(): new_total = run_total * rescale + jnp.sum(weights, axis=2)]
    another operation x1 -> x0, loops' own time: 9.85 us -> none  [fold_piece(): lax.scan(tile_step, carried, (key_tiles, value_tiles, tile_ids))]
    dynamic_slice x16 -> x0, local copies, waits for them, and re-layouts: 8.85 us -> none  [fold_piece(): lax.scan(tile_step, carried, (key_tiles, value_tiles, tile_ids))]
    ppermute x0 -> x12, waiting for transfers between devices: none -> 7.13 us  [flip(): return lax.ppermute(array, axis, [(i, i ^ mask) for i in range(size)])]
  transfers between devices with their start and end apart: 2 -> 12, of which waited for: 2 -> 9; matrix products, arithmetic and copies ran while one was open for 1% -> 3% of each run, Pallas kernels for 0% -> 13%
where the time goes in v4:
time: 30.1 us; the launch traced here: 29.9 us
  starting transfers between devices  13.9 us (46%)
  waiting for transfers between devices  7.13 us (24%)
  Pallas kernels  6.1 us (20%)
  other arithmetic  1.57 us (5%)
  local copies, waits for them, and re-layouts  1.04 us (3%)
    ppermute x12, starting transfers between devices, flip(): return lax.ppermute(array, axis, [(i, i ^ mask) for i in range(size)])  13.9 us
    ppermute x12, waiting for transfers between devices, flip(): return lax.ppermute(array, axis, [(i, i ^ mask) for i in range(size)])  7.13 us
    pallas_call x1, Pallas kernels, attend(): local_call(kernel, 'attend_first', outs, ins, 12, 1 << 31)  2.07 us
    pallas_call x1, Pallas kernels, attend(): local_call(kernel, 'attend_weigh', outs, ins, 12, 1 << 30)  1.47 us
    pallas_call x1, Pallas kernels, attend(): return finish(weights, rest, other_values)[0]  1.42 us
    unnamed x2, local copies, waits for them, and re-layouts  1.04 us
    pallas_call x1, Pallas kernels, shards(): local_call(functools.partial(select_kernel, cp_size), 'select', [part] *...  0.82 us
    another operation x3, other arithmetic, shards(): line = jnp.stack([far[j] for j in group])  0.81 us
  transfers between devices with their start and end apart: 12, of which 9 were waited for; matrix products, arithmetic and copies ran while one was open for 3% of the time, Pallas kernels for 13%

profile of v4, /device:TPU:0, one launch (start us, length us, event | category | flops | bytes accessed | tf_op | source)
XLA Modules:
  0.0 29.9 jit_solution(16533312991496754890)
XLA Ops:
  0.0 0.8 %fusion = (bf16[1,128,256]{2,1,0:T(8,128)(2,1)S(1)}, bf16[128,256]{1,0:T(8,128)(2,1)S(1)}) fusion(bf16[128,128]{1,0:T(8,128)(2,1)} %param.7, bf16[128,128]{1,0:T(8,128)(2,1)} %param.6), kind=kLoop, calls=%fused_computation.4 | loop fusion | flops 131072 | bytes 196608 | tf_op jit(solution)/shard_map/stack | solution.py:266
  0.8 5.1 %collective-permute-start.3 = (bf16[128,256]{1,0:T(8,128)(2,1)S(1)}, bf16[128,256]{1,0:T(8,128)(2,1)S(1)}, u32[]{:S(2)}, u32[]{:S(2)}) collective-permute-start(bf16[128,256]{1,0:T(8,128)(2,1)S(1)} %get-tuple-element.34.own_ref), channel_id=1, source_target_pairs={{0,24},{2,26},{4,28},{6,30},{8,16},{10,18},{12,20},{14,22},{16,8},... | collective-permute-start | bytes 196616 | tf_op jit(solution)/shard_map/ppermute | solution.py:21
  5.9 0.0 collective-permute-start.1
  5.9 0.6 %collective-permute-start = (bf16[128,256]{1,0:T(8,128)(2,1)S(1)}, bf16[128,256]{1,0:T(8,128)(2,1)S(1)}, u32[]{:S(2)}, u32[]{:S(2)}) collective-permute-start(bf16[128,256]{1,0:T(8,128)(2,1)S(1)} %get-tuple-element.34.own_ref), channel_id=1, source_target_pairs={{0,8},{2,10},{4,12},{6,14},{8,0},{10,2},{12,4},{14,6},{16,24},{18,... | collective-permute-start | bytes 196616 | tf_op jit(solution)/shard_map/ppermute | solution.py:21
  6.5 1.9 %collective-permute-done.3 = bf16[128,256]{1,0:T(8,128)(2,1)S(1)} collective-permute-done((bf16[128,256]{1,0:T(8,128)(2,1)S(1)}, bf16[128,256]{1,0:T(8,128)(2,1)S(1)}, u32[]{:S(2)}, u32[]{:S(2)}) %collective-permute-start.3) | collective-permute-done | bytes 65568 | tf_op jit(solution)/shard_map/ppermute | solution.py:21
  8.5 1.9 %collective-permute-start.4 = (bf16[2,128,256]{2,1,0:T(8,128)(2,1)S(1)}, bf16[2,128,256]{2,1,0:T(8,128)(2,1)S(1)}, u32[]{:S(2)}, u32[]{:S(2)}) collective-permute-start(bf16[2,128,256]{2,1,0:T(8,128)(2,1)S(1)} %pad_maximum_fusion.1.refs_0_), channel_id=1, source_target_pairs={{0,4},{2,6},{4,0},{6,2},{8,12},{10,14},{12,8},{14,10},{16,20},{18,... | collective-permute-start | bytes 393224 | tf_op jit(solution)/shard_map/ppermute | solution.py:21
  10.4 1.1 %collective-permute-done.1 = bf16[128,256]{1,0:T(8,128)(2,1)S(1)} collective-permute-done((bf16[128,256]{1,0:T(8,128)(2,1)S(1)}, bf16[128,256]{1,0:T(8,128)(2,1)S(1)}, u32[]{:S(2)}, u32[]{:S(2)}) %collective-permute-start.1) | collective-permute-done | bytes 65568 | tf_op jit(solution)/shard_map/ppermute | solution.py:21
  11.5 0.0 collective-permute-done
  11.5 1.6 %collective-permute-start.2 = (bf16[2,128,256]{2,1,0:T(8,128)(2,1)S(1)}, bf16[2,128,256]{2,1,0:T(8,128)(2,1)S(1)}, u32[]{:S(2)}, u32[]{:S(2)}) collective-permute-start(bf16[2,128,256]{2,1,0:T(8,128)(2,1)S(1)} %pad_maximum_fusion.refs_4_), channel_id=1, source_target_pairs={{0,4},{2,6},{4,0},{6,2},{8,12},{10,14},{12,8},{14,10},{16,20},{18,... | collective-permute-start | bytes 393224 | tf_op jit(solution)/shard_map/ppermute | solution.py:21
  13.1 1.5 %collective-permute-start.5 = (bf16[128,256]{1,0:T(8,128)(2,1)S(1)}, bf16[128,256]{1,0:T(8,128)(2,1)S(1)}, u32[]{:S(2)}, u32[]{:S(2)}) collective-permute-start(bf16[128,256]{1,0:T(8,128)(2,1)S(1)} %get-tuple-element.34.own_ref), channel_id=1, source_target_pairs={{0,1},{1,0},{2,3},{3,2},{4,5},{5,4},{6,7},{7,6},{8,9},{9,8},{10,11... | collective-permute-start | bytes 196616 | tf_op jit(solution)/shard_map/ppermute | solution.py:21
  14.6 0.0 copy-start
  14.6 1.0 %copy-done = bf16[256,1024]{1,0:T(8,128)(2,1)S(1)} copy-done((bf16[256,1024]{1,0:T(8,128)(2,1)S(1)}, bf16[256,1024]{1,0:T(8,128)(2,1)}, u32[]{:S(2)}) %copy-start) | copy-done | bytes 524312
  15.6 0.3 %stack_queries.1.q_ref = bf16[2,1024,128]{2,1,0:T(8,128)(2,1)S(1)} custom-call(bf16[256,1024]{1,0:T(8,128)(2,1)S(1)} %copy-done), custom_call_target="tpu_custom_call" | custom-call | flops 1048576 | bytes 1048576 | tf_op jit(solution)/shard_map/stack_queries/pallas_call | solution.py:222
  16.0 0.8 %pad_add_fusion.1.meta_ref = s32[50]{0:T(128)S(1)} fusion(s32[32]{0:T(128)} %param.8, s32[16]{0:T(128)} %param.9, s32[1]{0:T(128)} %bitcast.5, s32[1]{0:T(128)} %bitcast.4), kind=kLoop, calls=%fused_computation.3 | loop fusion | flops 150 | bytes 400 | tf_op jit(solution)/shard_map/concatenate | solution.py:253
  16.7 0.0 collective-permute-start.8
  16.7 0.5 %collective-permute-start.6 = (bf16[2,128,256]{2,1,0:T(8,128)(2,1)S(1)}, bf16[2,128,256]{2,1,0:T(8,128)(2,1)S(1)}, u32[]{:S(2)}, u32[]{:S(2)}) collective-permute-start(bf16[2,128,256]{2,1,0:T(8,128)(2,1)S(1)} %pad_maximum_fusion.1.refs_0_), channel_id=1, source_target_pairs={{0,2},{2,0},{4,6},{6,4},{8,10},{10,8},{12,14},{14,12},{16,18},{18,... | collective-permute-start | bytes 393224 | tf_op jit(solution)/shard_map/ppermute | solution.py:21
  17.2 0.1 collective-permute-done.5.other_ref
  17.4 0.0 collective-permute-done.4.refs_1_
  17.4 0.0 collective-permute-done.2.refs_5_
  17.4 0.0 collective-permute-start.9
  17.4 0.5 %collective-permute-start.7 = (bf16[2,128,256]{2,1,0:T(8,128)(2,1)S(1)}, bf16[2,128,256]{2,1,0:T(8,128)(2,1)S(1)}, u32[]{:S(2)}, u32[]{:S(2)}) collective-permute-start(bf16[2,128,256]{2,1,0:T(8,128)(2,1)S(1)} %collective-permute-done.4.refs_1_), channel_id=1, source_target_pairs={{0,2},{2,0},{4,6},{6,4},{8,10},{10,8},{12,14},{14,12},{16,18},{18,... | collective-permute-start | bytes 393224 | tf_op jit(solution)/shard_map/ppermute | solution.py:21
  17.9 0.2 collective-permute-done.8.refs_6_
  18.1 0.2 collective-permute-done.6.refs_2_
  18.3 0.5 %collective-permute-done.9.refs_7_ = bf16[2,128,256]{2,1,0:T(8,128)(2,1)S(1)} collective-permute-done((bf16[2,128,256]{2,1,0:T(8,128)(2,1)S(1)}, bf16[2,128,256]{2,1,0:T(8,128)(2,1)S(1)}, u32[]{:S(2)}, u32[]{:S(2)}) %collective-permute-start.9) | collective-permute-done | bytes 131104 | tf_op jit(solution)/shard_map/ppermute | solution.py:21
  18.7 0.2 collective-permute-done.7.refs_3_
  18.9 0.8 %select.3 = (bf16[512,128]{1,0:T(8,128)(2,1)S(1)}, bf16[512,128]{1,0:T(8,128)(2,1)S(1)}) custom-call(s32[50]{0:T(128)S(1)} %pad_add_fusion.1.meta_ref, bf16[2,128,256]{2,1,0:T(8,128)(2,1)S(1)} %pad_maximum_fusion.1.refs_0_, bf16[2,128,256]{2,1,0:T(8,128)(2,1)S(1)} %collective-permute-done.4.refs_1_, bf16[2,128,256]{2,1,0:T(8,128)(2,1)S(1)} %collective-permute-done.6.refs_2_, ...), custom_call_target="tpu_custom_call" | custom-call | flops 1048576 | bytes 1048576 | tf_op jit(solution)/shard_map/select/pallas_call | solution.py:270
  19.7 1.6 %collective-permute-start.10 = (bf16[512,128]{1,0:T(8,128)(2,1)S(1)}, bf16[512,128]{1,0:T(8,128)(2,1)S(1)}, u32[]{:S(2)}, u32[]{:S(2)}) collective-permute-start(bf16[512,128]{1,0:T(8,128)(2,1)S(1)} %get-tuple-element.26.keys_ref), channel_id=1, source_target_pairs={{0,1},{1,0},{2,3},{3,2},{4,5},{5,4},{6,7},{7,6},{8,9},{9,8},{10,11... | collective-permute-start | bytes 393224 | tf_op jit(solution)/shard_map/ppermute | solution.py:21
  21.3 0.5 %collective-permute-start.11 = (bf16[512,128]{1,0:T(8,128)(2,1)S(1)}, bf16[512,128]{1,0:T(8,128)(2,1)S(1)}, u32[]{:S(2)}, u32[]{:S(2)}) collective-permute-start(bf16[512,128]{1,0:T(8,128)(2,1)S(1)} %get-tuple-element.28.values_ref), channel_id=1, source_target_pairs={{0,1},{1,0},{2,3},{3,2},{4,5},{5,4},{6,7},{7,6},{8,9},{9,8},{10,11... | collective-permute-start | bytes 393224 | tf_op jit(solution)/shard_map/ppermute | solution.py:21
  21.8 2.1 %attend_first.1 = (f32[2,1024,128]{2,1,0:T(8,128)S(1)}, f32[2,1024,256]{2,1,0:T(8,128)S(1)}) custom-call(s32[50]{0:T(128)S(1)} %pad_add_fusion.1.meta_ref, bf16[2,1024,128]{2,1,0:T(8,128)(2,1)S(1)} %stack_queries.1.q_ref, bf16[128,256]{1,0:T(8,128)(2,1)S(1)} %get-tuple-element.34.own_ref, bf16[128,256]{1,0:T(8,128)(2,1)S(1)} %collective-permute-done.5.other_ref, ...), custom_call_target="tpu_custom_call" | custom-call | flops 2147483648 | bytes 1048576 | tf_op jit(solution)/shard_map/attend_first/pallas_call | solution.py:232
  23.9 2.2 %collective-permute-done.10.keys_ref = bf16[512,128]{1,0:T(8,128)(2,1)S(1)} collective-permute-done((bf16[512,128]{1,0:T(8,128)(2,1)S(1)}, bf16[512,128]{1,0:T(8,128)(2,1)S(1)}, u32[]{:S(2)}, u32[]{:S(2)}) %collective-permute-start.10) | collective-permute-done | bytes 131104 | tf_op jit(solution)/shard_map/ppermute | solution.py:21
  26.1 1.5 %attend_weigh.1 = (bf16[2,1024,512]{2,1,0:T(8,128)(2,1)S(1)}, f32[2,1024,128]{2,1,0:T(8,128)S(1)}) custom-call(s32[50]{0:T(128)S(1)} %pad_add_fusion.1.meta_ref, bf16[2,1024,128]{2,1,0:T(8,128)(2,1)S(1)} %stack_queries.1.q_ref, bf16[512,128]{1,0:T(8,128)(2,1)S(1)} %collective-permute-done.10.keys_ref, f32[2,1024,128]{2,1,0:T(8,128)S(1)} %get-tuple-element.29.max_ref, ...), custom_call_target="tpu_custom_call" | custom-call | flops 1073741824 | bytes 1048576 | tf_op jit(solution)/shard_map/attend_weigh/pallas_call | solution.py:235
  27.6 0.7 %collective-permute-done.11.values_ref = bf16[512,128]{1,0:T(8,128)(2,1)S(1)} collective-permute-done((bf16[512,128]{1,0:T(8,128)(2,1)S(1)}, bf16[512,128]{1,0:T(8,128)(2,1)S(1)}, u32[]{:S(2)}, u32[]{:S(2)}) %collective-permute-start.11) | collective-permute-done | bytes 131104 | tf_op jit(solution)/shard_map/ppermute | solution.py:21
  28.3 1.4 %attend_finish.1 = bf16[256,1024]{1,0:T(8,128)(2,1)} custom-call(bf16[2,1024,512]{2,1,0:T(8,128)(2,1)S(1)} %get-tuple-element.31.weights_ref, f32[2,1024,128]{2,1,0:T(8,128)S(1)} %get-tuple-element.32.rest_ref, bf16[512,128]{1,0:T(8,128)(2,1)S(1)} %collective-permute-done.11.values_ref), custom_call_target="tpu_custom_call" | custom-call | flops 536870912 | bytes 1048576 | tf_op jit(solution)/shard_map/attend_finish/pallas_call | solution.py:245
  (2 shorter events, 0.0 us)
Async XLA Ops:
  0.8 7.7 %collective-permute-start.3 = (bf16[128,256]{1,0:T(8,128)(2,1)S(1)}, bf16[128,256]{1,0:T(8,128)(2,1)S(1)}, u32[]{:S(2)}, u32[]{:S(2)}) collective-permute-start(bf16[128,256]{1,0:T(8,128)(2,1)S(1)} %get-tuple-element.34.own_ref), channel_id=1, source_target_pairs={{0,24},{2,26},{4,28},{6,30},{8,16},{10,18},{12,20},{14,22},{16,8},... | collective-permute-start | bytes 196616 | tf_op jit(solution)/shard_map/ppermute | solution.py:21
  5.9 5.6 %collective-permute-start.1 = (bf16[128,256]{1,0:T(8,128)(2,1)S(1)}, bf16[128,256]{1,0:T(8,128)(2,1)S(1)}, u32[]{:S(2)}, u32[]{:S(2)}) collective-permute-start(bf16[128,256]{1,0:T(8,128)(2,1)S(1)} %get-tuple-element.34.own_ref), channel_id=1, source_target_pairs={{0,16},{2,18},{4,20},{6,22},{8,24},{10,26},{12,28},{14,30},{16,0},... | collective-permute-start | bytes 196616 | tf_op jit(solution)/shard_map/ppermute | solution.py:21
  5.9 5.6 %collective-permute-start = (bf16[128,256]{1,0:T(8,128)(2,1)S(1)}, bf16[128,256]{1,0:T(8,128)(2,1)S(1)}, u32[]{:S(2)}, u32[]{:S(2)}) collective-permute-start(bf16[128,256]{1,0:T(8,128)(2,1)S(1)} %get-tuple-element.34.own_ref), channel_id=1, source_target_pairs={{0,8},{2,10},{4,12},{6,14},{8,0},{10,2},{12,4},{14,6},{16,24},{18,... | collective-permute-start | bytes 196616 | tf_op jit(solution)/shard_map/ppermute | solution.py:21
  8.5 8.9 %collective-permute-start.4 = (bf16[2,128,256]{2,1,0:T(8,128)(2,1)S(1)}, bf16[2,128,256]{2,1,0:T(8,128)(2,1)S(1)}, u32[]{:S(2)}, u32[]{:S(2)}) collective-permute-start(bf16[2,128,256]{2,1,0:T(8,128)(2,1)S(1)} %pad_maximum_fusion.1.refs_0_), channel_id=1, source_target_pairs={{0,4},{2,6},{4,0},{6,2},{8,12},{10,14},{12,8},{14,10},{16,20},{18,... | collective-permute-start | bytes 393224 | tf_op jit(solution)/shard_map/ppermute | solution.py:21
  11.5 5.8 %collective-permute-start.2 = (bf16[2,128,256]{2,1,0:T(8,128)(2,1)S(1)}, bf16[2,128,256]{2,1,0:T(8,128)(2,1)S(1)}, u32[]{:S(2)}, u32[]{:S(2)}) collective-permute-start(bf16[2,128,256]{2,1,0:T(8,128)(2,1)S(1)} %pad_maximum_fusion.refs_4_), channel_id=1, source_target_pairs={{0,4},{2,6},{4,0},{6,2},{8,12},{10,14},{12,8},{14,10},{16,20},{18,... | collective-permute-start | bytes 393224 | tf_op jit(solution)/shard_map/ppermute | solution.py:21
  13.1 4.3 %collective-permute-start.5 = (bf16[128,256]{1,0:T(8,128)(2,1)S(1)}, bf16[128,256]{1,0:T(8,128)(2,1)S(1)}, u32[]{:S(2)}, u32[]{:S(2)}) collective-permute-start(bf16[128,256]{1,0:T(8,128)(2,1)S(1)} %get-tuple-element.34.own_ref), channel_id=1, source_target_pairs={{0,1},{1,0},{2,3},{3,2},{4,5},{5,4},{6,7},{7,6},{8,9},{9,8},{10,11... | collective-permute-start | bytes 196616 | tf_op jit(solution)/shard_map/ppermute | solution.py:21
  14.6 1.0 %copy-start = (bf16[256,1024]{1,0:T(8,128)(2,1)S(1)}, bf16[256,1024]{1,0:T(8,128)(2,1)}, u32[]{:S(2)}) copy-start(bf16[256,1024]{1,0:T(8,128)(2,1)} %q_ref.1) | copy-start | bytes 1572868
  16.7 1.3 %collective-permute-start.8 = (bf16[2,128,256]{2,1,0:T(8,128)(2,1)S(1)}, bf16[2,128,256]{2,1,0:T(8,128)(2,1)S(1)}, u32[]{:S(2)}, u32[]{:S(2)}) collective-permute-start(bf16[2,128,256]{2,1,0:T(8,128)(2,1)S(1)} %pad_maximum_fusion.refs_4_), channel_id=1, source_target_pairs={{0,2},{2,0},{4,6},{6,4},{8,10},{10,8},{12,14},{14,12},{16,18},{18,... | collective-permute-start | bytes 393224 | tf_op jit(solution)/shard_map/ppermute | solution.py:21
  16.7 1.5 %collective-permute-start.6 = (bf16[2,128,256]{2,1,0:T(8,128)(2,1)S(1)}, bf16[2,128,256]{2,1,0:T(8,128)(2,1)S(1)}, u32[]{:S(2)}, u32[]{:S(2)}) collective-permute-start(bf16[2,128,256]{2,1,0:T(8,128)(2,1)S(1)} %pad_maximum_fusion.1.refs_0_), channel_id=1, source_target_pairs={{0,2},{2,0},{4,6},{6,4},{8,10},{10,8},{12,14},{14,12},{16,18},{18,... | collective-permute-start | bytes 393224 | tf_op jit(solution)/shard_map/ppermute | solution.py:21
  17.4 1.4 %collective-permute-start.9 = (bf16[2,128,256]{2,1,0:T(8,128)(2,1)S(1)}, bf16[2,128,256]{2,1,0:T(8,128)(2,1)S(1)}, u32[]{:S(2)}, u32[]{:S(2)}) collective-permute-start(bf16[2,128,256]{2,1,0:T(8,128)(2,1)S(1)} %collective-permute-done.2.refs_5_), channel_id=1, source_target_pairs={{0,2},{2,0},{4,6},{6,4},{8,10},{10,8},{12,14},{14,12},{16,18},{18,... | collective-permute-start | bytes 393224 | tf_op jit(solution)/shard_map/ppermute | solution.py:21
  17.4 1.5 %collective-permute-start.7 = (bf16[2,128,256]{2,1,0:T(8,128)(2,1)S(1)}, bf16[2,128,256]{2,1,0:T(8,128)(2,1)S(1)}, u32[]{:S(2)}, u32[]{:S(2)}) collective-permute-start(bf16[2,128,256]{2,1,0:T(8,128)(2,1)S(1)} %collective-permute-done.4.refs_1_), channel_id=1, source_target_pairs={{0,2},{2,0},{4,6},{6,4},{8,10},{10,8},{12,14},{14,12},{16,18},{18,... | collective-permute-start | bytes 393224 | tf_op jit(solution)/shard_map/ppermute | solution.py:21
  19.7 6.4 %collective-permute-start.10 = (bf16[512,128]{1,0:T(8,128)(2,1)S(1)}, bf16[512,128]{1,0:T(8,128)(2,1)S(1)}, u32[]{:S(2)}, u32[]{:S(2)}) collective-permute-start(bf16[512,128]{1,0:T(8,128)(2,1)S(1)} %get-tuple-element.26.keys_ref), channel_id=1, source_target_pairs={{0,1},{1,0},{2,3},{3,2},{4,5},{5,4},{6,7},{7,6},{8,9},{9,8},{10,11... | collective-permute-start | bytes 393224 | tf_op jit(solution)/shard_map/ppermute | solution.py:21
  21.3 7.0 %collective-permute-start.11 = (bf16[512,128]{1,0:T(8,128)(2,1)S(1)}, bf16[512,128]{1,0:T(8,128)(2,1)S(1)}, u32[]{:S(2)}, u32[]{:S(2)}) collective-permute-start(bf16[512,128]{1,0:T(8,128)(2,1)S(1)} %get-tuple-element.28.values_ref), channel_id=1, source_target_pairs={{0,1},{1,0},{2,3},{3,2},{4,5},{5,4},{6,7},{7,6},{8,9},{9,8},{10,11... | collective-permute-start | bytes 393224 | tf_op jit(solution)/shard_map/ppermute | solution.py:21

commit v5 on v4

--- a/solution.py
+++ b/solution.py
@@ -259,13 +259,15 @@
         by_y = lambda array: flip(array, "sp", sp_size, 1)
         by_core = lambda array: flip(array, "cp", cp_size, 1)
         far = {j: flip(own, "cp", cp_size, 4 * j) for j in (3, 2, 1)}
+        far[1], far[2], queries, meta = lax.optimization_barrier((far[1], far[2], queries, meta))
         far[0] = own
-        other = by_y(own)
         sources = []
         for group in LINES:
             line = jnp.stack([far[j] for j in group])
-            side, meta, other, queries = lax.optimization_barrier((by_x(line), meta, other, queries))
+            side = by_x(line)
             sources += [line, side, by_core(line), by_core(side)]
+        sources[5], own_late = lax.optimization_barrier((sources[5], own))
+        other = by_y(own_late)
         part = jax.ShapeDtypeStruct((reach * BLK, HD), jnp.bfloat16)
         picked = local_call(
             functools.partial(select_kernel, cp_size), "select", [part] * 2, [SMEM] + [VMEM] * len(sources), 4, 1 << 20

time: 30.1 us -> 29.5 us (0.980)
  starting transfers between devices: 13.9 us -> 13.4 us
  waiting for transfers between devices: 7.13 us -> 6.68 us
  Pallas kernels: 6.1 us -> 6.43 us
    ppermute x12, starting transfers between devices: 13.9 us -> 13.4 us  [flip(): return lax.ppermute(array, axis, [(i, i ^ mask) for i in range(size)])]
    ppermute x12, waiting for transfers between devices: 7.13 us -> 6.68 us  [flip(): return lax.ppermute(array, axis, [(i, i ^ mask) for i in range(size)])]
    pallas_call x1, Pallas kernels: 1.47 us -> 1.89 us  [attend(): local_call(kernel, 'attend_weigh', outs, ins, 12, 1 << 30)]
  transfers between devices with their start and end apart: 12 -> 12, of which waited for: 9 -> 5; matrix products, arithmetic and copies ran while one was open for 3% -> 3% of each run, Pallas kernels for 13% -> 17%
where the time goes in v5:
time: 29.5 us; the launch traced here: 29.3 us
  starting transfers between devices  13.4 us (45%)
  waiting for transfers between devices  6.68 us (23%)
  Pallas kernels  6.43 us (22%)
  other arithmetic  1.57 us (5%)
  local copies, waits for them, and re-layouts  1.04 us (4%)
    ppermute x12, starting transfers between devices, flip(): return lax.ppermute(array, axis, [(i, i ^ mask) for i in range(size)])  13.4 us
    ppermute x12, waiting for transfers between devices, flip(): return lax.ppermute(array, axis, [(i, i ^ mask) for i in range(size)])  6.68 us
    pallas_call x1, Pallas kernels, attend(): local_call(kernel, 'attend_first', outs, ins, 12, 1 << 31)  1.98 us
    pallas_call x1, Pallas kernels, attend(): local_call(kernel, 'attend_weigh', outs, ins, 12, 1 << 30)  1.89 us
    pallas_call x1, Pallas kernels, attend(): return finish(weights, rest, other_values)[0]  1.42 us
    unnamed x2, local copies, waits for them, and re-layouts  1.04 us
    pallas_call x1, Pallas kernels, shards(): local_call(functools.partial(select_kernel, cp_size), 'select', [part] *...  0.82 us
    another operation x3, other arithmetic, shards(): line = jnp.stack([far[j] for j in group])  0.81 us
  transfers between devices with their start and end apart: 12, of which 5 were waited for; matrix products, arithmetic and copies ran while one was open for 3% of the time, Pallas kernels for 17%

profile of v5, /device:TPU:0, one launch (start us, length us, event | category | flops | bytes accessed | tf_op | source)
XLA Modules:
  0.0 29.3 jit_solution(1549637006396251011)
XLA Ops:
  0.0 0.8 %fusion = (bf16[1,128,256]{2,1,0:T(8,128)(2,1)S(1)}, bf16[128,256]{1,0:T(8,128)(2,1)S(1)}) fusion(bf16[128,128]{1,0:T(8,128)(2,1)} %param.7, bf16[128,128]{1,0:T(8,128)(2,1)} %param.6), kind=kLoop, calls=%fused_computation.4 | loop fusion | flops 131072 | bytes 196608 | tf_op jit(solution)/shard_map/stack | solution.py:266
  0.8 5.1 %collective-permute-start.2 = (bf16[128,256]{1,0:T(8,128)(2,1)S(1)}, bf16[128,256]{1,0:T(8,128)(2,1)S(1)}, u32[]{:S(2)}, u32[]{:S(2)}) collective-permute-start(bf16[128,256]{1,0:T(8,128)(2,1)S(1)} %get-tuple-element.23.own_ref), channel_id=1, source_target_pairs={{0,24},{2,26},{4,28},{6,30},{8,16},{10,18},{12,20},{14,22},{16,8},... | collective-permute-start | bytes 196616 | tf_op jit(solution)/shard_map/ppermute | solution.py:21
  5.9 0.0 collective-permute-start.1
  5.9 0.6 %collective-permute-start = (bf16[128,256]{1,0:T(8,128)(2,1)S(1)}, bf16[128,256]{1,0:T(8,128)(2,1)S(1)}, u32[]{:S(2)}, u32[]{:S(2)}) collective-permute-start(bf16[128,256]{1,0:T(8,128)(2,1)S(1)} %get-tuple-element.23.own_ref), channel_id=1, source_target_pairs={{0,8},{2,10},{4,12},{6,14},{8,0},{10,2},{12,4},{14,6},{16,24},{18,... | collective-permute-start | bytes 196616 | tf_op jit(solution)/shard_map/ppermute | solution.py:21
  6.5 0.0 copy-start
  6.5 1.0 %copy-done = bf16[256,1024]{1,0:T(8,128)(2,1)S(1)} copy-done((bf16[256,1024]{1,0:T(8,128)(2,1)S(1)}, bf16[256,1024]{1,0:T(8,128)(2,1)}, u32[]{:S(2)}) %copy-start) | copy-done | bytes 524312
  7.6 0.3 %stack_queries.1.q_ref = bf16[2,1024,128]{2,1,0:T(8,128)(2,1)S(1)} custom-call(bf16[256,1024]{1,0:T(8,128)(2,1)S(1)} %copy-done), custom_call_target="tpu_custom_call" | custom-call | flops 1048576 | bytes 1048576 | tf_op jit(solution)/shard_map/stack_queries/pallas_call | solution.py:222
  7.9 0.8 %pad_add_fusion.1.meta_ref = s32[50]{0:T(128)S(1)} fusion(s32[32]{0:T(128)} %param.8, s32[16]{0:T(128)} %param.9, s32[1]{0:T(128)} %bitcast.1, s32[1]{0:T(128)} %bitcast), kind=kLoop, calls=%fused_computation.3 | loop fusion | flops 150 | bytes 400 | tf_op jit(solution)/shard_map/concatenate | solution.py:253
  8.7 0.0 collective-permute-done.2
  8.7 1.7 %collective-permute-start.3 = (bf16[2,128,256]{2,1,0:T(8,128)(2,1)S(1)}, bf16[2,128,256]{2,1,0:T(8,128)(2,1)S(1)}, u32[]{:S(2)}, u32[]{:S(2)}) collective-permute-start(bf16[2,128,256]{2,1,0:T(8,128)(2,1)S(1)} %pad_maximum_fusion.refs_0_), channel_id=1, source_target_pairs={{0,4},{2,6},{4,0},{6,2},{8,12},{10,14},{12,8},{14,10},{16,20},{18,... | collective-permute-start | bytes 393224 | tf_op jit(solution)/shard_map/ppermute | solution.py:21
  10.4 1.1 %collective-permute-done.1 = bf16[128,256]{1,0:T(8,128)(2,1)S(1)} collective-permute-done((bf16[128,256]{1,0:T(8,128)(2,1)S(1)}, bf16[128,256]{1,0:T(8,128)(2,1)S(1)}, u32[]{:S(2)}, u32[]{:S(2)}) %collective-permute-start.1) | collective-permute-done | bytes 65568 | tf_op jit(solution)/shard_map/ppermute | solution.py:21
  11.5 0.0 collective-permute-done
  11.5 1.6 %collective-permute-start.6 = (bf16[2,128,256]{2,1,0:T(8,128)(2,1)S(1)}, bf16[2,128,256]{2,1,0:T(8,128)(2,1)S(1)}, u32[]{:S(2)}, u32[]{:S(2)}) collective-permute-start(bf16[2,128,256]{2,1,0:T(8,128)(2,1)S(1)} %pad_maximum_fusion.1.refs_4_), channel_id=1, source_target_pairs={{0,4},{2,6},{4,0},{6,2},{8,12},{10,14},{12,8},{14,10},{16,20},{18,... | collective-permute-start | bytes 393224 | tf_op jit(solution)/shard_map/ppermute | solution.py:21
  13.1 0.0 collective-permute-start.4
  13.1 0.5 %collective-permute-start.7 = (bf16[2,128,256]{2,1,0:T(8,128)(2,1)S(1)}, bf16[2,128,256]{2,1,0:T(8,128)(2,1)S(1)}, u32[]{:S(2)}, u32[]{:S(2)}) collective-permute-start(bf16[2,128,256]{2,1,0:T(8,128)(2,1)S(1)} %pad_maximum_fusion.1.refs_4_), channel_id=1, source_target_pairs={{0,2},{2,0},{4,6},{6,4},{8,10},{10,8},{12,14},{14,12},{16,18},{18,... | collective-permute-start | bytes 393224 | tf_op jit(solution)/shard_map/ppermute | solution.py:21
  13.6 0.1 collective-permute-done.3.refs_1_
  13.7 0.0 collective-permute-start.5
  13.7 2.9 %collective-permute-done.6.refs_5_ = bf16[2,128,256]{2,1,0:T(8,128)(2,1)S(1)} collective-permute-done((bf16[2,128,256]{2,1,0:T(8,128)(2,1)S(1)}, bf16[2,128,256]{2,1,0:T(8,128)(2,1)S(1)}, u32[]{:S(2)}, u32[]{:S(2)}) %collective-permute-start.6) | collective-permute-done | bytes 131104 | tf_op jit(solution)/shard_map/ppermute | solution.py:21
  16.7 0.0 collective-permute-start.8
  16.7 1.7 %collective-permute-start.10 = (bf16[128,256]{1,0:T(8,128)(2,1)S(1)}, bf16[128,256]{1,0:T(8,128)(2,1)S(1)}, u32[]{:S(2)}, u32[]{:S(2)}) collective-permute-start(bf16[128,256]{1,0:T(8,128)(2,1)S(1)} %get-tuple-element.23.own_ref), channel_id=1, source_target_pairs={{0,1},{1,0},{2,3},{3,2},{4,5},{5,4},{6,7},{7,6},{8,9},{9,8},{10,11... | collective-permute-start | bytes 196616 | tf_op jit(solution)/shard_map/ppermute | solution.py:21
  18.4 0.0 collective-permute-done.4.refs_2_
  18.4 0.0 collective-permute-done.7.refs_6_
  18.4 0.0 collective-permute-done.5.refs_3_
  18.4 0.0 collective-permute-done.8.refs_7_
  18.4 0.8 %select.3 = (bf16[512,128]{1,0:T(8,128)(2,1)S(1)}, bf16[512,128]{1,0:T(8,128)(2,1)S(1)}) custom-call(s32[50]{0:T(128)S(1)} %pad_add_fusion.1.meta_ref, bf16[2,128,256]{2,1,0:T(8,128)(2,1)S(1)} %pad_maximum_fusion.refs_0_, bf16[2,128,256]{2,1,0:T(8,128)(2,1)S(1)} %collective-permute-done.3.refs_1_, bf16[2,128,256]{2,1,0:T(8,128)(2,1)S(1)} %collective-permute-done.4.refs_2_, ...), custom_call_target="tpu_custom_call" | custom-call | flops 1048576 | bytes 1048576 | tf_op jit(solution)/shard_map/select/pallas_call | solution.py:272
  19.2 1.4 %collective-permute-start.9 = (bf16[512,128]{1,0:T(8,128)(2,1)S(1)}, bf16[512,128]{1,0:T(8,128)(2,1)S(1)}, u32[]{:S(2)}, u32[]{:S(2)}) collective-permute-start(bf16[512,128]{1,0:T(8,128)(2,1)S(1)} %get-tuple-element.22.keys_ref), channel_id=1, source_target_pairs={{0,1},{1,0},{2,3},{3,2},{4,5},{5,4},{6,7},{7,6},{8,9},{9,8},{10,11... | collective-permute-start | bytes 393224 | tf_op jit(solution)/shard_map/ppermute | solution.py:21
  20.6 0.7 %collective-permute-start.11 = (bf16[512,128]{1,0:T(8,128)(2,1)S(1)}, bf16[512,128]{1,0:T(8,128)(2,1)S(1)}, u32[]{:S(2)}, u32[]{:S(2)}) collective-permute-start(bf16[512,128]{1,0:T(8,128)(2,1)S(1)} %get-tuple-element.24.values_ref), channel_id=1, source_target_pairs={{0,1},{1,0},{2,3},{3,2},{4,5},{5,4},{6,7},{7,6},{8,9},{9,8},{10,11... | collective-permute-start | bytes 393224 | tf_op jit(solution)/shard_map/ppermute | solution.py:21
  21.3 0.0 collective-permute-done.10.other_ref
  21.3 2.0 %attend_first.1 = (f32[2,1024,128]{2,1,0:T(8,128)S(1)}, f32[2,1024,256]{2,1,0:T(8,128)S(1)}) custom-call(s32[50]{0:T(128)S(1)} %pad_add_fusion.1.meta_ref, bf16[2,1024,128]{2,1,0:T(8,128)(2,1)S(1)} %stack_queries.1.q_ref, bf16[128,256]{1,0:T(8,128)(2,1)S(1)} %get-tuple-element.23.own_ref, bf16[128,256]{1,0:T(8,128)(2,1)S(1)} %collective-permute-done.10.other_ref, ...), custom_call_target="tpu_custom_call" | custom-call | flops 2147483648 | bytes 1048576 | tf_op jit(solution)/shard_map/attend_first/pallas_call | solution.py:232
  23.3 2.3 %collective-permute-done.9.keys_ref = bf16[512,128]{1,0:T(8,128)(2,1)S(1)} collective-permute-done((bf16[512,128]{1,0:T(8,128)(2,1)S(1)}, bf16[512,128]{1,0:T(8,128)(2,1)S(1)}, u32[]{:S(2)}, u32[]{:S(2)}) %collective-permute-start.9) | collective-permute-done | bytes 131104 | tf_op jit(solution)/shard_map/ppermute | solution.py:21
  25.6 1.9 %attend_weigh.1 = (bf16[2,1024,512]{2,1,0:T(8,128)(2,1)S(1)}, f32[2,1024,128]{2,1,0:T(8,128)S(1)}) custom-call(s32[50]{0:T(128)S(1)} %pad_add_fusion.1.meta_ref, bf16[2,1024,128]{2,1,0:T(8,128)(2,1)S(1)} %stack_queries.1.q_ref, bf16[512,128]{1,0:T(8,128)(2,1)S(1)} %collective-permute-done.9.keys_ref, f32[2,1024,128]{2,1,0:T(8,128)S(1)} %get-tuple-element.25.max_ref, ...), custom_call_target="tpu_custom_call" | custom-call | flops 1073741824 | bytes 1048576 | tf_op jit(solution)/shard_map/attend_weigh/pallas_call | solution.py:235
  27.5 0.2 collective-permute-done.11.values_ref
  27.7 1.4 %attend_finish.1 = bf16[256,1024]{1,0:T(8,128)(2,1)} custom-call(bf16[2,1024,512]{2,1,0:T(8,128)(2,1)S(1)} %get-tuple-element.27.weights_ref, f32[2,1024,128]{2,1,0:T(8,128)S(1)} %get-tuple-element.28.rest_ref, bf16[512,128]{1,0:T(8,128)(2,1)S(1)} %collective-permute-done.11.values_ref), custom_call_target="tpu_custom_call" | custom-call | flops 536870912 | bytes 1048576 | tf_op jit(solution)/shard_map/attend_finish/pallas_call | solution.py:245
  (2 shorter events, 0.0 us)
Async XLA Ops:
  0.8 7.9 %collective-permute-start.2 = (bf16[128,256]{1,0:T(8,128)(2,1)S(1)}, bf16[128,256]{1,0:T(8,128)(2,1)S(1)}, u32[]{:S(2)}, u32[]{:S(2)}) collective-permute-start(bf16[128,256]{1,0:T(8,128)(2,1)S(1)} %get-tuple-element.23.own_ref), channel_id=1, source_target_pairs={{0,24},{2,26},{4,28},{6,30},{8,16},{10,18},{12,20},{14,22},{16,8},... | collective-permute-start | bytes 196616 | tf_op jit(solution)/shard_map/ppermute | solution.py:21
  5.9 5.6 %collective-permute-start.1 = (bf16[128,256]{1,0:T(8,128)(2,1)S(1)}, bf16[128,256]{1,0:T(8,128)(2,1)S(1)}, u32[]{:S(2)}, u32[]{:S(2)}) collective-permute-start(bf16[128,256]{1,0:T(8,128)(2,1)S(1)} %get-tuple-element.23.own_ref), channel_id=1, source_target_pairs={{0,16},{2,18},{4,20},{6,22},{8,24},{10,26},{12,28},{14,30},{16,0},... | collective-permute-start | bytes 196616 | tf_op jit(solution)/shard_map/ppermute | solution.py:21
  5.9 5.6 %collective-permute-start = (bf16[128,256]{1,0:T(8,128)(2,1)S(1)}, bf16[128,256]{1,0:T(8,128)(2,1)S(1)}, u32[]{:S(2)}, u32[]{:S(2)}) collective-permute-start(bf16[128,256]{1,0:T(8,128)(2,1)S(1)} %get-tuple-element.23.own_ref), channel_id=1, source_target_pairs={{0,8},{2,10},{4,12},{6,14},{8,0},{10,2},{12,4},{14,6},{16,24},{18,... | collective-permute-start | bytes 196616 | tf_op jit(solution)/shard_map/ppermute | solution.py:21
  6.5 1.0 %copy-start = (bf16[256,1024]{1,0:T(8,128)(2,1)S(1)}, bf16[256,1024]{1,0:T(8,128)(2,1)}, u32[]{:S(2)}) copy-start(bf16[256,1024]{1,0:T(8,128)(2,1)} %q_ref.1) | copy-start | bytes 1572868
  8.7 5.0 %collective-permute-start.3 = (bf16[2,128,256]{2,1,0:T(8,128)(2,1)S(1)}, bf16[2,128,256]{2,1,0:T(8,128)(2,1)S(1)}, u32[]{:S(2)}, u32[]{:S(2)}) collective-permute-start(bf16[2,128,256]{2,1,0:T(8,128)(2,1)S(1)} %pad_maximum_fusion.refs_0_), channel_id=1, source_target_pairs={{0,4},{2,6},{4,0},{6,2},{8,12},{10,14},{12,8},{14,10},{16,20},{18,... | collective-permute-start | bytes 393224 | tf_op jit(solution)/shard_map/ppermute | solution.py:21
  11.5 5.1 %collective-permute-start.6 = (bf16[2,128,256]{2,1,0:T(8,128)(2,1)S(1)}, bf16[2,128,256]{2,1,0:T(8,128)(2,1)S(1)}, u32[]{:S(2)}, u32[]{:S(2)}) collective-permute-start(bf16[2,128,256]{2,1,0:T(8,128)(2,1)S(1)} %pad_maximum_fusion.1.refs_4_), channel_id=1, source_target_pairs={{0,4},{2,6},{4,0},{6,2},{8,12},{10,14},{12,8},{14,10},{16,20},{18,... | collective-permute-start | bytes 393224 | tf_op jit(solution)/shard_map/ppermute | solution.py:21
  13.1 5.3 %collective-permute-start.4 = (bf16[2,128,256]{2,1,0:T(8,128)(2,1)S(1)}, bf16[2,128,256]{2,1,0:T(8,128)(2,1)S(1)}, u32[]{:S(2)}, u32[]{:S(2)}) collective-permute-start(bf16[2,128,256]{2,1,0:T(8,128)(2,1)S(1)} %pad_maximum_fusion.refs_0_), channel_id=1, source_target_pairs={{0,2},{2,0},{4,6},{6,4},{8,10},{10,8},{12,14},{14,12},{16,18},{18,... | collective-permute-start | bytes 393224 | tf_op jit(solution)/shard_map/ppermute | solution.py:21
  13.1 5.3 %collective-permute-start.7 = (bf16[2,128,256]{2,1,0:T(8,128)(2,1)S(1)}, bf16[2,128,256]{2,1,0:T(8,128)(2,1)S(1)}, u32[]{:S(2)}, u32[]{:S(2)}) collective-permute-start(bf16[2,128,256]{2,1,0:T(8,128)(2,1)S(1)} %pad_maximum_fusion.1.refs_4_), channel_id=1, source_target_pairs={{0,2},{2,0},{4,6},{6,4},{8,10},{10,8},{12,14},{14,12},{16,18},{18,... | collective-permute-start | bytes 393224 | tf_op jit(solution)/shard_map/ppermute | solution.py:21
  13.7 4.7 %collective-permute-start.5 = (bf16[2,128,256]{2,1,0:T(8,128)(2,1)S(1)}, bf16[2,128,256]{2,1,0:T(8,128)(2,1)S(1)}, u32[]{:S(2)}, u32[]{:S(2)}) collective-permute-start(bf16[2,128,256]{2,1,0:T(8,128)(2,1)S(1)} %collective-permute-done.3.refs_1_), channel_id=1, source_target_pairs={{0,2},{2,0},{4,6},{6,4},{8,10},{10,8},{12,14},{14,12},{16,18},{18,... | collective-permute-start | bytes 393224 | tf_op jit(solution)/shard_map/ppermute | solution.py:21
  16.7 1.7 %collective-permute-start.8 = (bf16[2,128,256]{2,1,0:T(8,128)(2,1)S(1)}, bf16[2,128,256]{2,1,0:T(8,128)(2,1)S(1)}, u32[]{:S(2)}, u32[]{:S(2)}) collective-permute-start(bf16[2,128,256]{2,1,0:T(8,128)(2,1)S(1)} %collective-permute-done.6.refs_5_), channel_id=1, source_target_pairs={{0,2},{2,0},{4,6},{6,4},{8,10},{10,8},{12,14},{14,12},{16,18},{18,... | collective-permute-start | bytes 393224 | tf_op jit(solution)/shard_map/ppermute | solution.py:21
  16.7 4.7 %collective-permute-start.10 = (bf16[128,256]{1,0:T(8,128)(2,1)S(1)}, bf16[128,256]{1,0:T(8,128)(2,1)S(1)}, u32[]{:S(2)}, u32[]{:S(2)}) collective-permute-start(bf16[128,256]{1,0:T(8,128)(2,1)S(1)} %get-tuple-element.23.own_ref), channel_id=1, source_target_pairs={{0,1},{1,0},{2,3},{3,2},{4,5},{5,4},{6,7},{7,6},{8,9},{9,8},{10,11... | collective-permute-start | bytes 196616 | tf_op jit(solution)/shard_map/ppermute | solution.py:21
  19.2 6.4 %collective-permute-start.9 = (bf16[512,128]{1,0:T(8,128)(2,1)S(1)}, bf16[512,128]{1,0:T(8,128)(2,1)S(1)}, u32[]{:S(2)}, u32[]{:S(2)}) collective-permute-start(bf16[512,128]{1,0:T(8,128)(2,1)S(1)} %get-tuple-element.22.keys_ref), channel_id=1, source_target_pairs={{0,1},{1,0},{2,3},{3,2},{4,5},{5,4},{6,7},{7,6},{8,9},{9,8},{10,11... | collective-permute-start | bytes 393224 | tf_op jit(solution)/shard_map/ppermute | solution.py:21
  20.6 7.1 %collective-permute-start.11 = (bf16[512,128]{1,0:T(8,128)(2,1)S(1)}, bf16[512,128]{1,0:T(8,128)(2,1)S(1)}, u32[]{:S(2)}, u32[]{:S(2)}) collective-permute-start(bf16[512,128]{1,0:T(8,128)(2,1)S(1)} %get-tuple-element.24.values_ref), channel_id=1, source_target_pairs={{0,1},{1,0},{2,3},{3,2},{4,5},{5,4},{6,7},{7,6},{8,9},{9,8},{10,11... | collective-permute-start | bytes 393224 | tf_op jit(solution)/shard_map/ppermute | solution.py:21

commit v6 on v5

--- a/solution.py
+++ b/solution.py
@@ -29,13 +29,16 @@
 
 def select_kernel(cp_size, meta_ref, *refs):
     sources, (keys_ref, values_ref) = refs[:-2], refs[-2:]
-    cp = meta_ref[0]
-    own_span = meta_ref[HEAD + cp]
+    cp = meta_ref[0, 0]
+    order = [meta_ref[0, HEAD + index] for index in range(cp_size)]
+    own_span = jnp.int32(0)
+    for index in range(cp_size):
+        own_span = jnp.where(cp == index, order[index], own_span)
     for back in range(1, keys_ref.shape[0] // BLK + 1):
         span = jnp.maximum(own_span - back, 0)
         holder = jnp.int32(0)
         for index in range(cp_size):
-            holder = jnp.where(meta_ref[HEAD + index] == span, jnp.int32(index), holder)
+            holder = jnp.where(order[index] == span, jnp.int32(index), holder)
         source, slot = locate(holder ^ cp)
         for index, ref in enumerate(sources):
 
@@ -104,10 +107,13 @@
         pl.when(count == n)(functools.partial(body, n))
 
 
-def first_kernel(cp_size, chunk, meta_ref, q_ref, own_ref, other_ref, keys_ref, values_ref, max_ref, acc_ref):
+def first_kernel(cp_size, chunk, meta_ref, q_ref, own_ref, other_ref, keys_ref, values_ref, max_ref, acc_ref, plan_ref):
     half = meta_ref[1]
     reach = keys_ref.shape[0] // BLK
     count, same = extent(meta_ref, cp_size, half, reach)
+    beyond, same = extent(meta_ref, cp_size, 1 - half, reach)
+    plan_ref[0:1, :] = jnp.full((1, HD), beyond, jnp.int32)
+    plan_ref[1:2, :] = jnp.full((1, HD), jnp.where(same, 1, 0), jnp.int32)
     swap = half == 1
     mine, other = own_ref[...], other_ref[...]
     low, high = jnp.where(swap, other, mine), jnp.where(swap, mine, other)
@@ -151,9 +157,9 @@
         attend(1, high, 0)
 
 
-def weigh_kernel(cp_size, chunk, meta_ref, q_ref, keys_ref, max_ref, acc_ref, weights_ref, rest_ref):
+def weigh_kernel(chunk, plan_ref, q_ref, keys_ref, max_ref, acc_ref, weights_ref, rest_ref):
     reach = keys_ref.shape[0] // BLK
-    count, same = extent(meta_ref, cp_size, 1 - meta_ref[1], reach)
+    count, same = plan_ref[0, 0], plan_ref[1, 0] == 1
 
     def weigh(a, n):
         for group in range(q_ref.shape[1] // (BLK * chunk)):
@@ -228,11 +234,13 @@
     groups = rows // (BLK * chunk)
     state = lambda width, dtype=jnp.float32: jax.ShapeDtypeStruct((2, rows, width), dtype)
     kernel = functools.partial(first_kernel, cp_size, chunk)
-    outs, ins = [state(HD), state(2 * HD)], [SMEM] + [VMEM] * 5
-    top, acc = local_call(kernel, "attend_first", outs, ins, 12, 1 << 31)(meta, queries, own, other, keys, values)
-    kernel = functools.partial(weigh_kernel, cp_size, chunk)
-    outs, ins = [state(reach * BLK, jnp.bfloat16), state(HD)], [SMEM] + [VMEM] * 4
-    weights, rest = local_call(kernel, "attend_weigh", outs, ins, 12, 1 << 30)(meta, queries, other_keys, top, acc)
+    outs = [state(HD), state(2 * HD), jax.ShapeDtypeStruct((8, HD), jnp.int32)]
+    ins = [SMEM] + [VMEM] * 5
+    first = local_call(kernel, "attend_first", outs, ins, 12, 1 << 31)
+    top, acc, plan = first(meta, queries, own, other, keys, values)
+    kernel = functools.partial(weigh_kernel, chunk)
+    outs, ins = [state(reach * BLK, jnp.bfloat16), state(HD)], [VMEM] * 5
+    weights, rest = local_call(kernel, "attend_weigh", outs, ins, 12, 1 << 30)(plan, queries, other_keys, top, acc)
     outs = [jax.ShapeDtypeStruct((2 * BLK, rows // BLK * HD), queries.dtype)]
     scratch = [
         pltpu.VMEM((2, groups, BLK, chunk * HD), queries.dtype),
@@ -270,8 +278,8 @@
         other = by_y(own_late)
         part = jax.ShapeDtypeStruct((reach * BLK, HD), jnp.bfloat16)
         picked = local_call(
-            functools.partial(select_kernel, cp_size), "select", [part] * 2, [SMEM] + [VMEM] * len(sources), 4, 1 << 20
-        )(meta, *sources)
+            functools.partial(select_kernel, cp_size), "select", [part] * 2, [VMEM] * (1 + len(sources)), 4, 1 << 20
+        )(meta[None], *sources)
         others = [by_y(array) for array in picked]
     else:
         pair = lax.all_gather(own, ("cp", "sp"), axis=0, tiled=True).reshape(cp_size, 2, BLK, 2, HD)

time: 29.5 us -> 29.1 us (0.986)
  Pallas kernels: 6.43 us -> 5.95 us
    pallas_call x1, Pallas kernels: 0.82 us -> 0.39 us  [shards(): local_call(functools.partial(select_kernel, cp_size), 'select', [part] *...]
  transfers between devices with their start and end apart: 12 -> 12, of which waited for: 5 -> 6; matrix products, arithmetic and copies ran while one was open for 3% -> 3% of each run, Pallas kernels for 17% -> 16%
where the time goes in v6:
time: 29.1 us; the launch traced here: 28.9 us
  starting transfers between devices  13.4 us (46%)
  waiting for transfers between devices  6.74 us (23%)
  Pallas kernels  5.95 us (20%)
  other arithmetic  1.57 us (5%)
  local copies, waits for them, and re-layouts  1.04 us (4%)
    ppermute x12, starting transfers between devices, flip(): return lax.ppermute(array, axis, [(i, i ^ mask) for i in range(size)])  13.4 us
    ppermute x12, waiting for transfers between devices, flip(): return lax.ppermute(array, axis, [(i, i ^ mask) for i in range(size)])  6.74 us
    pallas_call x1, Pallas kernels, attend(): top, acc, plan = first(meta, queries, own, other, keys, values)  2.22 us
    pallas_call x1, Pallas kernels, attend(): local_call(kernel, 'attend_weigh', outs, ins, 12, 1 << 30)  1.6 us
    pallas_call x1, Pallas kernels, attend(): return finish(weights, rest, other_values)[0]  1.42 us
    unnamed x2, local copies, waits for them, and re-layouts  1.04 us
    another operation x3, other arithmetic, shards(): line = jnp.stack([far[j] for j in group])  0.81 us
    concatenate x1, other arithmetic, shards(): meta = jnp.concatenate([jnp.stack([cp_index, half]), span_order, doc_ids])  0.75 us
  transfers between devices with their start and end apart: 12, of which 6 were waited for; matrix products, arithmetic and copies ran while one was open for 3% of the time, Pallas kernels for 16%

profile of v6, /device:TPU:0, one launch (start us, length us, event | category | flops | bytes accessed | tf_op | source)
XLA Modules:
  0.0 28.9 jit_solution(15316292256523846206)
XLA Ops:
  0.0 0.8 %fusion = (bf16[1,128,256]{2,1,0:T(8,128)(2,1)S(1)}, bf16[128,256]{1,0:T(8,128)(2,1)S(1)}) fusion(bf16[128,128]{1,0:T(8,128)(2,1)} %param.7, bf16[128,128]{1,0:T(8,128)(2,1)} %param.6), kind=kLoop, calls=%fused_computation.4 | loop fusion | flops 131072 | bytes 196608 | tf_op jit(solution)/shard_map/stack | solution.py:274
  0.8 5.1 %collective-permute-start.4 = (bf16[128,256]{1,0:T(8,128)(2,1)S(1)}, bf16[128,256]{1,0:T(8,128)(2,1)S(1)}, u32[]{:S(2)}, u32[]{:S(2)}) collective-permute-start(bf16[128,256]{1,0:T(8,128)(2,1)S(1)} %get-tuple-element.22.own_ref), channel_id=1, source_target_pairs={{0,24},{2,26},{4,28},{6,30},{8,16},{10,18},{12,20},{14,22},{16,8},... | collective-permute-start | bytes 196616 | tf_op jit(solution)/shard_map/ppermute | solution.py:21
  5.9 0.0 collective-permute-start.1
  5.9 0.6 %collective-permute-start = (bf16[128,256]{1,0:T(8,128)(2,1)S(1)}, bf16[128,256]{1,0:T(8,128)(2,1)S(1)}, u32[]{:S(2)}, u32[]{:S(2)}) collective-permute-start(bf16[128,256]{1,0:T(8,128)(2,1)S(1)} %get-tuple-element.22.own_ref), channel_id=1, source_target_pairs={{0,8},{2,10},{4,12},{6,14},{8,0},{10,2},{12,4},{14,6},{16,24},{18,... | collective-permute-start | bytes 196616 | tf_op jit(solution)/shard_map/ppermute | solution.py:21
  6.5 0.0 copy-start
  6.5 1.0 %copy-done = bf16[256,1024]{1,0:T(8,128)(2,1)S(1)} copy-done((bf16[256,1024]{1,0:T(8,128)(2,1)S(1)}, bf16[256,1024]{1,0:T(8,128)(2,1)}, u32[]{:S(2)}) %copy-start) | copy-done | bytes 524312
  7.6 0.3 %stack_queries.1.q_ref = bf16[2,1024,128]{2,1,0:T(8,128)(2,1)S(1)} custom-call(bf16[256,1024]{1,0:T(8,128)(2,1)S(1)} %copy-done), custom_call_target="tpu_custom_call" | custom-call | flops 1048576 | bytes 1048576 | tf_op jit(solution)/shard_map/stack_queries/pallas_call | solution.py:228
  7.9 0.8 %pad_add_fusion.1.meta_ref = s32[50]{0:T(128)S(1)} fusion(s32[32]{0:T(128)} %param.8, s32[16]{0:T(128)} %param.9, s32[1]{0:T(128)} %bitcast.1, s32[1]{0:T(128)} %bitcast), kind=kLoop, calls=%fused_computation.3 | loop fusion | flops 150 | bytes 400 | tf_op jit(solution)/shard_map/concatenate | solution.py:261
  8.7 0.0 collective-permute-done.4
  8.7 1.7 %collective-permute-start.5 = (bf16[2,128,256]{2,1,0:T(8,128)(2,1)S(1)}, bf16[2,128,256]{2,1,0:T(8,128)(2,1)S(1)}, u32[]{:S(2)}, u32[]{:S(2)}) collective-permute-start(bf16[2,128,256]{2,1,0:T(8,128)(2,1)S(1)} %pad_maximum_fusion.1.refs_0_), channel_id=1, source_target_pairs={{0,4},{2,6},{4,0},{6,2},{8,12},{10,14},{12,8},{14,10},{16,20},{18,... | collective-permute-start | bytes 393224 | tf_op jit(solution)/shard_map/ppermute | solution.py:21
  10.4 1.1 %collective-permute-done.1 = bf16[128,256]{1,0:T(8,128)(2,1)S(1)} collective-permute-done((bf16[128,256]{1,0:T(8,128)(2,1)S(1)}, bf16[128,256]{1,0:T(8,128)(2,1)S(1)}, u32[]{:S(2)}, u32[]{:S(2)}) %collective-permute-start.1) | collective-permute-done | bytes 65568 | tf_op jit(solution)/shard_map/ppermute | solution.py:21
  11.5 0.0 collective-permute-done
  11.5 1.6 %collective-permute-start.2 = (bf16[2,128,256]{2,1,0:T(8,128)(2,1)S(1)}, bf16[2,128,256]{2,1,0:T(8,128)(2,1)S(1)}, u32[]{:S(2)}, u32[]{:S(2)}) collective-permute-start(bf16[2,128,256]{2,1,0:T(8,128)(2,1)S(1)} %pad_maximum_fusion.refs_4_), channel_id=1, source_target_pairs={{0,4},{2,6},{4,0},{6,2},{8,12},{10,14},{12,8},{14,10},{16,20},{18,... | collective-permute-start | bytes 393224 | tf_op jit(solution)/shard_map/ppermute | solution.py:21
  13.1 0.0 collective-permute-start.6
  13.1 0.5 %collective-permute-start.8 = (bf16[2,128,256]{2,1,0:T(8,128)(2,1)S(1)}, bf16[2,128,256]{2,1,0:T(8,128)(2,1)S(1)}, u32[]{:S(2)}, u32[]{:S(2)}) collective-permute-start(bf16[2,128,256]{2,1,0:T(8,128)(2,1)S(1)} %pad_maximum_fusion.refs_4_), channel_id=1, source_target_pairs={{0,2},{2,0},{4,6},{6,4},{8,10},{10,8},{12,14},{14,12},{16,18},{18,... | collective-permute-start | bytes 393224 | tf_op jit(solution)/shard_map/ppermute | solution.py:21
  13.6 0.1 collective-permute-done.5.refs_1_
  13.7 0.0 collective-permute-start.7
  13.7 2.9 %collective-permute-done.2.refs_5_ = bf16[2,128,256]{2,1,0:T(8,128)(2,1)S(1)} collective-permute-done((bf16[2,128,256]{2,1,0:T(8,128)(2,1)S(1)}, bf16[2,128,256]{2,1,0:T(8,128)(2,1)S(1)}, u32[]{:S(2)}, u32[]{:S(2)}) %collective-permute-start.2) | collective-permute-done | bytes 131104 | tf_op jit(solution)/shard_map/ppermute | solution.py:21
  16.7 0.0 collective-permute-start.9
  16.7 1.7 %collective-permute-start.3 = (bf16[128,256]{1,0:T(8,128)(2,1)S(1)}, bf16[128,256]{1,0:T(8,128)(2,1)S(1)}, u32[]{:S(2)}, u32[]{:S(2)}) collective-permute-start(bf16[128,256]{1,0:T(8,128)(2,1)S(1)} %get-tuple-element.22.own_ref), channel_id=1, source_target_pairs={{0,1},{1,0},{2,3},{3,2},{4,5},{5,4},{6,7},{7,6},{8,9},{9,8},{10,11... | collective-permute-start | bytes 196616 | tf_op jit(solution)/shard_map/ppermute | solution.py:21
  18.4 0.0 collective-permute-done.6.refs_2_
  18.4 0.0 collective-permute-done.8.refs_6_
  18.4 0.0 collective-permute-done.7.refs_3_
  18.4 0.0 collective-permute-done.9.refs_7_
  18.4 0.4 %select.3 = (bf16[512,128]{1,0:T(8,128)(2,1)S(1)}, bf16[512,128]{1,0:T(8,128)(2,1)S(1)}) custom-call(s32[1,50]{1,0:T(1,128)S(1)} %bitcast.8, bf16[2,128,256]{2,1,0:T(8,128)(2,1)S(1)} %pad_maximum_fusion.1.refs_0_, bf16[2,128,256]{2,1,0:T(8,128)(2,1)S(1)} %collective-permute-done.5.refs_1_, bf16[2,128,256]{2,1,0:T(8,128)(2,1)S(1)} %collective-permute-done.6.refs_2_, ...), custom_call_target="tpu_custom_call" | custom-call | flops 1048576 | bytes 1048576 | tf_op jit(solution)/shard_map/select/pallas_call | solution.py:280
  18.8 1.4 %collective-permute-start.10 = (bf16[512,128]{1,0:T(8,128)(2,1)S(1)}, bf16[512,128]{1,0:T(8,128)(2,1)S(1)}, u32[]{:S(2)}, u32[]{:S(2)}) collective-permute-start(bf16[512,128]{1,0:T(8,128)(2,1)S(1)} %get-tuple-element.24.keys_ref), channel_id=1, source_target_pairs={{0,1},{1,0},{2,3},{3,2},{4,5},{5,4},{6,7},{7,6},{8,9},{9,8},{10,11... | collective-permute-start | bytes 393224 | tf_op jit(solution)/shard_map/ppermute | solution.py:21
  20.2 0.7 %collective-permute-start.11 = (bf16[512,128]{1,0:T(8,128)(2,1)S(1)}, bf16[512,128]{1,0:T(8,128)(2,1)S(1)}, u32[]{:S(2)}, u32[]{:S(2)}) collective-permute-start(bf16[512,128]{1,0:T(8,128)(2,1)S(1)} %get-tuple-element.25.values_ref), channel_id=1, source_target_pairs={{0,1},{1,0},{2,3},{3,2},{4,5},{5,4},{6,7},{7,6},{8,9},{9,8},{10,11... | collective-permute-start | bytes 393224 | tf_op jit(solution)/shard_map/ppermute | solution.py:21
  20.9 0.3 collective-permute-done.3.other_ref
  21.2 2.2 %attend_first.1 = (f32[2,1024,128]{2,1,0:T(8,128)S(1)}, f32[2,1024,256]{2,1,0:T(8,128)S(1)}, s32[8,128]{1,0:T(8,128)S(1)}) custom-call(s32[50]{0:T(128)S(1)} %pad_add_fusion.1.meta_ref, bf16[2,1024,128]{2,1,0:T(8,128)(2,1)S(1)} %stack_queries.1.q_ref, bf16[128,256]{1,0:T(8,128)(2,1)S(1)} %get-tuple-element.22.own_ref, ...), custom_call_target="tpu_custom_call" | custom-call | flops 2147483648 | bytes 1048576 | tf_op jit(solution)/shard_map/attend_first/pallas_call | solution.py:240
  23.4 1.8 %collective-permute-done.10.keys_ref = bf16[512,128]{1,0:T(8,128)(2,1)S(1)} collective-permute-done((bf16[512,128]{1,0:T(8,128)(2,1)S(1)}, bf16[512,128]{1,0:T(8,128)(2,1)S(1)}, u32[]{:S(2)}, u32[]{:S(2)}) %collective-permute-start.10) | collective-permute-done | bytes 131104 | tf_op jit(solution)/shard_map/ppermute | solution.py:21
  25.2 1.6 %attend_weigh.1 = (bf16[2,1024,512]{2,1,0:T(8,128)(2,1)S(1)}, f32[2,1024,128]{2,1,0:T(8,128)S(1)}) custom-call(s32[8,128]{1,0:T(8,128)S(1)} %get-tuple-element.26.plan_ref, bf16[2,1024,128]{2,1,0:T(8,128)(2,1)S(1)} %stack_queries.1.q_ref, bf16[512,128]{1,0:T(8,128)(2,1)S(1)} %collective-permute-done.10.keys_ref, ...), custom_call_target="tpu_custom_call" | custom-call | flops 1073741824 | bytes 1048576 | tf_op jit(solution)/shard_map/attend_weigh/pallas_call | solution.py:243
  26.8 0.5 %collective-permute-done.11.values_ref = bf16[512,128]{1,0:T(8,128)(2,1)S(1)} collective-permute-done((bf16[512,128]{1,0:T(8,128)(2,1)S(1)}, bf16[512,128]{1,0:T(8,128)(2,1)S(1)}, u32[]{:S(2)}, u32[]{:S(2)}) %collective-permute-start.11) | collective-permute-done | bytes 131104 | tf_op jit(solution)/shard_map/ppermute | solution.py:21
  27.3 1.4 %attend_finish.1 = bf16[256,1024]{1,0:T(8,128)(2,1)} custom-call(bf16[2,1024,512]{2,1,0:T(8,128)(2,1)S(1)} %get-tuple-element.29.weights_ref, f32[2,1024,128]{2,1,0:T(8,128)S(1)} %get-tuple-element.30.rest_ref, bf16[512,128]{1,0:T(8,128)(2,1)S(1)} %collective-permute-done.11.values_ref), custom_call_target="tpu_custom_call" | custom-call | flops 536870912 | bytes 1048576 | tf_op jit(solution)/shard_map/attend_finish/pallas_call | solution.py:253
  (2 shorter events, 0.0 us)
Async XLA Ops:
  0.8 7.9 %collective-permute-start.4 = (bf16[128,256]{1,0:T(8,128)(2,1)S(1)}, bf16[128,256]{1,0:T(8,128)(2,1)S(1)}, u32[]{:S(2)}, u32[]{:S(2)}) collective-permute-start(bf16[128,256]{1,0:T(8,128)(2,1)S(1)} %get-tuple-element.22.own_ref), channel_id=1, source_target_pairs={{0,24},{2,26},{4,28},{6,30},{8,16},{10,18},{12,20},{14,22},{16,8},... | collective-permute-start | bytes 196616 | tf_op jit(solution)/shard_map/ppermute | solution.py:21
  5.9 5.6 %collective-permute-start.1 = (bf16[128,256]{1,0:T(8,128)(2,1)S(1)}, bf16[128,256]{1,0:T(8,128)(2,1)S(1)}, u32[]{:S(2)}, u32[]{:S(2)}) collective-permute-start(bf16[128,256]{1,0:T(8,128)(2,1)S(1)} %get-tuple-element.22.own_ref), channel_id=1, source_target_pairs={{0,16},{2,18},{4,20},{6,22},{8,24},{10,26},{12,28},{14,30},{16,0},... | collective-permute-start | bytes 196616 | tf_op jit(solution)/shard_map/ppermute | solution.py:21
  5.9 5.6 %collective-permute-start = (bf16[128,256]{1,0:T(8,128)(2,1)S(1)}, bf16[128,256]{1,0:T(8,128)(2,1)S(1)}, u32[]{:S(2)}, u32[]{:S(2)}) collective-permute-start(bf16[128,256]{1,0:T(8,128)(2,1)S(1)} %get-tuple-element.22.own_ref), channel_id=1, source_target_pairs={{0,8},{2,10},{4,12},{6,14},{8,0},{10,2},{12,4},{14,6},{16,24},{18,... | collective-permute-start | bytes 196616 | tf_op jit(solution)/shard_map/ppermute | solution.py:21
  6.5 1.0 %copy-start = (bf16[256,1024]{1,0:T(8,128)(2,1)S(1)}, bf16[256,1024]{1,0:T(8,128)(2,1)}, u32[]{:S(2)}) copy-start(bf16[256,1024]{1,0:T(8,128)(2,1)} %q_ref.1) | copy-start | bytes 1572868
  8.7 5.0 %collective-permute-start.5 = (bf16[2,128,256]{2,1,0:T(8,128)(2,1)S(1)}, bf16[2,128,256]{2,1,0:T(8,128)(2,1)S(1)}, u32[]{:S(2)}, u32[]{:S(2)}) collective-permute-start(bf16[2,128,256]{2,1,0:T(8,128)(2,1)S(1)} %pad_maximum_fusion.1.refs_0_), channel_id=1, source_target_pairs={{0,4},{2,6},{4,0},{6,2},{8,12},{10,14},{12,8},{14,10},{16,20},{18,... | collective-permute-start | bytes 393224 | tf_op jit(solution)/shard_map/ppermute | solution.py:21
  11.5 5.1 %collective-permute-start.2 = (bf16[2,128,256]{2,1,0:T(8,128)(2,1)S(1)}, bf16[2,128,256]{2,1,0:T(8,128)(2,1)S(1)}, u32[]{:S(2)}, u32[]{:S(2)}) collective-permute-start(bf16[2,128,256]{2,1,0:T(8,128)(2,1)S(1)} %pad_maximum_fusion.refs_4_), channel_id=1, source_target_pairs={{0,4},{2,6},{4,0},{6,2},{8,12},{10,14},{12,8},{14,10},{16,20},{18,... | collective-permute-start | bytes 393224 | tf_op jit(solution)/shard_map/ppermute | solution.py:21
  13.1 5.3 %collective-permute-start.6 = (bf16[2,128,256]{2,1,0:T(8,128)(2,1)S(1)}, bf16[2,128,256]{2,1,0:T(8,128)(2,1)S(1)}, u32[]{:S(2)}, u32[]{:S(2)}) collective-permute-start(bf16[2,128,256]{2,1,0:T(8,128)(2,1)S(1)} %pad_maximum_fusion.1.refs_0_), channel_id=1, source_target_pairs={{0,2},{2,0},{4,6},{6,4},{8,10},{10,8},{12,14},{14,12},{16,18},{18,... | collective-permute-start | bytes 393224 | tf_op jit(solution)/shard_map/ppermute | solution.py:21
  13.1 5.3 %collective-permute-start.8 = (bf16[2,128,256]{2,1,0:T(8,128)(2,1)S(1)}, bf16[2,128,256]{2,1,0:T(8,128)(2,1)S(1)}, u32[]{:S(2)}, u32[]{:S(2)}) collective-permute-start(bf16[2,128,256]{2,1,0:T(8,128)(2,1)S(1)} %pad_maximum_fusion.refs_4_), channel_id=1, source_target_pairs={{0,2},{2,0},{4,6},{6,4},{8,10},{10,8},{12,14},{14,12},{16,18},{18,... | collective-permute-start | bytes 393224 | tf_op jit(solution)/shard_map/ppermute | solution.py:21
  13.7 4.7 %collective-permute-start.7 = (bf16[2,128,256]{2,1,0:T(8,128)(2,1)S(1)}, bf16[2,128,256]{2,1,0:T(8,128)(2,1)S(1)}, u32[]{:S(2)}, u32[]{:S(2)}) collective-permute-start(bf16[2,128,256]{2,1,0:T(8,128)(2,1)S(1)} %collective-permute-done.5.refs_1_), channel_id=1, source_target_pairs={{0,2},{2,0},{4,6},{6,4},{8,10},{10,8},{12,14},{14,12},{16,18},{18,... | collective-permute-start | bytes 393224 | tf_op jit(solution)/shard_map/ppermute | solution.py:21
  16.7 1.7 %collective-permute-start.9 = (bf16[2,128,256]{2,1,0:T(8,128)(2,1)S(1)}, bf16[2,128,256]{2,1,0:T(8,128)(2,1)S(1)}, u32[]{:S(2)}, u32[]{:S(2)}) collective-permute-start(bf16[2,128,256]{2,1,0:T(8,128)(2,1)S(1)} %collective-permute-done.2.refs_5_), channel_id=1, source_target_pairs={{0,2},{2,0},{4,6},{6,4},{8,10},{10,8},{12,14},{14,12},{16,18},{18,... | collective-permute-start | bytes 393224 | tf_op jit(solution)/shard_map/ppermute | solution.py:21
  16.7 4.5 %collective-permute-start.3 = (bf16[128,256]{1,0:T(8,128)(2,1)S(1)}, bf16[128,256]{1,0:T(8,128)(2,1)S(1)}, u32[]{:S(2)}, u32[]{:S(2)}) collective-permute-start(bf16[128,256]{1,0:T(8,128)(2,1)S(1)} %get-tuple-element.22.own_ref), channel_id=1, source_target_pairs={{0,1},{1,0},{2,3},{3,2},{4,5},{5,4},{6,7},{7,6},{8,9},{9,8},{10,11... | collective-permute-start | bytes 196616 | tf_op jit(solution)/shard_map/ppermute | solution.py:21
  18.8 6.4 %collective-permute-start.10 = (bf16[512,128]{1,0:T(8,128)(2,1)S(1)}, bf16[512,128]{1,0:T(8,128)(2,1)S(1)}, u32[]{:S(2)}, u32[]{:S(2)}) collective-permute-start(bf16[512,128]{1,0:T(8,128)(2,1)S(1)} %get-tuple-element.24.keys_ref), channel_id=1, source_target_pairs={{0,1},{1,0},{2,3},{3,2},{4,5},{5,4},{6,7},{7,6},{8,9},{9,8},{10,11... | collective-permute-start | bytes 393224 | tf_op jit(solution)/shard_map/ppermute | solution.py:21
  20.2 7.1 %collective-permute-start.11 = (bf16[512,128]{1,0:T(8,128)(2,1)S(1)}, bf16[512,128]{1,0:T(8,128)(2,1)S(1)}, u32[]{:S(2)}, u32[]{:S(2)}) collective-permute-start(bf16[512,128]{1,0:T(8,128)(2,1)S(1)} %get-tuple-element.25.values_ref), channel_id=1, source_target_pairs={{0,1},{1,0},{2,3},{3,2},{4,5},{5,4},{6,7},{7,6},{8,9},{9,8},{10,11... | collective-permute-start | bytes 393224 | tf_op jit(solution)/shard_map/ppermute | solution.py:21

commit v7 on v6

--- a/solution.py
+++ b/solution.py
@@ -185,23 +185,36 @@
         cases(count if a == 0 else jnp.where(same, count, 0), reach, functools.partial(weigh, a))
 
 
-def finish_kernel(chunk, weights_ref, rest_ref, values_ref, out_ref, done, sems):
+def finish_kernel(chunk, plan_ref, weights_ref, rest_ref, values_ref, out_ref, done, sems):
+    reach = values_ref.shape[0] // BLK
     groups = rest_ref.shape[1] // (BLK * chunk)
-    copies = []
-    for a in range(2):
-        for group in range(groups):
+    places = [(a, group) for a in range(2) for group in range(groups)]
+    copies = [
+        pltpu.make_async_copy(
+            done.at[a, group],
+            out_ref.at[pl.ds(a * BLK, BLK), pl.ds(group * chunk * HD, chunk * HD)],
+            sems.at[a, group],
+        )
+        for a, group in places
+    ]
+
+    def finish(pairs):
+        depth = min(2 * pairs, reach) * BLK
+        for (a, group), copy in zip(places, copies):
             at = slice(group * chunk * BLK, (group + 1) * chunk * BLK)
-            result = rest_ref[a, at] + jnp.dot(
-                weights_ref[a, at], values_ref[...], preferred_element_type=jnp.float32
-            )
+            result = rest_ref[a, at]
+            if depth:
+                result = result + jnp.dot(
+                    weights_ref[a, at, 0:depth], values_ref[0:depth, :], preferred_element_type=jnp.float32
+                )
             result = result.astype(done.dtype)
             for h in range(chunk):
                 done[a, group, :, h * HD : (h + 1) * HD] = result[h * BLK : (h + 1) * BLK]
-            place = out_ref.at[pl.ds(a * BLK, BLK), pl.ds(group * chunk * HD, chunk * HD)]
-            copies.append(pltpu.make_async_copy(done.at[a, group], place, sems.at[a, group]))
-            copies[-1].start()
-    for copy in copies:
-        copy.wait()
+            copy.start()
+        for copy in copies:
+            copy.wait()
+
+    cases((plan_ref[0, 0] + 1) // 2, (reach + 1) // 2, finish)
 
 
 VMEM = pl.BlockSpec(memory_space=pltpu.VMEM)
@@ -248,9 +261,9 @@
     ]
     kernel = functools.partial(finish_kernel, chunk)
     finish = local_call(
-        kernel, "attend_finish", outs, [VMEM] * 3, 8, 1 << 29, out_specs=[ANY], scratch_shapes=scratch
+        kernel, "attend_finish", outs, [VMEM] * 4, 8, 1 << 29, out_specs=[ANY], scratch_shapes=scratch
     )
-    return finish(weights, rest, other_values)[0]
+    return finish(plan, weights, rest, other_values)[0]
 
 
 def shards(cp_size, sp_size, queries, keys, values, doc_ids, span_order):

time: 29.1 us -> 28.9 us (level)
  Pallas kernels: 5.95 us -> 5.31 us
  waiting for transfers between devices: 6.74 us -> 7.18 us
    ppermute x12, waiting for transfers between devices: 6.74 us -> 7.18 us  [flip(): return lax.ppermute(array, axis, [(i, i ^ mask) for i in range(size)])]
  transfers between devices with their start and end apart: 12 -> 12, of which waited for: 6 -> 6; matrix products, arithmetic and copies ran while one was open for 3% -> 3% of each run, Pallas kernels for 16% -> 14%
where the time goes in v7:
time: 28.9 us; the launch traced here: 28.7 us
  starting transfers between devices  13.4 us (46%)
  waiting for transfers between devices  7.18 us (25%)
  Pallas kernels  5.31 us (18%)
  other arithmetic  1.57 us (5%)
  local copies, waits for them, and re-layouts  1.04 us (4%)
    ppermute x12, starting transfers between devices, flip(): return lax.ppermute(array, axis, [(i, i ^ mask) for i in range(size)])  13.4 us
    ppermute x12, waiting for transfers between devices, flip(): return lax.ppermute(array, axis, [(i, i ^ mask) for i in range(size)])  7.18 us
    pallas_call x1, Pallas kernels, attend(): top, acc, plan = first(meta, queries, own, other, keys, values)  1.99 us
    pallas_call x1, Pallas kernels, attend(): local_call(kernel, 'attend_weigh', outs, ins, 12, 1 << 30)  1.38 us
    pallas_call x1, Pallas kernels, attend(): return finish(plan, weights, rest, other_values)[0]  1.23 us
    unnamed x2, local copies, waits for them, and re-layouts  1.04 us
    another operation x3, other arithmetic, shards(): line = jnp.stack([far[j] for j in group])  0.81 us
    concatenate x1, other arithmetic, shards(): meta = jnp.concatenate([jnp.stack([cp_index, half]), span_order, doc_ids])  0.75 us
  transfers between devices with their start and end apart: 12, of which 6 were waited for; matrix products, arithmetic and copies ran while one was open for 3% of the time, Pallas kernels for 14%

profile of v7, /device:TPU:0, one launch (start us, length us, event | category | flops | bytes accessed | tf_op | source)
XLA Modules:
  0.0 28.7 jit_solution(10570827491869649579)
XLA Ops:
  0.0 0.8 %fusion = (bf16[1,128,256]{2,1,0:T(8,128)(2,1)S(1)}, bf16[128,256]{1,0:T(8,128)(2,1)S(1)}) fusion(bf16[128,128]{1,0:T(8,128)(2,1)} %param.7, bf16[128,128]{1,0:T(8,128)(2,1)} %param.6), kind=kLoop, calls=%fused_computation.4 | loop fusion | flops 131072 | bytes 196608 | tf_op jit(solution)/shard_map/stack | solution.py:287
  0.8 5.1 %collective-permute-start.4 = (bf16[128,256]{1,0:T(8,128)(2,1)S(1)}, bf16[128,256]{1,0:T(8,128)(2,1)S(1)}, u32[]{:S(2)}, u32[]{:S(2)}) collective-permute-start(bf16[128,256]{1,0:T(8,128)(2,1)S(1)} %get-tuple-element.22.own_ref), channel_id=1, source_target_pairs={{0,24},{2,26},{4,28},{6,30},{8,16},{10,18},{12,20},{14,22},{16,8},... | collective-permute-start | bytes 196616 | tf_op jit(solution)/shard_map/ppermute | solution.py:21
  5.9 0.0 collective-permute-start.1
  5.9 0.6 %collective-permute-start = (bf16[128,256]{1,0:T(8,128)(2,1)S(1)}, bf16[128,256]{1,0:T(8,128)(2,1)S(1)}, u32[]{:S(2)}, u32[]{:S(2)}) collective-permute-start(bf16[128,256]{1,0:T(8,128)(2,1)S(1)} %get-tuple-element.22.own_ref), channel_id=1, source_target_pairs={{0,8},{2,10},{4,12},{6,14},{8,0},{10,2},{12,4},{14,6},{16,24},{18,... | collective-permute-start | bytes 196616 | tf_op jit(solution)/shard_map/ppermute | solution.py:21
  6.5 0.0 copy-start
  6.5 1.0 %copy-done = bf16[256,1024]{1,0:T(8,128)(2,1)S(1)} copy-done((bf16[256,1024]{1,0:T(8,128)(2,1)S(1)}, bf16[256,1024]{1,0:T(8,128)(2,1)}, u32[]{:S(2)}) %copy-start) | copy-done | bytes 524312
  7.6 0.3 %stack_queries.1.q_ref = bf16[2,1024,128]{2,1,0:T(8,128)(2,1)S(1)} custom-call(bf16[256,1024]{1,0:T(8,128)(2,1)S(1)} %copy-done), custom_call_target="tpu_custom_call" | custom-call | flops 1048576 | bytes 1048576 | tf_op jit(solution)/shard_map/stack_queries/pallas_call | solution.py:241
  7.9 0.8 %pad_add_fusion.1.meta_ref = s32[50]{0:T(128)S(1)} fusion(s32[32]{0:T(128)} %param.8, s32[16]{0:T(128)} %param.9, s32[1]{0:T(128)} %bitcast.1, s32[1]{0:T(128)} %bitcast), kind=kLoop, calls=%fused_computation.3 | loop fusion | flops 150 | bytes 400 | tf_op jit(solution)/shard_map/concatenate | solution.py:274
  8.7 0.0 collective-permute-done.4
  8.7 1.7 %collective-permute-start.5 = (bf16[2,128,256]{2,1,0:T(8,128)(2,1)S(1)}, bf16[2,128,256]{2,1,0:T(8,128)(2,1)S(1)}, u32[]{:S(2)}, u32[]{:S(2)}) collective-permute-start(bf16[2,128,256]{2,1,0:T(8,128)(2,1)S(1)} %pad_maximum_fusion.1.refs_0_), channel_id=1, source_target_pairs={{0,4},{2,6},{4,0},{6,2},{8,12},{10,14},{12,8},{14,10},{16,20},{18,... | collective-permute-start | bytes 393224 | tf_op jit(solution)/shard_map/ppermute | solution.py:21
  10.4 1.1 %collective-permute-done.1 = bf16[128,256]{1,0:T(8,128)(2,1)S(1)} collective-permute-done((bf16[128,256]{1,0:T(8,128)(2,1)S(1)}, bf16[128,256]{1,0:T(8,128)(2,1)S(1)}, u32[]{:S(2)}, u32[]{:S(2)}) %collective-permute-start.1) | collective-permute-done | bytes 65568 | tf_op jit(solution)/shard_map/ppermute | solution.py:21
  11.5 0.0 collective-permute-done
  11.5 1.6 %collective-permute-start.2 = (bf16[2,128,256]{2,1,0:T(8,128)(2,1)S(1)}, bf16[2,128,256]{2,1,0:T(8,128)(2,1)S(1)}, u32[]{:S(2)}, u32[]{:S(2)}) collective-permute-start(bf16[2,128,256]{2,1,0:T(8,128)(2,1)S(1)} %pad_maximum_fusion.refs_4_), channel_id=1, source_target_pairs={{0,4},{2,6},{4,0},{6,2},{8,12},{10,14},{12,8},{14,10},{16,20},{18,... | collective-permute-start | bytes 393224 | tf_op jit(solution)/shard_map/ppermute | solution.py:21
  13.1 0.0 collective-permute-start.6
  13.1 0.5 %collective-permute-start.8 = (bf16[2,128,256]{2,1,0:T(8,128)(2,1)S(1)}, bf16[2,128,256]{2,1,0:T(8,128)(2,1)S(1)}, u32[]{:S(2)}, u32[]{:S(2)}) collective-permute-start(bf16[2,128,256]{2,1,0:T(8,128)(2,1)S(1)} %pad_maximum_fusion.refs_4_), channel_id=1, source_target_pairs={{0,2},{2,0},{4,6},{6,4},{8,10},{10,8},{12,14},{14,12},{16,18},{18,... | collective-permute-start | bytes 393224 | tf_op jit(solution)/shard_map/ppermute | solution.py:21
  13.6 0.1 collective-permute-done.5.refs_1_
  13.7 0.0 collective-permute-start.7
  13.7 2.9 %collective-permute-done.2.refs_5_ = bf16[2,128,256]{2,1,0:T(8,128)(2,1)S(1)} collective-permute-done((bf16[2,128,256]{2,1,0:T(8,128)(2,1)S(1)}, bf16[2,128,256]{2,1,0:T(8,128)(2,1)S(1)}, u32[]{:S(2)}, u32[]{:S(2)}) %collective-permute-start.2) | collective-permute-done | bytes 131104 | tf_op jit(solution)/shard_map/ppermute | solution.py:21
  16.7 0.0 collective-permute-start.9
  16.7 1.7 %collective-permute-start.3 = (bf16[128,256]{1,0:T(8,128)(2,1)S(1)}, bf16[128,256]{1,0:T(8,128)(2,1)S(1)}, u32[]{:S(2)}, u32[]{:S(2)}) collective-permute-start(bf16[128,256]{1,0:T(8,128)(2,1)S(1)} %get-tuple-element.22.own_ref), channel_id=1, source_target_pairs={{0,1},{1,0},{2,3},{3,2},{4,5},{5,4},{6,7},{7,6},{8,9},{9,8},{10,11... | collective-permute-start | bytes 196616 | tf_op jit(solution)/shard_map/ppermute | solution.py:21
  18.4 0.0 collective-permute-done.6.refs_2_
  18.4 0.0 collective-permute-done.8.refs_6_
  18.4 0.0 collective-permute-done.7.refs_3_
  18.4 0.0 collective-permute-done.9.refs_7_
  18.4 0.4 %select.3 = (bf16[512,128]{1,0:T(8,128)(2,1)S(1)}, bf16[512,128]{1,0:T(8,128)(2,1)S(1)}) custom-call(s32[1,50]{1,0:T(1,128)S(1)} %bitcast.8, bf16[2,128,256]{2,1,0:T(8,128)(2,1)S(1)} %pad_maximum_fusion.1.refs_0_, bf16[2,128,256]{2,1,0:T(8,128)(2,1)S(1)} %collective-permute-done.5.refs_1_, bf16[2,128,256]{2,1,0:T(8,128)(2,1)S(1)} %collective-permute-done.6.refs_2_, ...), custom_call_target="tpu_custom_call" | custom-call | flops 1048576 | bytes 1048576 | tf_op jit(solution)/shard_map/select/pallas_call | solution.py:293
  18.8 1.4 %collective-permute-start.10 = (bf16[512,128]{1,0:T(8,128)(2,1)S(1)}, bf16[512,128]{1,0:T(8,128)(2,1)S(1)}, u32[]{:S(2)}, u32[]{:S(2)}) collective-permute-start(bf16[512,128]{1,0:T(8,128)(2,1)S(1)} %get-tuple-element.24.keys_ref), channel_id=1, source_target_pairs={{0,1},{1,0},{2,3},{3,2},{4,5},{5,4},{6,7},{7,6},{8,9},{9,8},{10,11... | collective-permute-start | bytes 393224 | tf_op jit(solution)/shard_map/ppermute | solution.py:21
  20.2 0.7 %collective-permute-start.11 = (bf16[512,128]{1,0:T(8,128)(2,1)S(1)}, bf16[512,128]{1,0:T(8,128)(2,1)S(1)}, u32[]{:S(2)}, u32[]{:S(2)}) collective-permute-start(bf16[512,128]{1,0:T(8,128)(2,1)S(1)} %get-tuple-element.25.values_ref), channel_id=1, source_target_pairs={{0,1},{1,0},{2,3},{3,2},{4,5},{5,4},{6,7},{7,6},{8,9},{9,8},{10,11... | collective-permute-start | bytes 393224 | tf_op jit(solution)/shard_map/ppermute | solution.py:21
  20.9 0.3 %collective-permute-done.3.other_ref = bf16[128,256]{1,0:T(8,128)(2,1)S(1)} collective-permute-done((bf16[128,256]{1,0:T(8,128)(2,1)S(1)}, bf16[128,256]{1,0:T(8,128)(2,1)S(1)}, u32[]{:S(2)}, u32[]{:S(2)}) %collective-permute-start.3) | collective-permute-done | bytes 65568 | tf_op jit(solution)/shard_map/ppermute | solution.py:21
  21.2 2.0 %attend_first.1 = (f32[2,1024,128]{2,1,0:T(8,128)S(1)}, f32[2,1024,256]{2,1,0:T(8,128)S(1)}, s32[8,128]{1,0:T(8,128)S(1)}) custom-call(s32[50]{0:T(128)S(1)} %pad_add_fusion.1.meta_ref, bf16[2,1024,128]{2,1,0:T(8,128)(2,1)S(1)} %stack_queries.1.q_ref, bf16[128,256]{1,0:T(8,128)(2,1)S(1)} %get-tuple-element.22.own_ref, ...), custom_call_target="tpu_custom_call" | custom-call | flops 2147483648 | bytes 1048576 | tf_op jit(solution)/shard_map/attend_first/pallas_call | solution.py:253
  23.2 2.0 %collective-permute-done.10.keys_ref = bf16[512,128]{1,0:T(8,128)(2,1)S(1)} collective-permute-done((bf16[512,128]{1,0:T(8,128)(2,1)S(1)}, bf16[512,128]{1,0:T(8,128)(2,1)S(1)}, u32[]{:S(2)}, u32[]{:S(2)}) %collective-permute-start.10) | collective-permute-done | bytes 131104 | tf_op jit(solution)/shard_map/ppermute | solution.py:21
  25.2 1.4 %attend_weigh.1 = (bf16[2,1024,512]{2,1,0:T(8,128)(2,1)S(1)}, f32[2,1024,128]{2,1,0:T(8,128)S(1)}) custom-call(s32[8,128]{1,0:T(8,128)S(1)} %get-tuple-element.26.plan_ref, bf16[2,1024,128]{2,1,0:T(8,128)(2,1)S(1)} %stack_queries.1.q_ref, bf16[512,128]{1,0:T(8,128)(2,1)S(1)} %collective-permute-done.10.keys_ref, ...), custom_call_target="tpu_custom_call" | custom-call | flops 1073741824 | bytes 1048576 | tf_op jit(solution)/shard_map/attend_weigh/pallas_call | solution.py:256
  26.6 0.7 %collective-permute-done.11.values_ref = bf16[512,128]{1,0:T(8,128)(2,1)S(1)} collective-permute-done((bf16[512,128]{1,0:T(8,128)(2,1)S(1)}, bf16[512,128]{1,0:T(8,128)(2,1)S(1)}, u32[]{:S(2)}, u32[]{:S(2)}) %collective-permute-start.11) | collective-permute-done | bytes 131104 | tf_op jit(solution)/shard_map/ppermute | solution.py:21
  27.3 1.2 %attend_finish.1 = bf16[256,1024]{1,0:T(8,128)(2,1)} custom-call(s32[8,128]{1,0:T(8,128)S(1)} %get-tuple-element.26.plan_ref, bf16[2,1024,512]{2,1,0:T(8,128)(2,1)S(1)} %get-tuple-element.29.weights_ref, f32[2,1024,128]{2,1,0:T(8,128)S(1)} %get-tuple-element.30.rest_ref, bf16[512,128]{1,0:T(8,128)(2,1)S(1)} %collective-permute-done.11.values_ref), custom_call_target="tpu_custom_call" | custom-call | flops 536870912 | bytes 1048576 | tf_op jit(solution)/shard_map/attend_finish/pallas_call | solution.py:266
  (2 shorter events, 0.0 us)
Async XLA Ops:
  0.8 7.9 %collective-permute-start.4 = (bf16[128,256]{1,0:T(8,128)(2,1)S(1)}, bf16[128,256]{1,0:T(8,128)(2,1)S(1)}, u32[]{:S(2)}, u32[]{:S(2)}) collective-permute-start(bf16[128,256]{1,0:T(8,128)(2,1)S(1)} %get-tuple-element.22.own_ref), channel_id=1, source_target_pairs={{0,24},{2,26},{4,28},{6,30},{8,16},{10,18},{12,20},{14,22},{16,8},... | collective-permute-start | bytes 196616 | tf_op jit(solution)/shard_map/ppermute | solution.py:21
  5.9 5.6 %collective-permute-start.1 = (bf16[128,256]{1,0:T(8,128)(2,1)S(1)}, bf16[128,256]{1,0:T(8,128)(2,1)S(1)}, u32[]{:S(2)}, u32[]{:S(2)}) collective-permute-start(bf16[128,256]{1,0:T(8,128)(2,1)S(1)} %get-tuple-element.22.own_ref), channel_id=1, source_target_pairs={{0,16},{2,18},{4,20},{6,22},{8,24},{10,26},{12,28},{14,30},{16,0},... | collective-permute-start | bytes 196616 | tf_op jit(solution)/shard_map/ppermute | solution.py:21
  5.9 5.6 %collective-permute-start = (bf16[128,256]{1,0:T(8,128)(2,1)S(1)}, bf16[128,256]{1,0:T(8,128)(2,1)S(1)}, u32[]{:S(2)}, u32[]{:S(2)}) collective-permute-start(bf16[128,256]{1,0:T(8,128)(2,1)S(1)} %get-tuple-element.22.own_ref), channel_id=1, source_target_pairs={{0,8},{2,10},{4,12},{6,14},{8,0},{10,2},{12,4},{14,6},{16,24},{18,... | collective-permute-start | bytes 196616 | tf_op jit(solution)/shard_map/ppermute | solution.py:21
  6.5 1.0 %copy-start = (bf16[256,1024]{1,0:T(8,128)(2,1)S(1)}, bf16[256,1024]{1,0:T(8,128)(2,1)}, u32[]{:S(2)}) copy-start(bf16[256,1024]{1,0:T(8,128)(2,1)} %q_ref.1) | copy-start | bytes 1572868
  8.7 5.0 %collective-permute-start.5 = (bf16[2,128,256]{2,1,0:T(8,128)(2,1)S(1)}, bf16[2,128,256]{2,1,0:T(8,128)(2,1)S(1)}, u32[]{:S(2)}, u32[]{:S(2)}) collective-permute-start(bf16[2,128,256]{2,1,0:T(8,128)(2,1)S(1)} %pad_maximum_fusion.1.refs_0_), channel_id=1, source_target_pairs={{0,4},{2,6},{4,0},{6,2},{8,12},{10,14},{12,8},{14,10},{16,20},{18,... | collective-permute-start | bytes 393224 | tf_op jit(solution)/shard_map/ppermute | solution.py:21
  11.5 5.1 %collective-permute-start.2 = (bf16[2,128,256]{2,1,0:T(8,128)(2,1)S(1)}, bf16[2,128,256]{2,1,0:T(8,128)(2,1)S(1)}, u32[]{:S(2)}, u32[]{:S(2)}) collective-permute-start(bf16[2,128,256]{2,1,0:T(8,128)(2,1)S(1)} %pad_maximum_fusion.refs_4_), channel_id=1, source_target_pairs={{0,4},{2,6},{4,0},{6,2},{8,12},{10,14},{12,8},{14,10},{16,20},{18,... | collective-permute-start | bytes 393224 | tf_op jit(solution)/shard_map/ppermute | solution.py:21
  13.1 5.3 %collective-permute-start.6 = (bf16[2,128,256]{2,1,0:T(8,128)(2,1)S(1)}, bf16[2,128,256]{2,1,0:T(8,128)(2,1)S(1)}, u32[]{:S(2)}, u32[]{:S(2)}) collective-permute-start(bf16[2,128,256]{2,1,0:T(8,128)(2,1)S(1)} %pad_maximum_fusion.1.refs_0_), channel_id=1, source_target_pairs={{0,2},{2,0},{4,6},{6,4},{8,10},{10,8},{12,14},{14,12},{16,18},{18,... | collective-permute-start | bytes 393224 | tf_op jit(solution)/shard_map/ppermute | solution.py:21
  13.1 5.3 %collective-permute-start.8 = (bf16[2,128,256]{2,1,0:T(8,128)(2,1)S(1)}, bf16[2,128,256]{2,1,0:T(8,128)(2,1)S(1)}, u32[]{:S(2)}, u32[]{:S(2)}) collective-permute-start(bf16[2,128,256]{2,1,0:T(8,128)(2,1)S(1)} %pad_maximum_fusion.refs_4_), channel_id=1, source_target_pairs={{0,2},{2,0},{4,6},{6,4},{8,10},{10,8},{12,14},{14,12},{16,18},{18,... | collective-permute-start | bytes 393224 | tf_op jit(solution)/shard_map/ppermute | solution.py:21
  13.7 4.7 %collective-permute-start.7 = (bf16[2,128,256]{2,1,0:T(8,128)(2,1)S(1)}, bf16[2,128,256]{2,1,0:T(8,128)(2,1)S(1)}, u32[]{:S(2)}, u32[]{:S(2)}) collective-permute-start(bf16[2,128,256]{2,1,0:T(8,128)(2,1)S(1)} %collective-permute-done.5.refs_1_), channel_id=1, source_target_pairs={{0,2},{2,0},{4,6},{6,4},{8,10},{10,8},{12,14},{14,12},{16,18},{18,... | collective-permute-start | bytes 393224 | tf_op jit(solution)/shard_map/ppermute | solution.py:21
  16.7 1.7 %collective-permute-start.9 = (bf16[2,128,256]{2,1,0:T(8,128)(2,1)S(1)}, bf16[2,128,256]{2,1,0:T(8,128)(2,1)S(1)}, u32[]{:S(2)}, u32[]{:S(2)}) collective-permute-start(bf16[2,128,256]{2,1,0:T(8,128)(2,1)S(1)} %collective-permute-done.2.refs_5_), channel_id=1, source_target_pairs={{0,2},{2,0},{4,6},{6,4},{8,10},{10,8},{12,14},{14,12},{16,18},{18,... | collective-permute-start | bytes 393224 | tf_op jit(solution)/shard_map/ppermute | solution.py:21
  16.7 4.5 %collective-permute-start.3 = (bf16[128,256]{1,0:T(8,128)(2,1)S(1)}, bf16[128,256]{1,0:T(8,128)(2,1)S(1)}, u32[]{:S(2)}, u32[]{:S(2)}) collective-permute-start(bf16[128,256]{1,0:T(8,128)(2,1)S(1)} %get-tuple-element.22.own_ref), channel_id=1, source_target_pairs={{0,1},{1,0},{2,3},{3,2},{4,5},{5,4},{6,7},{7,6},{8,9},{9,8},{10,11... | collective-permute-start | bytes 196616 | tf_op jit(solution)/shard_map/ppermute | solution.py:21
  18.8 6.4 %collective-permute-start.10 = (bf16[512,128]{1,0:T(8,128)(2,1)S(1)}, bf16[512,128]{1,0:T(8,128)(2,1)S(1)}, u32[]{:S(2)}, u32[]{:S(2)}) collective-permute-start(bf16[512,128]{1,0:T(8,128)(2,1)S(1)} %get-tuple-element.24.keys_ref), channel_id=1, source_target_pairs={{0,1},{1,0},{2,3},{3,2},{4,5},{5,4},{6,7},{7,6},{8,9},{9,8},{10,11... | collective-permute-start | bytes 393224 | tf_op jit(solution)/shard_map/ppermute | solution.py:21
  20.2 7.1 %collective-permute-start.11 = (bf16[512,128]{1,0:T(8,128)(2,1)S(1)}, bf16[512,128]{1,0:T(8,128)(2,1)S(1)}, u32[]{:S(2)}, u32[]{:S(2)}) collective-permute-start(bf16[512,128]{1,0:T(8,128)(2,1)S(1)} %get-tuple-element.25.values_ref), channel_id=1, source_target_pairs={{0,1},{1,0},{2,3},{3,2},{4,5},{5,4},{6,7},{7,6},{8,9},{9,8},{10,11... | collective-permute-start | bytes 393224 | tf_op jit(solution)/shard_map/ppermute | solution.py:21

commit v8 on v7

--- a/solution.py
+++ b/solution.py
@@ -27,26 +27,17 @@
     return group * 4 + (apart & 1) * 2 + ((apart >> 1) & 1), 1 - (line & 1)
 
 
-def select_kernel(cp_size, meta_ref, *refs):
+def select_kernel(code_ref, *refs):
     sources, (keys_ref, values_ref) = refs[:-2], refs[-2:]
-    cp = meta_ref[0, 0]
-    order = [meta_ref[0, HEAD + index] for index in range(cp_size)]
-    own_span = jnp.int32(0)
-    for index in range(cp_size):
-        own_span = jnp.where(cp == index, order[index], own_span)
-    for back in range(1, keys_ref.shape[0] // BLK + 1):
-        span = jnp.maximum(own_span - back, 0)
-        holder = jnp.int32(0)
-        for index in range(cp_size):
-            holder = jnp.where(order[index] == span, jnp.int32(index), holder)
-        source, slot = locate(holder ^ cp)
-        for index, ref in enumerate(sources):
-
-            @pl.when(source == index)
+    for index in range(keys_ref.shape[0] // BLK):
+        rows = slice(index * BLK, (index + 1) * BLK)
+        code = code_ref[index, 0]
+        for number, source in enumerate(sources):
+
+            @pl.when((code >> 1) == number)
             def _():
-                rows = slice((back - 1) * BLK, back * BLK)
-                keys_ref[rows, :] = ref[slot, :, 0:HD]
-                values_ref[rows, :] = ref[slot, :, HD:]
+                keys_ref[rows, :] = source[code & 1, :, 0:HD]
+                values_ref[rows, :] = source[code & 1, :, HD:]
 
 
 def extent(meta_ref, cp_size, half, reach):
@@ -61,7 +52,7 @@
     return count, doc == meta_ref[doc_at + 2 * span + 1]
 
 
-def stack_kernel(q_ref, out_ref, sems):
+def stack_kernel(cp_size, reach, meta_ref, q_ref, out_ref, code_ref, sems):
     heads = out_ref.shape[1] // BLK
     copies = [
         pltpu.make_async_copy(
@@ -72,6 +63,18 @@
     ]
     for copy in copies:
         copy.start()
+    cp = meta_ref[0, 0]
+    order = [meta_ref[0, HEAD + index] for index in range(cp_size)]
+    own_span = jnp.int32(0)
+    for index in range(cp_size):
+        own_span = jnp.where(cp == index, order[index], own_span)
+    for back in range(1, reach + 1):
+        span = jnp.maximum(own_span - back, 0)
+        holder = jnp.int32(0)
+        for index in range(cp_size):
+            holder = jnp.where(order[index] == span, jnp.int32(index), holder)
+        source, slot = locate(holder ^ cp)
+        code_ref[back - 1 : back, :] = jnp.full((1, HD), source * 2 + slot, jnp.int32)
     for copy in copies:
         copy.wait()
 
@@ -234,11 +237,15 @@
     )
 
 
-def stack_queries(queries):
+def stack_queries(cp_size, reach, meta, queries):
     heads = queries.shape[1] // HD
-    outs = [jax.ShapeDtypeStruct((2, heads * BLK, HD), queries.dtype)]
+    outs = [
+        jax.ShapeDtypeStruct((2, heads * BLK, HD), queries.dtype),
+        jax.ShapeDtypeStruct(((reach + 7) // 8 * 8, HD), jnp.int32),
+    ]
     scratch = [pltpu.SemaphoreType.DMA((2, heads))]
-    return local_call(stack_kernel, "stack_queries", outs, [ANY], 4, 1 << 20, scratch_shapes=scratch)(queries)[0]
+    kernel = functools.partial(stack_kernel, cp_size, reach)
+    return local_call(kernel, "stack_queries", outs, [VMEM, ANY], 4, 1 << 20, scratch_shapes=scratch)(meta[None], queries)
 
 
 def attend(cp_size, meta, queries, own, other, keys, values, other_keys, other_values):
@@ -274,7 +281,7 @@
     meta = jnp.concatenate([jnp.stack([cp_index, half]), span_order, doc_ids])
     own = lax.pad(keys, jnp.bfloat16(0), ((0, 0, 0), (0, HD, 0)))
     own = own + lax.pad(values, jnp.bfloat16(0), ((0, 0, 0), (HD, 0, 0)))
-    queries = stack_queries(queries)
+    queries, codes = stack_queries(cp_size, reach, meta, queries)
     if staged:
         by_x = lambda array: flip(array, "cp", cp_size, 2)
         by_y = lambda array: flip(array, "sp", sp_size, 1)
@@ -291,8 +298,8 @@
         other = by_y(own_late)
         part = jax.ShapeDtypeStruct((reach * BLK, HD), jnp.bfloat16)
         picked = local_call(
-            functools.partial(select_kernel, cp_size), "select", [part] * 2, [VMEM] * (1 + len(sources)), 4, 1 << 20
-        )(meta[None], *sources)
+            select_kernel, "select", [part] * 2, [VMEM] * (1 + len(sources)), 4, 1 << 20
+        )(codes, *sources)
         others = [by_y(array) for array in picked]
     else:
         pair = lax.all_gather(own, ("cp", "sp"), axis=0, tiled=True).reshape(cp_size, 2, BLK, 2, HD)

time: 28.9 us -> 29 us (level)
  Pallas kernels: 5.31 us -> 5.88 us
  waiting for transfers between devices: 7.18 us -> 6.87 us
    pallas_call x1, Pallas kernels: 1.99 us -> 2.42 us  [attend(): top, acc, plan = first(meta, queries, own, other, keys, values)]
    ppermute x12, waiting for transfers between devices: 7.18 us -> 6.87 us  [flip(): return lax.ppermute(array, axis, [(i, i ^ mask) for i in range(size)])]
  transfers between devices with their start and end apart: 12 -> 12, of which waited for: 6 -> 6; matrix products, arithmetic and copies ran while one was open for 3% -> 3% of each run, Pallas kernels for 14% -> 15%
where the time goes in v8:
time: 29 us; the launch traced here: 28.9 us
  starting transfers between devices  13.3 us (46%)
  waiting for transfers between devices  6.87 us (24%)
  Pallas kernels  5.88 us (20%)
  other arithmetic  1.56 us (5%)
  local copies, waits for them, and re-layouts  1.04 us (4%)
    ppermute x12, starting transfers between devices, flip(): return lax.ppermute(array, axis, [(i, i ^ mask) for i in range(size)])  13.3 us
    ppermute x12, waiting for transfers between devices, flip(): return lax.ppermute(array, axis, [(i, i ^ mask) for i in range(size)])  6.87 us
    pallas_call x1, Pallas kernels, attend(): top, acc, plan = first(meta, queries, own, other, keys, values)  2.42 us
    pallas_call x1, Pallas kernels, attend(): return finish(plan, weights, rest, other_values)[0]  1.45 us
    pallas_call x1, Pallas kernels, attend(): local_call(kernel, 'attend_weigh', outs, ins, 12, 1 << 30)  1.17 us
    unnamed x2, local copies, waits for them, and re-layouts  1.04 us
    another operation x3, other arithmetic, shards(): line = jnp.stack([far[j] for j in group])  0.81 us
    concatenate x1, other arithmetic, shards(): meta = jnp.concatenate([jnp.stack([cp_index, half]), span_order, doc_ids])  0.75 us
  transfers between devices with their start and end apart: 12, of which 6 were waited for; matrix products, arithmetic and copies ran while one was open for 3% of the time, Pallas kernels for 15%

profile of v8, /device:TPU:0, one launch (start us, length us, event | category | flops | bytes accessed | tf_op | source)
XLA Modules:
  0.0 28.9 jit_solution(15969080373773335230)
XLA Ops:
  0.0 0.8 %fusion = (bf16[1,128,256]{2,1,0:T(8,128)(2,1)S(1)}, bf16[128,256]{1,0:T(8,128)(2,1)S(1)}) fusion(bf16[128,128]{1,0:T(8,128)(2,1)} %param.7, bf16[128,128]{1,0:T(8,128)(2,1)} %param.6), kind=kLoop, calls=%fused_computation.4 | loop fusion | flops 131072 | bytes 196608 | tf_op jit(solution)/shard_map/stack | solution.py:294
  0.8 5.1 %collective-permute-start.4 = (bf16[128,256]{1,0:T(8,128)(2,1)S(1)}, bf16[128,256]{1,0:T(8,128)(2,1)S(1)}, u32[]{:S(2)}, u32[]{:S(2)}) collective-permute-start(bf16[128,256]{1,0:T(8,128)(2,1)S(1)} %get-tuple-element.25.own_ref), channel_id=1, source_target_pairs={{0,24},{2,26},{4,28},{6,30},{8,16},{10,18},{12,20},{14,22},{16,8},... | collective-permute-start | bytes 196616 | tf_op jit(solution)/shard_map/ppermute | solution.py:21
  5.9 0.0 collective-permute-start.1
  5.9 0.6 %collective-permute-start = (bf16[128,256]{1,0:T(8,128)(2,1)S(1)}, bf16[128,256]{1,0:T(8,128)(2,1)S(1)}, u32[]{:S(2)}, u32[]{:S(2)}) collective-permute-start(bf16[128,256]{1,0:T(8,128)(2,1)S(1)} %get-tuple-element.25.own_ref), channel_id=1, source_target_pairs={{0,8},{2,10},{4,12},{6,14},{8,0},{10,2},{12,4},{14,6},{16,24},{18,... | collective-permute-start | bytes 196616 | tf_op jit(solution)/shard_map/ppermute | solution.py:21
  6.5 0.7 %pad_add_fusion.1.meta_ref = s32[50]{0:T(128)S(1)} fusion(s32[32]{0:T(128)} %param.8, s32[16]{0:T(128)} %param.9, s32[1]{0:T(128)} %bitcast.1, s32[1]{0:T(128)} %bitcast), kind=kLoop, calls=%fused_computation.3 | loop fusion | flops 150 | bytes 400 | tf_op jit(solution)/shard_map/concatenate | solution.py:281
  7.3 0.0 copy-start
  7.3 1.0 %copy-done = bf16[256,1024]{1,0:T(8,128)(2,1)S(1)} copy-done((bf16[256,1024]{1,0:T(8,128)(2,1)S(1)}, bf16[256,1024]{1,0:T(8,128)(2,1)}, u32[]{:S(2)}) %copy-start) | copy-done | bytes 524312
  8.3 0.5 %stack_queries.1 = (bf16[2,1024,128]{2,1,0:T(8,128)(2,1)S(1)}, s32[8,128]{1,0:T(8,128)S(1)}) custom-call(s32[1,50]{1,0:T(1,128)S(1)} %bitcast.8, bf16[256,1024]{1,0:T(8,128)(2,1)S(1)} %copy-done), custom_call_target="tpu_custom_call" | custom-call | flops 1048576 | bytes 1048576 | tf_op jit(solution)/shard_map/stack_queries/pallas_call | solution.py:248
  8.8 0.0 collective-permute-done.4
  8.9 1.7 %collective-permute-start.5 = (bf16[2,128,256]{2,1,0:T(8,128)(2,1)S(1)}, bf16[2,128,256]{2,1,0:T(8,128)(2,1)S(1)}, u32[]{:S(2)}, u32[]{:S(2)}) collective-permute-start(bf16[2,128,256]{2,1,0:T(8,128)(2,1)S(1)} %pad_maximum_fusion.1.refs_0_), channel_id=1, source_target_pairs={{0,4},{2,6},{4,0},{6,2},{8,12},{10,14},{12,8},{14,10},{16,20},{18,... | collective-permute-start | bytes 393224 | tf_op jit(solution)/shard_map/ppermute | solution.py:21
  10.6 0.9 %collective-permute-done.1 = bf16[128,256]{1,0:T(8,128)(2,1)S(1)} collective-permute-done((bf16[128,256]{1,0:T(8,128)(2,1)S(1)}, bf16[128,256]{1,0:T(8,128)(2,1)S(1)}, u32[]{:S(2)}, u32[]{:S(2)}) %collective-permute-start.1) | collective-permute-done | bytes 65568 | tf_op jit(solution)/shard_map/ppermute | solution.py:21
  11.5 0.0 collective-permute-done
  11.5 1.6 %collective-permute-start.2 = (bf16[2,128,256]{2,1,0:T(8,128)(2,1)S(1)}, bf16[2,128,256]{2,1,0:T(8,128)(2,1)S(1)}, u32[]{:S(2)}, u32[]{:S(2)}) collective-permute-start(bf16[2,128,256]{2,1,0:T(8,128)(2,1)S(1)} %pad_maximum_fusion.refs_4_), channel_id=1, source_target_pairs={{0,4},{2,6},{4,0},{6,2},{8,12},{10,14},{12,8},{14,10},{16,20},{18,... | collective-permute-start | bytes 393224 | tf_op jit(solution)/shard_map/ppermute | solution.py:21
  13.1 0.0 collective-permute-start.6
  13.1 0.5 %collective-permute-start.8 = (bf16[2,128,256]{2,1,0:T(8,128)(2,1)S(1)}, bf16[2,128,256]{2,1,0:T(8,128)(2,1)S(1)}, u32[]{:S(2)}, u32[]{:S(2)}) collective-permute-start(bf16[2,128,256]{2,1,0:T(8,128)(2,1)S(1)} %pad_maximum_fusion.refs_4_), channel_id=1, source_target_pairs={{0,2},{2,0},{4,6},{6,4},{8,10},{10,8},{12,14},{14,12},{16,18},{18,... | collective-permute-start | bytes 393224 | tf_op jit(solution)/shard_map/ppermute | solution.py:21
  13.6 0.3 %collective-permute-done.5.refs_1_ = bf16[2,128,256]{2,1,0:T(8,128)(2,1)S(1)} collective-permute-done((bf16[2,128,256]{2,1,0:T(8,128)(2,1)S(1)}, bf16[2,128,256]{2,1,0:T(8,128)(2,1)S(1)}, u32[]{:S(2)}, u32[]{:S(2)}) %collective-permute-start.5) | collective-permute-done | bytes 131104 | tf_op jit(solution)/shard_map/ppermute | solution.py:21
  13.9 0.0 collective-permute-start.7
  13.9 2.8 %collective-permute-done.2.refs_5_ = bf16[2,128,256]{2,1,0:T(8,128)(2,1)S(1)} collective-permute-done((bf16[2,128,256]{2,1,0:T(8,128)(2,1)S(1)}, bf16[2,128,256]{2,1,0:T(8,128)(2,1)S(1)}, u32[]{:S(2)}, u32[]{:S(2)}) %collective-permute-start.2) | collective-permute-done | bytes 131104 | tf_op jit(solution)/shard_map/ppermute | solution.py:21
  16.7 0.0 collective-permute-start.9
  16.7 1.7 %collective-permute-start.3 = (bf16[128,256]{1,0:T(8,128)(2,1)S(1)}, bf16[128,256]{1,0:T(8,128)(2,1)S(1)}, u32[]{:S(2)}, u32[]{:S(2)}) collective-permute-start(bf16[128,256]{1,0:T(8,128)(2,1)S(1)} %get-tuple-element.25.own_ref), channel_id=1, source_target_pairs={{0,1},{1,0},{2,3},{3,2},{4,5},{5,4},{6,7},{7,6},{8,9},{9,8},{10,11... | collective-permute-start | bytes 196616 | tf_op jit(solution)/shard_map/ppermute | solution.py:21
  18.4 0.0 collective-permute-done.6.refs_2_
  18.4 0.0 collective-permute-done.8.refs_6_
  18.4 0.0 collective-permute-done.7.refs_3_
  18.4 0.0 collective-permute-done.9.refs_7_
  18.4 0.3 %select.3 = (bf16[512,128]{1,0:T(8,128)(2,1)S(1)}, bf16[512,128]{1,0:T(8,128)(2,1)S(1)}) custom-call(s32[8,128]{1,0:T(8,128)S(1)} %get-tuple-element.26.code_ref, bf16[2,128,256]{2,1,0:T(8,128)(2,1)S(1)} %pad_maximum_fusion.1.refs_0_, bf16[2,128,256]{2,1,0:T(8,128)(2,1)S(1)} %collective-permute-done.5.refs_1_, ...), custom_call_target="tpu_custom_call" | custom-call | flops 1048576 | bytes 1048576 | tf_op jit(solution)/shard_map/select/pallas_call | solution.py:300
  18.8 1.4 %collective-permute-start.10 = (bf16[512,128]{1,0:T(8,128)(2,1)S(1)}, bf16[512,128]{1,0:T(8,128)(2,1)S(1)}, u32[]{:S(2)}, u32[]{:S(2)}) collective-permute-start(bf16[512,128]{1,0:T(8,128)(2,1)S(1)} %get-tuple-element.28.keys_ref), channel_id=1, source_target_pairs={{0,1},{1,0},{2,3},{3,2},{4,5},{5,4},{6,7},{7,6},{8,9},{9,8},{10,11... | collective-permute-start | bytes 393224 | tf_op jit(solution)/shard_map/ppermute | solution.py:21
  20.1 0.7 %collective-permute-start.11 = (bf16[512,128]{1,0:T(8,128)(2,1)S(1)}, bf16[512,128]{1,0:T(8,128)(2,1)S(1)}, u32[]{:S(2)}, u32[]{:S(2)}) collective-permute-start(bf16[512,128]{1,0:T(8,128)(2,1)S(1)} %get-tuple-element.29.values_ref), channel_id=1, source_target_pairs={{0,1},{1,0},{2,3},{3,2},{4,5},{5,4},{6,7},{7,6},{8,9},{9,8},{10,11... | collective-permute-start | bytes 393224 | tf_op jit(solution)/shard_map/ppermute | solution.py:21
  20.8 0.4 %collective-permute-done.3.other_ref = bf16[128,256]{1,0:T(8,128)(2,1)S(1)} collective-permute-done((bf16[128,256]{1,0:T(8,128)(2,1)S(1)}, bf16[128,256]{1,0:T(8,128)(2,1)S(1)}, u32[]{:S(2)}, u32[]{:S(2)}) %collective-permute-start.3) | collective-permute-done | bytes 65568 | tf_op jit(solution)/shard_map/ppermute | solution.py:21
  21.2 2.4 %attend_first.1 = (f32[2,1024,128]{2,1,0:T(8,128)S(1)}, f32[2,1024,256]{2,1,0:T(8,128)S(1)}, s32[8,128]{1,0:T(8,128)S(1)}) custom-call(s32[50]{0:T(128)S(1)} %pad_add_fusion.1.meta_ref, bf16[2,1024,128]{2,1,0:T(8,128)(2,1)S(1)} %get-tuple-element.22.q_ref, bf16[128,256]{1,0:T(8,128)(2,1)S(1)} %get-tuple-element.25.own_ref, ...), custom_call_target="tpu_custom_call" | custom-call | flops 2147483648 | bytes 1048576 | tf_op jit(solution)/shard_map/attend_first/pallas_call | solution.py:260
  23.6 1.5 %collective-permute-done.10.keys_ref = bf16[512,128]{1,0:T(8,128)(2,1)S(1)} collective-permute-done((bf16[512,128]{1,0:T(8,128)(2,1)S(1)}, bf16[512,128]{1,0:T(8,128)(2,1)S(1)}, u32[]{:S(2)}, u32[]{:S(2)}) %collective-permute-start.10) | collective-permute-done | bytes 131104 | tf_op jit(solution)/shard_map/ppermute | solution.py:21
  25.2 1.2 %attend_weigh.1 = (bf16[2,1024,512]{2,1,0:T(8,128)(2,1)S(1)}, f32[2,1024,128]{2,1,0:T(8,128)S(1)}) custom-call(s32[8,128]{1,0:T(8,128)S(1)} %get-tuple-element.30.plan_ref, bf16[2,1024,128]{2,1,0:T(8,128)(2,1)S(1)} %get-tuple-element.22.q_ref, bf16[512,128]{1,0:T(8,128)(2,1)S(1)} %collective-permute-done.10.keys_ref, ...), custom_call_target="tpu_custom_call" | custom-call | flops 1073741824 | bytes 1048576 | tf_op jit(solution)/shard_map/attend_weigh/pallas_call | solution.py:263
  26.3 0.9 %collective-permute-done.11.values_ref = bf16[512,128]{1,0:T(8,128)(2,1)S(1)} collective-permute-done((bf16[512,128]{1,0:T(8,128)(2,1)S(1)}, bf16[512,128]{1,0:T(8,128)(2,1)S(1)}, u32[]{:S(2)}, u32[]{:S(2)}) %collective-permute-start.11) | collective-permute-done | bytes 131104 | tf_op jit(solution)/shard_map/ppermute | solution.py:21
  27.3 1.5 %attend_finish.1 = bf16[256,1024]{1,0:T(8,128)(2,1)} custom-call(s32[8,128]{1,0:T(8,128)S(1)} %get-tuple-element.30.plan_ref, bf16[2,1024,512]{2,1,0:T(8,128)(2,1)S(1)} %get-tuple-element.33.weights_ref, f32[2,1024,128]{2,1,0:T(8,128)S(1)} %get-tuple-element.34.rest_ref, bf16[512,128]{1,0:T(8,128)(2,1)S(1)} %collective-permute-done.11.values_ref), custom_call_target="tpu_custom_call" | custom-call | flops 536870912 | bytes 1048576 | tf_op jit(solution)/shard_map/attend_finish/pallas_call | solution.py:273
  (2 shorter events, 0.0 us)
Async XLA Ops:
  0.8 8.0 %collective-permute-start.4 = (bf16[128,256]{1,0:T(8,128)(2,1)S(1)}, bf16[128,256]{1,0:T(8,128)(2,1)S(1)}, u32[]{:S(2)}, u32[]{:S(2)}) collective-permute-start(bf16[128,256]{1,0:T(8,128)(2,1)S(1)} %get-tuple-element.25.own_ref), channel_id=1, source_target_pairs={{0,24},{2,26},{4,28},{6,30},{8,16},{10,18},{12,20},{14,22},{16,8},... | collective-permute-start | bytes 196616 | tf_op jit(solution)/shard_map/ppermute | solution.py:21
  5.9 5.6 %collective-permute-start.1 = (bf16[128,256]{1,0:T(8,128)(2,1)S(1)}, bf16[128,256]{1,0:T(8,128)(2,1)S(1)}, u32[]{:S(2)}, u32[]{:S(2)}) collective-permute-start(bf16[128,256]{1,0:T(8,128)(2,1)S(1)} %get-tuple-element.25.own_ref), channel_id=1, source_target_pairs={{0,16},{2,18},{4,20},{6,22},{8,24},{10,26},{12,28},{14,30},{16,0},... | collective-permute-start | bytes 196616 | tf_op jit(solution)/shard_map/ppermute | solution.py:21
  5.9 5.6 %collective-permute-start = (bf16[128,256]{1,0:T(8,128)(2,1)S(1)}, bf16[128,256]{1,0:T(8,128)(2,1)S(1)}, u32[]{:S(2)}, u32[]{:S(2)}) collective-permute-start(bf16[128,256]{1,0:T(8,128)(2,1)S(1)} %get-tuple-element.25.own_ref), channel_id=1, source_target_pairs={{0,8},{2,10},{4,12},{6,14},{8,0},{10,2},{12,4},{14,6},{16,24},{18,... | collective-permute-start | bytes 196616 | tf_op jit(solution)/shard_map/ppermute | solution.py:21
  7.3 1.0 %copy-start = (bf16[256,1024]{1,0:T(8,128)(2,1)S(1)}, bf16[256,1024]{1,0:T(8,128)(2,1)}, u32[]{:S(2)}) copy-start(bf16[256,1024]{1,0:T(8,128)(2,1)} %q_ref.1) | copy-start | bytes 1572868
  8.9 5.0 %collective-permute-start.5 = (bf16[2,128,256]{2,1,0:T(8,128)(2,1)S(1)}, bf16[2,128,256]{2,1,0:T(8,128)(2,1)S(1)}, u32[]{:S(2)}, u32[]{:S(2)}) collective-permute-start(bf16[2,128,256]{2,1,0:T(8,128)(2,1)S(1)} %pad_maximum_fusion.1.refs_0_), channel_id=1, source_target_pairs={{0,4},{2,6},{4,0},{6,2},{8,12},{10,14},{12,8},{14,10},{16,20},{18,... | collective-permute-start | bytes 393224 | tf_op jit(solution)/shard_map/ppermute | solution.py:21
  11.5 5.2 %collective-permute-start.2 = (bf16[2,128,256]{2,1,0:T(8,128)(2,1)S(1)}, bf16[2,128,256]{2,1,0:T(8,128)(2,1)S(1)}, u32[]{:S(2)}, u32[]{:S(2)}) collective-permute-start(bf16[2,128,256]{2,1,0:T(8,128)(2,1)S(1)} %pad_maximum_fusion.refs_4_), channel_id=1, source_target_pairs={{0,4},{2,6},{4,0},{6,2},{8,12},{10,14},{12,8},{14,10},{16,20},{18,... | collective-permute-start | bytes 393224 | tf_op jit(solution)/shard_map/ppermute | solution.py:21
  13.1 5.3 %collective-permute-start.6 = (bf16[2,128,256]{2,1,0:T(8,128)(2,1)S(1)}, bf16[2,128,256]{2,1,0:T(8,128)(2,1)S(1)}, u32[]{:S(2)}, u32[]{:S(2)}) collective-permute-start(bf16[2,128,256]{2,1,0:T(8,128)(2,1)S(1)} %pad_maximum_fusion.1.refs_0_), channel_id=1, source_target_pairs={{0,2},{2,0},{4,6},{6,4},{8,10},{10,8},{12,14},{14,12},{16,18},{18,... | collective-permute-start | bytes 393224 | tf_op jit(solution)/shard_map/ppermute | solution.py:21
  13.1 5.3 %collective-permute-start.8 = (bf16[2,128,256]{2,1,0:T(8,128)(2,1)S(1)}, bf16[2,128,256]{2,1,0:T(8,128)(2,1)S(1)}, u32[]{:S(2)}, u32[]{:S(2)}) collective-permute-start(bf16[2,128,256]{2,1,0:T(8,128)(2,1)S(1)} %pad_maximum_fusion.refs_4_), channel_id=1, source_target_pairs={{0,2},{2,0},{4,6},{6,4},{8,10},{10,8},{12,14},{14,12},{16,18},{18,... | collective-permute-start | bytes 393224 | tf_op jit(solution)/shard_map/ppermute | solution.py:21
  13.9 4.5 %collective-permute-start.7 = (bf16[2,128,256]{2,1,0:T(8,128)(2,1)S(1)}, bf16[2,128,256]{2,1,0:T(8,128)(2,1)S(1)}, u32[]{:S(2)}, u32[]{:S(2)}) collective-permute-start(bf16[2,128,256]{2,1,0:T(8,128)(2,1)S(1)} %collective-permute-done.5.refs_1_), channel_id=1, source_target_pairs={{0,2},{2,0},{4,6},{6,4},{8,10},{10,8},{12,14},{14,12},{16,18},{18,... | collective-permute-start | bytes 393224 | tf_op jit(solution)/shard_map/ppermute | solution.py:21
  16.7 1.7 %collective-permute-start.9 = (bf16[2,128,256]{2,1,0:T(8,128)(2,1)S(1)}, bf16[2,128,256]{2,1,0:T(8,128)(2,1)S(1)}, u32[]{:S(2)}, u32[]{:S(2)}) collective-permute-start(bf16[2,128,256]{2,1,0:T(8,128)(2,1)S(1)} %collective-permute-done.2.refs_5_), channel_id=1, source_target_pairs={{0,2},{2,0},{4,6},{6,4},{8,10},{10,8},{12,14},{14,12},{16,18},{18,... | collective-permute-start | bytes 393224 | tf_op jit(solution)/shard_map/ppermute | solution.py:21
  16.7 4.5 %collective-permute-start.3 = (bf16[128,256]{1,0:T(8,128)(2,1)S(1)}, bf16[128,256]{1,0:T(8,128)(2,1)S(1)}, u32[]{:S(2)}, u32[]{:S(2)}) collective-permute-start(bf16[128,256]{1,0:T(8,128)(2,1)S(1)} %get-tuple-element.25.own_ref), channel_id=1, source_target_pairs={{0,1},{1,0},{2,3},{3,2},{4,5},{5,4},{6,7},{7,6},{8,9},{9,8},{10,11... | collective-permute-start | bytes 196616 | tf_op jit(solution)/shard_map/ppermute | solution.py:21
  18.8 6.4 %collective-permute-start.10 = (bf16[512,128]{1,0:T(8,128)(2,1)S(1)}, bf16[512,128]{1,0:T(8,128)(2,1)S(1)}, u32[]{:S(2)}, u32[]{:S(2)}) collective-permute-start(bf16[512,128]{1,0:T(8,128)(2,1)S(1)} %get-tuple-element.28.keys_ref), channel_id=1, source_target_pairs={{0,1},{1,0},{2,3},{3,2},{4,5},{5,4},{6,7},{7,6},{8,9},{9,8},{10,11... | collective-permute-start | bytes 393224 | tf_op jit(solution)/shard_map/ppermute | solution.py:21
  20.1 7.1 %collective-permute-start.11 = (bf16[512,128]{1,0:T(8,128)(2,1)S(1)}, bf16[512,128]{1,0:T(8,128)(2,1)S(1)}, u32[]{:S(2)}, u32[]{:S(2)}) collective-permute-start(bf16[512,128]{1,0:T(8,128)(2,1)S(1)} %get-tuple-element.29.values_ref), channel_id=1, source_target_pairs={{0,1},{1,0},{2,3},{3,2},{4,5},{5,4},{6,7},{7,6},{8,9},{9,8},{10,11... | collective-permute-start | bytes 393224 | tf_op jit(solution)/shard_map/ppermute | solution.py:21
